TPU v7x, 256 devices: a whole 4x4x8 slice. The times are simulated.
256 devices in a mesh: group: 8 (over z), seq: 32 (over x, y, core).
Axes of the slice: x: 4, y: 4, z: 8, core: 2. Of those that a mesh axis runs over, the one named last changes fastest.
Arguments:
- queries: bfloat16 [8, 1024, 4096], P('group', 'seq')
- keys: bfloat16 [8, 1024, 4096], P('group', 'seq')
- values: bfloat16 [8, 1024, 4096], P('group', 'seq'), may hold values from -6 to 6
- valid: int32 [8], replicated, may hold values from 256 to 1024, as said below
- levels: int32 [8], replicated, may hold values from 0 to 63
- gate_table: float32 [64, 4096], replicated, may hold values from 0.5 to 2
Outputs:
- mixed: bfloat16 [8, 1024, 4096], P('group', 'seq')
Inputs may be any that keep to these rules, and one draw needn't show every extreme that they name: Each group has at least 256 valid tokens, and at least one group has all 1024.
All inputs are finite; a program needn't handle non-finite values.
Results may differ from a plain program's by a relative error of at most 0.0075.
Values may be sent and summed in bfloat16 or wider, within the bound.
No kernel may reach another device: no remote copies, remote signals or barrier semaphores. Data moves between devices by JAX's collectives and lax.ppermute only.
A program may use at most 128 MiB of HBM per device.

v0:
```python
import math

import jax
import jax.numpy as jnp
from jax import lax
from jax.sharding import PartitionSpec as P

HD = 128


def from_behind(value, axis, by):
    peers = lax.axis_size(axis)
    pairs = [(i, i + by) for i in range(peers) if 0 <= i + by < peers]
    return lax.ppermute(value, axis, pairs)


def lookup(table, index):
    return jnp.sum(jnp.where(jnp.arange(table.shape[0]) == index, table, 0))


def shards(queries, keys, values, valid, levels, gate_table):
    tokens_here = queries.shape[1]
    width = queries.shape[2]
    heads_all = width // HD
    query_heads, key_heads, value_heads = (
        lax.all_to_all(
            queries.reshape(tokens_here, heads_all, HD),
            "seq",
            split_axis=1,
            concat_axis=0,
            tiled=True,
        ),
        lax.all_to_all(
            keys.reshape(tokens_here, heads_all, HD), "seq", split_axis=1, concat_axis=0, tiled=True
        ),
        lax.all_to_all(
            values.reshape(tokens_here, heads_all, HD),
            "seq",
            split_axis=1,
            concat_axis=0,
            tiled=True,
        ),
    )
    group_len = query_heads.shape[0]
    heads_here = query_heads.shape[1]
    own_group = lax.axis_index("group")
    positions = jnp.arange(group_len, dtype=jnp.int32)
    score_scale = 1.0 / math.sqrt(HD)

    def absorb(state, key_block, value_block, group_id):
        running_max, running_sum, running_acc = state
        live_count = lookup(valid, group_id)
        key_live = (positions < live_count) & (group_id <= own_group)
        score = (
            jnp.einsum("qhd,khd->hqk", query_heads, key_block, preferred_element_type=jnp.float32)
            * score_scale
        )
        score = jnp.where(key_live[None, None, :], score, -1e30)
        new_max = jnp.maximum(running_max, jnp.max(score, axis=2))
        weight = jnp.where(key_live[None, None, :], jnp.exp(score - new_max[:, :, None]), 0.0)
        factor = jnp.exp(running_max - new_max)
        new_sum = running_sum * factor + jnp.sum(weight, axis=2)
        product = jnp.einsum(
            "hqk,khd->hqd",
            weight.astype(jnp.bfloat16),
            value_block,
            preferred_element_type=jnp.float32,
        )
        return (new_max, new_sum, running_acc * factor[:, :, None] + product)

    initial = (
        jnp.full((heads_here, group_len), -1e30, jnp.float32),
        jnp.zeros((heads_here, group_len), jnp.float32),
        jnp.zeros((heads_here, group_len, HD), jnp.float32),
    )
    state = absorb(initial, key_heads, value_heads, own_group)
    carried = (key_heads, value_heads)
    for offset in range(1, lax.axis_size("group")):
        carried = from_behind((carried[0], carried[1]), "group", 1)
        state = absorb(state, carried[0], carried[1], own_group - offset)
    running_max, running_sum, running_acc = state
    attended = (running_acc / running_sum[:, :, None]).transpose(1, 0, 2)
    own_count = lookup(valid, own_group)
    attended = jnp.where((positions < own_count)[:, None, None], attended, 0.0).astype(jnp.bfloat16)
    returned = lax.all_to_all(attended, "seq", split_axis=0, concat_axis=1, tiled=True)
    level_index = lookup(levels, own_group)
    gate_row = jnp.sum(
        jnp.where((jnp.arange(gate_table.shape[0]) == level_index)[:, None], gate_table, 0.0),
        axis=0,
    )
    mixed = returned.reshape(tokens_here, width).astype(jnp.float32) * gate_row[None, :]
    return mixed.astype(jnp.bfloat16)[None]


def solution(mesh):
    in_specs = (
        P("group", "seq", None),
        P("group", "seq", None),
        P("group", "seq", None),
        P(),
        P(),
        P(),
    )
    out_specs = P("group", "seq", None)
    return jax.shard_map(shards, mesh=mesh, in_specs=in_specs, out_specs=out_specs, check_vma=False)
```

profile of v0, /device:TPU:97, one launch (start us, length us, event | category | flops | bytes accessed | tf_op | source)
XLA Modules:
  0.0 163.6 jit_solution(11064423773304236006)
XLA Ops:
  1.8 7.8 %all-to-all-start.1 = ((bf16[32,32,128]{2,0,1:T(8,128)(2,1)}), bf16[32,32,128]{2,0,1:T(8,128)(2,1)S(1)}, u32[]{:S(2)}, u32[]{:S(2)}) async-start(bf16[32,32,128]{2,0,1:T(8,128)(2,1)} %copy.16), calls=%async_computation.1 | async-start | bytes 524288 | tf_op jit(solution)/shard_map/all_to_all | solution.py:33
  9.6 1.5 fusion.141
  14.2 4.4 %all-to-all-done.1 = bf16[32,32,128]{2,0,1:T(8,128)(2,1)S(1)} async-done(((bf16[32,32,128]{2,0,1:T(8,128)(2,1)}), bf16[32,32,128]{2,0,1:T(8,128)(2,1)S(1)}, u32[]{:S(2)}, u32[]{:S(2)}) %all-to-all-start.1) | async-done | bytes 262176 | tf_op jit(solution)/shard_map/all_to_all | solution.py:33
  18.5 3.7 %all-to-all-start.2 = ((bf16[32,32,128]{2,0,1:T(8,128)(2,1)}), bf16[32,32,128]{2,0,1:T(8,128)(2,1)S(1)}, u32[]{:S(2)}, u32[]{:S(2)}) async-start(bf16[32,32,128]{2,0,1:T(8,128)(2,1)} %copy.17), calls=%async_computation.2 | async-start | bytes 524288 | tf_op jit(solution)/shard_map/all_to_all | solution.py:36
  22.9 1.0 copy.20
  25.9 5.5 %all-to-all-done.2 = bf16[32,32,128]{2,0,1:T(8,128)(2,1)S(1)} async-done(((bf16[32,32,128]{2,0,1:T(8,128)(2,1)}), bf16[32,32,128]{2,0,1:T(8,128)(2,1)S(1)}, u32[]{:S(2)}, u32[]{:S(2)}) %all-to-all-start.2) | async-done | bytes 262176 | tf_op jit(solution)/shard_map/all_to_all | solution.py:36
  31.4 3.7 %all-to-all-start = ((bf16[32,32,128]{2,0,1:T(8,128)(2,1)}), bf16[32,32,128]{2,0,1:T(8,128)(2,1)S(1)}, u32[]{:S(2)}, u32[]{:S(2)}) async-start(bf16[32,32,128]{2,0,1:T(8,128)(2,1)} %copy.15), calls=%async_computation | async-start | bytes 524288 | tf_op jit(solution)/shard_map/all_to_all | solution.py:26
  37.1 4.8 %collective-permute-start = (bf16[1024,1,128]{2,0,1:T(8,128)(2,1)S(1)}, bf16[1024,1,128]{2,0,1:T(8,128)(2,1)S(1)}, u32[]{:S(2)}, u32[]{:S(2)}) collective-permute-start(bf16[1024,1,128]{2,0,1:T(8,128)(2,1)S(1)} %bitcast.112), channel_id=1, source_target_pairs={{0,32},{32,64},{64,96},{96,128},{128,160},{160,192},{192,224},{1,3... | collective-permute-start | bytes 786440 | tf_op jit(solution)/shard_map/ppermute | solution.py:14
  41.8 2.6 %collective-permute-start.1 = (bf16[1024,1,128]{2,0,1:T(8,128)(2,1)S(1)}, bf16[1024,1,128]{2,0,1:T(8,128)(2,1)S(1)}, u32[]{:S(2)}, u32[]{:S(2)}) collective-permute-start(bf16[1024,1,128]{2,0,1:T(8,128)(2,1)S(1)} %bitcast.120), channel_id=1, source_target_pairs={{0,32},{32,64},{64,96},{96,128},{128,160},{160,192},{192,224},{1,3... | collective-permute-start | bytes 786440 | tf_op jit(solution)/shard_map/ppermute | solution.py:14
  44.5 1.0 fusion
  45.5 1.6 collective-permute-done
  47.1 5.3 %collective-permute-start.2 = (bf16[1024,1,128]{2,0,1:T(8,128)(2,1)S(1)}, bf16[1024,1,128]{2,0,1:T(8,128)(2,1)S(1)}, u32[]{:S(2)}, u32[]{:S(2)}) collective-permute-start(bf16[1024,1,128]{2,0,1:T(8,128)(2,1)S(1)} %collective-permute-done), channel_id=1, source_target_pairs={{0,32},{32,64},{64,96},{96,128},{128,160},{160,192},{192,224},{1,3... | collective-permute-start | bytes 786440 | tf_op jit(solution)/shard_map/ppermute | solution.py:14
  52.8 5.3 %collective-permute-start.3 = (bf16[1024,1,128]{2,0,1:T(8,128)(2,1)S(1)}, bf16[1024,1,128]{2,0,1:T(8,128)(2,1)S(1)}, u32[]{:S(2)}, u32[]{:S(2)}) collective-permute-start(bf16[1024,1,128]{2,0,1:T(8,128)(2,1)S(1)} %collective-permute-done.1), channel_id=1, source_target_pairs={{0,32},{32,64},{64,96},{96,128},{128,160},{160,192},{192,224},{1,3... | collective-permute-start | bytes 786440 | tf_op jit(solution)/shard_map/ppermute | solution.py:14
  58.1 1.1 fusion.1
  59.2 3.4 %collective-permute-start.4 = (bf16[1024,1,128]{2,0,1:T(8,128)(2,1)S(1)}, bf16[1024,1,128]{2,0,1:T(8,128)(2,1)S(1)}, u32[]{:S(2)}, u32[]{:S(2)}) collective-permute-start(bf16[1024,1,128]{2,0,1:T(8,128)(2,1)S(1)} %collective-permute-done.2), channel_id=1, source_target_pairs={{0,32},{32,64},{64,96},{96,128},{128,160},{160,192},{192,224},{1,3... | collective-permute-start | bytes 786440 | tf_op jit(solution)/shard_map/ppermute | solution.py:14
  63.1 5.3 %collective-permute-start.5 = (bf16[1024,1,128]{2,0,1:T(8,128)(2,1)S(1)}, bf16[1024,1,128]{2,0,1:T(8,128)(2,1)S(1)}, u32[]{:S(2)}, u32[]{:S(2)}) collective-permute-start(bf16[1024,1,128]{2,0,1:T(8,128)(2,1)S(1)} %collective-permute-done.3), channel_id=1, source_target_pairs={{0,32},{32,64},{64,96},{96,128},{128,160},{160,192},{192,224},{1,3... | collective-permute-start | bytes 786440 | tf_op jit(solution)/shard_map/ppermute | solution.py:14
  68.5 1.0 fusion.2
  69.5 4.5 %collective-permute-start.6 = (bf16[1024,1,128]{2,0,1:T(8,128)(2,1)S(1)}, bf16[1024,1,128]{2,0,1:T(8,128)(2,1)S(1)}, u32[]{:S(2)}, u32[]{:S(2)}) collective-permute-start(bf16[1024,1,128]{2,0,1:T(8,128)(2,1)S(1)} %collective-permute-done.4), channel_id=1, source_target_pairs={{0,32},{32,64},{64,96},{96,128},{128,160},{160,192},{192,224},{1,3... | collective-permute-start | bytes 786440 | tf_op jit(solution)/shard_map/ppermute | solution.py:14
  74.1 4.5 %collective-permute-start.7 = (bf16[1024,1,128]{2,0,1:T(8,128)(2,1)S(1)}, bf16[1024,1,128]{2,0,1:T(8,128)(2,1)S(1)}, u32[]{:S(2)}, u32[]{:S(2)}) collective-permute-start(bf16[1024,1,128]{2,0,1:T(8,128)(2,1)S(1)} %collective-permute-done.5), channel_id=1, source_target_pairs={{0,32},{32,64},{64,96},{96,128},{128,160},{160,192},{192,224},{1,3... | collective-permute-start | bytes 786440 | tf_op jit(solution)/shard_map/ppermute | solution.py:14
  78.6 1.1 fusion.3
  79.7 4.8 %collective-permute-start.8 = (bf16[1024,1,128]{2,0,1:T(8,128)(2,1)S(1)}, bf16[1024,1,128]{2,0,1:T(8,128)(2,1)S(1)}, u32[]{:S(2)}, u32[]{:S(2)}) collective-permute-start(bf16[1024,1,128]{2,0,1:T(8,128)(2,1)S(1)} %collective-permute-done.6), channel_id=1, source_target_pairs={{0,32},{32,64},{64,96},{96,128},{128,160},{160,192},{192,224},{1,3... | collective-permute-start | bytes 786440 | tf_op jit(solution)/shard_map/ppermute | solution.py:14
  84.8 5.3 %collective-permute-start.9 = (bf16[1024,1,128]{2,0,1:T(8,128)(2,1)S(1)}, bf16[1024,1,128]{2,0,1:T(8,128)(2,1)S(1)}, u32[]{:S(2)}, u32[]{:S(2)}) collective-permute-start(bf16[1024,1,128]{2,0,1:T(8,128)(2,1)S(1)} %collective-permute-done.7), channel_id=1, source_target_pairs={{0,32},{32,64},{64,96},{96,128},{128,160},{160,192},{192,224},{1,3... | collective-permute-start | bytes 786440 | tf_op jit(solution)/shard_map/ppermute | solution.py:14
  90.1 1.1 fusion.4
  91.1 3.9 %collective-permute-start.10 = (bf16[1024,1,128]{2,0,1:T(8,128)(2,1)S(1)}, bf16[1024,1,128]{2,0,1:T(8,128)(2,1)S(1)}, u32[]{:S(2)}, u32[]{:S(2)}) collective-permute-start(bf16[1024,1,128]{2,0,1:T(8,128)(2,1)S(1)} %collective-permute-done.8), channel_id=1, source_target_pairs={{0,32},{32,64},{64,96},{96,128},{128,160},{160,192},{192,224},{1,3... | collective-permute-start | bytes 786440 | tf_op jit(solution)/shard_map/ppermute | solution.py:14
  96.0 5.3 %collective-permute-start.11 = (bf16[1024,1,128]{2,0,1:T(8,128)(2,1)S(1)}, bf16[1024,1,128]{2,0,1:T(8,128)(2,1)S(1)}, u32[]{:S(2)}, u32[]{:S(2)}) collective-permute-start(bf16[1024,1,128]{2,0,1:T(8,128)(2,1)S(1)} %collective-permute-done.9), channel_id=1, source_target_pairs={{0,32},{32,64},{64,96},{96,128},{128,160},{160,192},{192,224},{1,3... | collective-permute-start | bytes 786440 | tf_op jit(solution)/shard_map/ppermute | solution.py:14
  101.3 1.1 fusion.5
  102.3 4.5 %collective-permute-start.12 = (bf16[1024,1,128]{2,0,1:T(8,128)(2,1)S(1)}, bf16[1024,1,128]{2,0,1:T(8,128)(2,1)S(1)}, u32[]{:S(2)}, u32[]{:S(2)}) collective-permute-start(bf16[1024,1,128]{2,0,1:T(8,128)(2,1)S(1)} %collective-permute-done.10), channel_id=1, source_target_pairs={{0,32},{32,64},{64,96},{96,128},{128,160},{160,192},{192,224},{1,3... | collective-permute-start | bytes 786440 | tf_op jit(solution)/shard_map/ppermute | solution.py:14
  106.9 4.5 %collective-permute-start.13 = (bf16[1024,1,128]{2,0,1:T(8,128)(2,1)S(1)}, bf16[1024,1,128]{2,0,1:T(8,128)(2,1)S(1)}, u32[]{:S(2)}, u32[]{:S(2)}) collective-permute-start(bf16[1024,1,128]{2,0,1:T(8,128)(2,1)S(1)} %collective-permute-done.11), channel_id=1, source_target_pairs={{0,32},{32,64},{64,96},{96,128},{128,160},{160,192},{192,224},{1,3... | collective-permute-start | bytes 786440 | tf_op jit(solution)/shard_map/ppermute | solution.py:14
  111.4 1.1 fusion.6
  112.5 1.2 fusion.7
  113.8 1.1 fusion.8
  114.8 1.1 fusion.10
  115.9 1.1 fusion.12
  117.0 1.1 fusion.14
  118.0 1.1 fusion.16
  119.1 1.1 fusion.18
  120.2 1.1 fusion.20
  121.3 1.1 fusion.22
  122.4 1.5 fusion.90
  123.9 1.5 fusion.87
  125.4 1.7 %fusion.84 = f32[1024,128]{1,0:T(8,128)S(1)} fusion(f32[1024,128]{1,0:T(8,128)S(1)} %fusion.87, f32[1024,1024]{0,1:T(8,128)S(1)} %get-tuple-element.41, f32[1024]{0:T(1024)S(1)} %get-tuple-element.26, pred[1024]{0:T(1024)(128)(4,1)S(1)} %fusion.127, bf16[1024,1,128]{2,0,1:T(8,128)(2,1)S(1)} %collective-permute-done.3, f32[1024]{0:T(1024)S(1)} %get-tuple-element.18), kind=kOutput, calls=%fused_computation.68 | convolution fusion | flops 273940480 | bytes 5514240 | tf_op jit(solution)/shard_map/hqk,khd->hqd/dot_general | solution.py:63
  127.1 1.5 fusion.81
  128.7 1.5 fusion.78
  130.2 1.5 fusion.75
  131.7 1.5 fusion.72
  133.2 1.5 fusion.102
  136.8 15.8 %all-to-all-start.3 = ((bf16[32,2,2048]{2,1,0:T(2,128)(2,1)}), bf16[32,2,2048]{2,1,0:T(2,128)(2,1)S(1)}, u32[]{:S(2)}, u32[]{:S(2)}) async-start(bf16[32,2,2048]{2,1,0:T(2,128)(2,1)} %reshape.731), calls=%async_computation.3 | async-start | bytes 524288 | tf_op jit(solution)/shard_map/all_to_all | solution.py:85
  153.4 8.2 %all-to-all-done.3 = bf16[32,2,2048]{2,1,0:T(2,128)(2,1)S(1)} async-done(((bf16[32,2,2048]{2,1,0:T(2,128)(2,1)}), bf16[32,2,2048]{2,1,0:T(2,128)(2,1)S(1)}, u32[]{:S(2)}, u32[]{:S(2)}) %all-to-all-start.3) | async-done | bytes 262176 | tf_op jit(solution)/shard_map/all_to_all | solution.py:85
  (41 shorter events, 16.4 us)
Async XLA Ops:
  1.8 16.8 %all-to-all-start.1 = ((bf16[32,32,128]{2,0,1:T(8,128)(2,1)}), bf16[32,32,128]{2,0,1:T(8,128)(2,1)S(1)}, u32[]{:S(2)}, u32[]{:S(2)}) async-start(bf16[32,32,128]{2,0,1:T(8,128)(2,1)} %copy.16), calls=%async_computation.1 | async-start | bytes 524288 | tf_op jit(solution)/shard_map/all_to_all | solution.py:33
  18.5 12.8 %all-to-all-start.2 = ((bf16[32,32,128]{2,0,1:T(8,128)(2,1)}), bf16[32,32,128]{2,0,1:T(8,128)(2,1)S(1)}, u32[]{:S(2)}, u32[]{:S(2)}) async-start(bf16[32,32,128]{2,0,1:T(8,128)(2,1)} %copy.17), calls=%async_computation.2 | async-start | bytes 524288 | tf_op jit(solution)/shard_map/all_to_all | solution.py:36
  31.4 13.1 %all-to-all-start = ((bf16[32,32,128]{2,0,1:T(8,128)(2,1)}), bf16[32,32,128]{2,0,1:T(8,128)(2,1)S(1)}, u32[]{:S(2)}, u32[]{:S(2)}) async-start(bf16[32,32,128]{2,0,1:T(8,128)(2,1)} %copy.15), calls=%async_computation | async-start | bytes 524288 | tf_op jit(solution)/shard_map/all_to_all | solution.py:26
  37.1 10.1 %collective-permute-start = (bf16[1024,1,128]{2,0,1:T(8,128)(2,1)S(1)}, bf16[1024,1,128]{2,0,1:T(8,128)(2,1)S(1)}, u32[]{:S(2)}, u32[]{:S(2)}) collective-permute-start(bf16[1024,1,128]{2,0,1:T(8,128)(2,1)S(1)} %bitcast.112), channel_id=1, source_target_pairs={{0,32},{32,64},{64,96},{96,128},{128,160},{160,192},{192,224},{1,3... | collective-permute-start | bytes 786440 | tf_op jit(solution)/shard_map/ppermute | solution.py:14
  41.8 10.9 %collective-permute-start.1 = (bf16[1024,1,128]{2,0,1:T(8,128)(2,1)S(1)}, bf16[1024,1,128]{2,0,1:T(8,128)(2,1)S(1)}, u32[]{:S(2)}, u32[]{:S(2)}) collective-permute-start(bf16[1024,1,128]{2,0,1:T(8,128)(2,1)S(1)} %bitcast.120), channel_id=1, source_target_pairs={{0,32},{32,64},{64,96},{96,128},{128,160},{160,192},{192,224},{1,3... | collective-permute-start | bytes 786440 | tf_op jit(solution)/shard_map/ppermute | solution.py:14
  47.1 12.0 %collective-permute-start.2 = (bf16[1024,1,128]{2,0,1:T(8,128)(2,1)S(1)}, bf16[1024,1,128]{2,0,1:T(8,128)(2,1)S(1)}, u32[]{:S(2)}, u32[]{:S(2)}) collective-permute-start(bf16[1024,1,128]{2,0,1:T(8,128)(2,1)S(1)} %collective-permute-done), channel_id=1, source_target_pairs={{0,32},{32,64},{64,96},{96,128},{128,160},{160,192},{192,224},{1,3... | collective-permute-start | bytes 786440 | tf_op jit(solution)/shard_map/ppermute | solution.py:14
  52.8 10.4 %collective-permute-start.3 = (bf16[1024,1,128]{2,0,1:T(8,128)(2,1)S(1)}, bf16[1024,1,128]{2,0,1:T(8,128)(2,1)S(1)}, u32[]{:S(2)}, u32[]{:S(2)}) collective-permute-start(bf16[1024,1,128]{2,0,1:T(8,128)(2,1)S(1)} %collective-permute-done.1), channel_id=1, source_target_pairs={{0,32},{32,64},{64,96},{96,128},{128,160},{160,192},{192,224},{1,3... | collective-permute-start | bytes 786440 | tf_op jit(solution)/shard_map/ppermute | solution.py:14
  59.2 10.4 %collective-permute-start.4 = (bf16[1024,1,128]{2,0,1:T(8,128)(2,1)S(1)}, bf16[1024,1,128]{2,0,1:T(8,128)(2,1)S(1)}, u32[]{:S(2)}, u32[]{:S(2)}) collective-permute-start(bf16[1024,1,128]{2,0,1:T(8,128)(2,1)S(1)} %collective-permute-done.2), channel_id=1, source_target_pairs={{0,32},{32,64},{64,96},{96,128},{128,160},{160,192},{192,224},{1,3... | collective-permute-start | bytes 786440 | tf_op jit(solution)/shard_map/ppermute | solution.py:14
  63.1 10.9 %collective-permute-start.5 = (bf16[1024,1,128]{2,0,1:T(8,128)(2,1)S(1)}, bf16[1024,1,128]{2,0,1:T(8,128)(2,1)S(1)}, u32[]{:S(2)}, u32[]{:S(2)}) collective-permute-start(bf16[1024,1,128]{2,0,1:T(8,128)(2,1)S(1)} %collective-permute-done.3), channel_id=1, source_target_pairs={{0,32},{32,64},{64,96},{96,128},{128,160},{160,192},{192,224},{1,3... | collective-permute-start | bytes 786440 | tf_op jit(solution)/shard_map/ppermute | solution.py:14
  69.5 10.1 %collective-permute-start.6 = (bf16[1024,1,128]{2,0,1:T(8,128)(2,1)S(1)}, bf16[1024,1,128]{2,0,1:T(8,128)(2,1)S(1)}, u32[]{:S(2)}, u32[]{:S(2)}) collective-permute-start(bf16[1024,1,128]{2,0,1:T(8,128)(2,1)S(1)} %collective-permute-done.4), channel_id=1, source_target_pairs={{0,32},{32,64},{64,96},{96,128},{128,160},{160,192},{192,224},{1,3... | collective-permute-start | bytes 786440 | tf_op jit(solution)/shard_map/ppermute | solution.py:14
  74.1 10.7 %collective-permute-start.7 = (bf16[1024,1,128]{2,0,1:T(8,128)(2,1)S(1)}, bf16[1024,1,128]{2,0,1:T(8,128)(2,1)S(1)}, u32[]{:S(2)}, u32[]{:S(2)}) collective-permute-start(bf16[1024,1,128]{2,0,1:T(8,128)(2,1)S(1)} %collective-permute-done.5), channel_id=1, source_target_pairs={{0,32},{32,64},{64,96},{96,128},{128,160},{160,192},{192,224},{1,3... | collective-permute-start | bytes 786440 | tf_op jit(solution)/shard_map/ppermute | solution.py:14
  79.7 11.5 %collective-permute-start.8 = (bf16[1024,1,128]{2,0,1:T(8,128)(2,1)S(1)}, bf16[1024,1,128]{2,0,1:T(8,128)(2,1)S(1)}, u32[]{:S(2)}, u32[]{:S(2)}) collective-permute-start(bf16[1024,1,128]{2,0,1:T(8,128)(2,1)S(1)} %collective-permute-done.6), channel_id=1, source_target_pairs={{0,32},{32,64},{64,96},{96,128},{128,160},{160,192},{192,224},{1,3... | collective-permute-start | bytes 786440 | tf_op jit(solution)/shard_map/ppermute | solution.py:14
  84.8 11.2 %collective-permute-start.9 = (bf16[1024,1,128]{2,0,1:T(8,128)(2,1)S(1)}, bf16[1024,1,128]{2,0,1:T(8,128)(2,1)S(1)}, u32[]{:S(2)}, u32[]{:S(2)}) collective-permute-start(bf16[1024,1,128]{2,0,1:T(8,128)(2,1)S(1)} %collective-permute-done.7), channel_id=1, source_target_pairs={{0,32},{32,64},{64,96},{96,128},{128,160},{160,192},{192,224},{1,3... | collective-permute-start | bytes 786440 | tf_op jit(solution)/shard_map/ppermute | solution.py:14
  91.1 11.2 %collective-permute-start.10 = (bf16[1024,1,128]{2,0,1:T(8,128)(2,1)S(1)}, bf16[1024,1,128]{2,0,1:T(8,128)(2,1)S(1)}, u32[]{:S(2)}, u32[]{:S(2)}) collective-permute-start(bf16[1024,1,128]{2,0,1:T(8,128)(2,1)S(1)} %collective-permute-done.8), channel_id=1, source_target_pairs={{0,32},{32,64},{64,96},{96,128},{128,160},{160,192},{192,224},{1,3... | collective-permute-start | bytes 786440 | tf_op jit(solution)/shard_map/ppermute | solution.py:14
  96.0 10.9 %collective-permute-start.11 = (bf16[1024,1,128]{2,0,1:T(8,128)(2,1)S(1)}, bf16[1024,1,128]{2,0,1:T(8,128)(2,1)S(1)}, u32[]{:S(2)}, u32[]{:S(2)}) collective-permute-start(bf16[1024,1,128]{2,0,1:T(8,128)(2,1)S(1)} %collective-permute-done.9), channel_id=1, source_target_pairs={{0,32},{32,64},{64,96},{96,128},{128,160},{160,192},{192,224},{1,3... | collective-permute-start | bytes 786440 | tf_op jit(solution)/shard_map/ppermute | solution.py:14
  102.3 10.2 %collective-permute-start.12 = (bf16[1024,1,128]{2,0,1:T(8,128)(2,1)S(1)}, bf16[1024,1,128]{2,0,1:T(8,128)(2,1)S(1)}, u32[]{:S(2)}, u32[]{:S(2)}) collective-permute-start(bf16[1024,1,128]{2,0,1:T(8,128)(2,1)S(1)} %collective-permute-done.10), channel_id=1, source_target_pairs={{0,32},{32,64},{64,96},{96,128},{128,160},{160,192},{192,224},{1,3... | collective-permute-start | bytes 786440 | tf_op jit(solution)/shard_map/ppermute | solution.py:14
  106.9 26.3 %collective-permute-start.13 = (bf16[1024,1,128]{2,0,1:T(8,128)(2,1)S(1)}, bf16[1024,1,128]{2,0,1:T(8,128)(2,1)S(1)}, u32[]{:S(2)}, u32[]{:S(2)}) collective-permute-start(bf16[1024,1,128]{2,0,1:T(8,128)(2,1)S(1)} %collective-permute-done.11), channel_id=1, source_target_pairs={{0,32},{32,64},{64,96},{96,128},{128,160},{160,192},{192,224},{1,3... | collective-permute-start | bytes 786440 | tf_op jit(solution)/shard_map/ppermute | solution.py:14
  133.2 20.0 %copy-start = (f32[64,4096]{1,0:T(8,128)S(1)}, f32[64,4096]{1,0:T(8,128)}, u32[]{:S(2)}) copy-start(f32[64,4096]{1,0:T(8,128)} %param.11) | copy-start | bytes 3145732
  136.8 24.8 %all-to-all-start.3 = ((bf16[32,2,2048]{2,1,0:T(2,128)(2,1)}), bf16[32,2,2048]{2,1,0:T(2,128)(2,1)S(1)}, u32[]{:S(2)}, u32[]{:S(2)}) async-start(bf16[32,2,2048]{2,1,0:T(2,128)(2,1)} %reshape.731), calls=%async_computation.3 | async-start | bytes 524288 | tf_op jit(solution)/shard_map/all_to_all | solution.py:85
where the time goes:
time: 165 us; the launch traced here: 164 us
  starting transfers between devices  95.1 us (58%)
  waiting for transfers between devices  21.7 us (13%)
  matrix products  20.9 us (13%)
  other arithmetic  18 us (11%)
  local copies, waits for them, and re-layouts  7.33 us (4%)
    ppermute x14, starting transfers between devices, from_behind(): return lax.ppermute(value, axis, pairs)  64.2 us
    all_to_all x1, starting transfers between devices, shards(): lax.all_to_all(attended, 'seq', split_axis=0, concat_axis=1, tiled=True)  15.8 us
    dot_general x8, matrix products, absorb(): jnp.einsum('hqk,khd->hqd', weight.astype(jnp.bfloat16), value_block, pref...  12.3 us
    dot_general x8, matrix products, absorb(): jnp.einsum('qhd,khd->hqk', query_heads, key_block, preferred_element_type...  8.62 us
    reduce_sum x8, other arithmetic, absorb(): new_sum = running_sum * factor + jnp.sum(weight, axis=2)  8.48 us
    all_to_all x1, waiting for transfers between devices, shards(): lax.all_to_all(attended, 'seq', split_axis=0, concat_axis=1, tiled=True)  8.17 us
    all_to_all x1, starting transfers between devices, shards(): lax.all_to_all(keys.reshape(tokens_here, heads_all, HD), 'seq', split_axi...  7.76 us
    all_to_all x1, waiting for transfers between devices, shards(): lax.all_to_all(values.reshape(tokens_here, heads_all, HD), 'seq', split_a...  5.45 us
  transfers between devices with their start and end apart: 18, of which 8 were waited for; matrix products, arithmetic and copies ran while one was open for 24% of the time, Pallas kernels for 0%

commit v1 on v0

v1 whole, which is shorter than its diff:
```python
import functools
import math

import jax
import jax.numpy as jnp
from jax import lax
from jax.experimental import pallas as pl
from jax.experimental.pallas import tpu as pltpu
from jax.sharding import Mesh
from jax.sharding import PartitionSpec as P

HD = 128
AX = ("group", "y")
DEAD = -3.0e38
VMEM = pltpu.VMEM
MIB = 1024 * 1024


def pack_kernel(n, *refs):
    out = refs[n]
    for h in range(out.shape[0]):
        for i in range(n):
            out[h, :, i * HD : (i + 1) * HD] = refs[i][:, h * HD : (h + 1) * HD]


def pack(*arrays):
    tokens, width = arrays[0].shape
    n = len(arrays)
    return pl.pallas_call(
        functools.partial(pack_kernel, n),
        out_shape=jax.ShapeDtypeStruct((width // HD, tokens, n * HD), arrays[0].dtype),
        in_specs=[pl.BlockSpec(memory_space=VMEM)] * n,
        out_specs=pl.BlockSpec(memory_space=VMEM),
        compiler_params=pltpu.CompilerParams(vmem_limit_bytes=8 * MIB),
        name="pack",
    )(*arrays)


def attend_kernel(places, valid_ref, q_ref, *refs):
    n = len(places)
    kv_in, out_ref, kv, scores, sems = refs[:n], refs[n], refs[n + 1], refs[n + 2], refs[n + 3]
    groups, slots, rows, _ = kv.shape
    x = lax.axis_index("x")
    core = lax.axis_index("core")
    copies = []
    for i, (_, _, first, slot) in enumerate(places):
        count = kv_in[i].shape[0]
        copies.append(
            pltpu.make_async_copy(kv_in[i], kv.at[pl.ds(first, count), slot], sems.at[i])
        )
        copies[-1].start()
    lane = lax.broadcasted_iota(jnp.int32, (1, rows), 1)
    spread = (lane // 32) * 64 + lane % 32
    offset = {}
    for dist, other, _, slot in places:
        source = lax.rem(x + dist, 4)
        side = 1 - core if other else core
        offset[slot] = source * 256 + side * 32
    scale = math.log2(math.e) / math.sqrt(HD)
    for copy in copies:
        copy.wait()
    pairs = groups // 2
    for p in range(pairs):
        q = jnp.concatenate([q_ref[2 * p], q_ref[2 * p + 1]], axis=0)
        q_rows = q.shape[0]

        def score(j, most, last):
            live_count = valid_ref[j]
            for s in range(slots):
                keys = kv[j, s, :, :HD]
                part = lax.dot_general(
                    q, keys, (((1,), (1,)), ((), ())), preferred_element_type=jnp.float32
                )
                live = spread + offset[s] < live_count
                part = jnp.where(live, part, DEAD)
                if last:
                    early = lax.broadcasted_iota(jnp.int32, part.shape, 0) < q_rows // 2
                    part = jnp.where(early, DEAD, part)
                scores[j, s] = part
                most = jnp.maximum(most, part)
            return most

        most = jnp.full((q_rows, rows), DEAD, jnp.float32)
        most = lax.fori_loop(0, 2 * p + 1, lambda j, c: score(j, c, False), most)
        most = score(2 * p + 1, most, True)
        top = jnp.max(most, axis=1, keepdims=True)

        def weigh(j, state):
            acc, total = state
            for s in range(slots):
                weight = jnp.exp2((scores[j, s] - top) * scale)
                total = total + weight
                acc = acc + jnp.dot(
                    weight.astype(jnp.bfloat16),
                    kv[j, s, :, HD:],
                    preferred_element_type=jnp.float32,
                )
            return acc, total

        zero = jnp.zeros((q_rows, rows), jnp.float32)
        acc, total = lax.fori_loop(0, 2 * p + 2, weigh, (zero, zero))
        total = jnp.sum(total, axis=1, keepdims=True)
        attended = acc / total
        at = lax.broadcasted_iota(jnp.int32, (rows, 1), 0)
        at = (at // 32) * 64 + at % 32 + x * 256 + core * 32
        for half in range(2):
            c = 2 * p + half
            part = attended[half * rows : (half + 1) * rows]
            part = jnp.where(at < valid_ref[c], part, 0.0)
            out_ref[c] = part.astype(out_ref.dtype)


def attend(valid, q, arrays, places):
    groups, rows, _ = q.shape
    slots = 1 + max(place[3] for place in places)
    pairs = groups * (groups + 1) // 2 * rows * rows * slots
    return pl.pallas_call(
        functools.partial(attend_kernel, places),
        out_shape=jax.ShapeDtypeStruct(q.shape, q.dtype),
        in_specs=[pl.BlockSpec(memory_space=pltpu.SMEM), pl.BlockSpec(memory_space=VMEM)]
        + [pl.BlockSpec(memory_space=pl.ANY)] * len(arrays),
        out_specs=pl.BlockSpec(memory_space=VMEM),
        scratch_shapes=[
            pltpu.VMEM((groups, slots, rows, 2 * HD), jnp.bfloat16),
            pltpu.VMEM((groups, slots, 2 * rows, rows), jnp.float32),
            pltpu.SemaphoreType.DMA((len(arrays),)),
        ],
        compiler_params=pltpu.CompilerParams(vmem_limit_bytes=32 * MIB),
        cost_estimate=pl.CostEstimate(
            flops=4 * pairs * HD, bytes_accessed=8 * MIB, transcendentals=pairs
        ),
        name="attend",
    )(valid, q, *arrays)


def shift(value, by):
    n = lax.axis_size("x")
    return lax.ppermute(value, "x", [(i, (i + by) % n) for i in range(n)])


def swap(value):
    return lax.ppermute(value, "core", [(0, 1), (1, 0)])


def shards(queries, keys, values, valid, levels, gate_table):
    tokens, width = queries.shape[1:]
    groups = lax.axis_size("group")
    kv = lax.all_to_all(pack(keys[0], values[0]), AX, 0, 0, tiled=True)
    kv = kv.reshape(groups, -1, 2 * HD)
    q = lax.all_to_all(pack(queries[0]), AX, 0, 0, tiled=True)
    q = q.reshape(groups, -1, HD)
    half = groups // 2
    low, high = kv[:half], kv[half:]
    low_l, high_r = shift(low, 1), shift(high, -1)
    high_l, low_r = shift(high, 1), shift(low, -1)
    low_o, high_o = shift(low_l, 1), shift(high_r, -1)
    arrays, places = [], []
    for value, dist, first, chunk in (
        (kv, 0, 0, 0),
        (low_l, 3, 0, 1),
        (high_r, 1, half, 2),
        (high_l, 3, half, 1),
        (low_r, 1, 0, 2),
        (low_o, 2, 0, 3),
        (high_o, 2, half, 3),
    ):
        for other in (False, True):
            arrays.append(swap(value) if other else value)
            places.append((dist, other, first, 2 * chunk + other))
    attended = attend(valid, q, arrays, places)
    returned = lax.all_to_all(attended.reshape(-1, tokens, HD), AX, 0, 0, tiled=True)
    own = lax.axis_index("group")
    level = lax.dynamic_index_in_dim(levels, own, 0, keepdims=False)
    gate = lax.dynamic_index_in_dim(gate_table, level, 0, keepdims=True)
    mixed = returned.transpose(1, 0, 2).reshape(tokens, width).astype(jnp.float32) * gate
    return mixed.astype(jnp.bfloat16)[None]


def solution(mesh):
    fine = Mesh(mesh.devices.reshape(8, 4, 4, 2), ("group", "x", "y", "core"))
    rows = P("group", ("x", "y", "core"), None)
    return jax.shard_map(
        shards,
        mesh=fine,
        in_specs=(rows, rows, rows, P(), P(), P()),
        out_specs=rows,
        check_vma=False,
    )
```

time: 165 us -> 99.8 us (0.60)
  the two profiles are of different devices: /device:TPU:97 before, /device:TPU:6 now
where the time goes in v1:
time: 99.8 us; the launch traced here: 98.5 us
  waiting for transfers between devices  30.4 us (30%)
  blocking collectives  29 us (29%)
  Pallas kernels  17 us (17%)
  starting transfers between devices  14.8 us (15%)
  local copies, waits for them, and re-layouts  4.46 us (4%)
  between operations  2.03 us (2%)
    all_to_all x1, blocking collectives, shards(): kv = lax.all_to_all(pack(keys[0], values[0]), AX, 0, 0, tiled=True)  29 us
    pallas_call x1, Pallas kernels, attend(): pl.pallas_call(functools.partial(attend_kernel, places), out_shape=jax.Sh...  16.2 us
    ppermute x6, waiting for transfers between devices, shift(): return lax.ppermute(value, 'x', [(i, (i + by) % n) for i in range(n)])  12 us
    all_to_all x1, waiting for transfers between devices, shards(): q = lax.all_to_all(pack(queries[0]), AX, 0, 0, tiled=True)  9.83 us
    all_to_all x1, waiting for transfers between devices, shards(): lax.all_to_all(attended.reshape(-1, tokens, HD), AX, 0, 0, tiled=True)  8.5 us
    ppermute x6, starting transfers between devices, shift(): return lax.ppermute(value, 'x', [(i, (i + by) % n) for i in range(n)])  5.16 us
    all_to_all x1, starting transfers between devices, shards(): q = lax.all_to_all(pack(queries[0]), AX, 0, 0, tiled=True)  4.68 us
    all_to_all x1, starting transfers between devices, shards(): lax.all_to_all(attended.reshape(-1, tokens, HD), AX, 0, 0, tiled=True)  3.88 us
  transfers between devices with their start and end apart: 15, of which 6 were waited for; matrix products, arithmetic and copies ran while one was open for 1% of the time, Pallas kernels for 1%

profile of v1, /device:TPU:6, one launch (start us, length us, event | category | flops | bytes accessed | tf_op | source)
XLA Modules:
  0.0 98.5 jit_solution(12617883498176109162)
XLA Ops:
  0.0 0.0 copy-start
  0.0 1.0 %copy-done.2 = bf16[1,32,4096]{2,1,0:T(8,128)(2,1)S(1)} copy-done((bf16[1,32,4096]{2,1,0:T(8,128)(2,1)S(1)}, bf16[1,32,4096]{2,1,0:T(8,128)(2,1)}, u32[]{:S(2)}) %copy-start.2) | copy-done | bytes 262168
  1.0 0.9 copy-done.3
  2.0 0.1 pack.3
  2.1 29.0 %all_to_all.15 = bf16[32,32,256]{2,1,0:T(8,128)(2,1)S(1)} all-to-all(bf16[32,32,256]{2,1,0:T(8,128)(2,1)S(1)} %pack.3), channel_id=1, replica_groups=mesh['group'=8,'x'=4,'y'=4,'core'=2] {'group','y'}, dimensions={0} | all-to-all | bytes 1048576 | tf_op jit(solution)/shard_map/all_to_all | solution.py:148
  31.1 0.0 collective-permute-start
  31.1 0.7 fusion
  31.8 0.5 collective-permute-start.1
  32.3 1.5 %collective-permute-start.3 = (bf16[4,128,256]{2,1,0:T(8,128)(2,1)S(1)}, bf16[4,128,256]{2,1,0:T(8,128)(2,1)S(1)}, u32[]{:S(2)}, u32[]{:S(2)}) collective-permute-start(bf16[4,128,256]{2,1,0:T(8,128)(2,1)S(1)} %bitcast.18), channel_id=1, source_target_pairs={{0,24},{8,0},{16,8},{24,16},{1,25},{9,1},{17,9},{25,17},{2,26},{10... | collective-permute-start | bytes 786440 | tf_op jit(solution)/shard_map/ppermute | solution.py:138
  33.9 1.7 %collective-permute-start.5 = (bf16[4,128,256]{2,1,0:T(8,128)(2,1)S(1)}, bf16[4,128,256]{2,1,0:T(8,128)(2,1)S(1)}, u32[]{:S(2)}, u32[]{:S(2)}) collective-permute-start(bf16[4,128,256]{2,1,0:T(8,128)(2,1)S(1)} %bitcast.19), channel_id=1, source_target_pairs={{0,8},{8,16},{16,24},{24,0},{1,9},{9,17},{17,25},{25,1},{2,10},{10... | collective-permute-start | bytes 786440 | tf_op jit(solution)/shard_map/ppermute | solution.py:138
  35.5 0.3 collective-permute-start.7
  35.9 5.3 %collective-permute-done.1.refs_2_ = bf16[4,128,256]{2,1,0:T(8,128)(2,1)S(1)} collective-permute-done((bf16[4,128,256]{2,1,0:T(8,128)(2,1)}, bf16[4,128,256]{2,1,0:T(8,128)(2,1)S(1)}, u32[]{:S(2)}, u32[]{:S(2)}) %collective-permute-start.1) | collective-permute-done | bytes 262176 | tf_op jit(solution)/shard_map/ppermute | solution.py:138
  41.1 0.0 collective-permute-start.2
  41.1 1.5 %collective-permute-done.3.refs_4_ = bf16[4,128,256]{2,1,0:T(8,128)(2,1)S(1)} collective-permute-done((bf16[4,128,256]{2,1,0:T(8,128)(2,1)S(1)}, bf16[4,128,256]{2,1,0:T(8,128)(2,1)S(1)}, u32[]{:S(2)}, u32[]{:S(2)}) %collective-permute-start.3) | collective-permute-done | bytes 262176 | tf_op jit(solution)/shard_map/ppermute | solution.py:138
  42.7 0.3 collective-permute-start.9
  42.9 3.8 %collective-permute-done.5.refs_6_ = bf16[4,128,256]{2,1,0:T(8,128)(2,1)S(1)} collective-permute-done((bf16[4,128,256]{2,1,0:T(8,128)(2,1)S(1)}, bf16[4,128,256]{2,1,0:T(8,128)(2,1)S(1)}, u32[]{:S(2)}, u32[]{:S(2)}) %collective-permute-start.5) | collective-permute-done | bytes 262176 | tf_op jit(solution)/shard_map/ppermute | solution.py:138
  46.8 0.8 collective-permute-start.11
  47.6 0.0 copy-done.1
  47.6 0.7 pack.2
  48.3 4.7 %all-to-all-start = ((bf16[32,32,128]{2,1,0:T(8,128)(2,1)}), bf16[32,32,128]{2,1,0:T(8,128)(2,1)S(1)}, u32[]{:S(2)}, u32[]{:S(2)}) async-start(bf16[32,32,128]{2,1,0:T(8,128)(2,1)} %pack.2), calls=%async_computation | async-start | bytes 524288 | tf_op jit(solution)/shard_map/all_to_all | solution.py:150
  53.0 0.0 copy-start.4
  53.0 0.0 collective-permute-done.7.refs_8_
  53.0 0.1 collective-permute-start.4
  53.2 0.0 collective-permute-done.refs_1_
  53.2 0.5 collective-permute-start.6
  53.7 0.0 collective-permute-done.2.refs_3_
  53.7 0.1 collective-permute-start.8
  53.8 0.0 collective-permute-done.9.refs_10_
  53.8 0.4 collective-permute-start.10
  54.2 1.5 %collective-permute-done.11.refs_12_ = bf16[4,128,256]{2,1,0:T(8,128)(2,1)} collective-permute-done((bf16[4,128,256]{2,1,0:T(8,128)(2,1)S(1)}, bf16[4,128,256]{2,1,0:T(8,128)(2,1)}, u32[]{:S(2)}, u32[]{:S(2)}) %collective-permute-start.11) | collective-permute-done | bytes 262176 | tf_op jit(solution)/shard_map/ppermute | solution.py:138
  55.6 0.0 collective-permute-start.12
  55.6 9.8 %all-to-all-done = bf16[32,32,128]{2,1,0:T(8,128)(2,1)S(1)} async-done(((bf16[32,32,128]{2,1,0:T(8,128)(2,1)}), bf16[32,32,128]{2,1,0:T(8,128)(2,1)S(1)}, u32[]{:S(2)}, u32[]{:S(2)}) %all-to-all-start) | async-done | bytes 262176 | tf_op jit(solution)/shard_map/all_to_all | solution.py:150
  65.5 0.0 collective-permute-done.4.refs_5_
  65.5 0.0 collective-permute-done.6.refs_7_
  65.5 0.0 collective-permute-done.8.refs_9_
  65.5 0.0 collective-permute-done.10.refs_11_
  65.5 0.0 collective-permute-done.12.refs_13_
  65.5 0.0 copy-done.4
  65.5 16.2 %attend.1 = bf16[8,128,128]{2,1,0:T(8,128)(2,1)} custom-call(s32[8]{0:T(128)S(1)} %copy-done.4, bf16[8,128,128]{2,1,0:T(8,128)(2,1)S(1)} %bitcast.15, bf16[8,128,256]{2,1,0:T(8,128)(2,1)S(1)} %bitcast.13, bf16[8,128,256]{2,1,0:T(8,128)(2,1)S(1)} %collective-permute-done.refs_1_, bf16[4,128,256]{2,1,0:T(8,128)(2,1)S(1)} %collective-permute-done.1.refs_2_, ...), custom_call_target="tpu_custom_call" | custom-call | flops 2415919104 | bytes 8388608 | tf_op jit(solution)/shard_map/attend/pallas_call | solution.py:117
  81.7 3.9 %all-to-all-start.2 = ((bf16[32,32,128]{2,1,0:T(8,128)(2,1)}), bf16[32,32,128]{2,1,0:T(8,128)(2,1)S(1)}, u32[]{:S(2)}, u32[]{:S(2)}) async-start(bf16[32,32,128]{2,1,0:T(8,128)(2,1)} %bitcast.7), calls=%async_computation.2 | async-start | bytes 524288 | tf_op jit(solution)/shard_map/all_to_all | solution.py:171
  85.6 0.0 copy-start.5
  85.6 0.6 copy-done.5
  86.2 0.6 dynamic_slice.8
  88.7 0.0 copy-done
  88.8 8.5 %all-to-all-done.2 = bf16[32,32,128]{2,1,0:T(8,128)(2,1)S(1)} async-done(((bf16[32,32,128]{2,1,0:T(8,128)(2,1)}), bf16[32,32,128]{2,1,0:T(8,128)(2,1)S(1)}, u32[]{:S(2)}, u32[]{:S(2)}) %all-to-all-start.2) | async-done | bytes 262176 | tf_op jit(solution)/shard_map/all_to_all | solution.py:171
  97.3 0.3 copy.7
  97.7 0.1 reshape.57
  97.8 0.7 multiply_convert_fusion
  (5 shorter events, 0.1 us)
Async XLA Ops:
  0.0 88.7 %copy-start = (f32[64,4096]{1,0:T(8,128)S(1)}, f32[64,4096]{1,0:T(8,128)}, u32[]{:S(2)}) copy-start(f32[64,4096]{1,0:T(8,128)} %param.11) | copy-start | bytes 3145732
  0.0 1.0 %copy-start.2 = (bf16[1,32,4096]{2,1,0:T(8,128)(2,1)S(1)}, bf16[1,32,4096]{2,1,0:T(8,128)(2,1)}, u32[]{:S(2)}) copy-start(bf16[1,32,4096]{2,1,0:T(8,128)(2,1)} %param.7) | copy-start | bytes 786436
  1.0 0.9 copy-start.3
  31.1 16.5 %copy-start.1 = (bf16[1,32,4096]{2,1,0:T(8,128)(2,1)S(1)}, bf16[1,32,4096]{2,1,0:T(8,128)(2,1)}, u32[]{:S(2)}) copy-start(bf16[1,32,4096]{2,1,0:T(8,128)(2,1)} %param.6) | copy-start | bytes 786436
  31.1 22.1 %collective-permute-start = (bf16[8,128,256]{2,1,0:T(8,128)(2,1)S(1)}, bf16[8,128,256]{2,1,0:T(8,128)(2,1)S(1)}, u32[]{:S(2)}, u32[]{:S(2)}) collective-permute-start(bf16[8,128,256]{2,1,0:T(8,128)(2,1)S(1)} %bitcast.12), channel_id=1, source_target_pairs={{0,1},{1,0},{2,3},{3,2},{4,5},{5,4},{6,7},{7,6},{8,9},{9,8},{10,11... | collective-permute-start | bytes 1572872 | tf_op jit(solution)/shard_map/ppermute | solution.py:142
  31.8 9.3 %collective-permute-start.1 = (bf16[4,128,256]{2,1,0:T(8,128)(2,1)}, bf16[4,128,256]{2,1,0:T(8,128)(2,1)S(1)}, u32[]{:S(2)}, u32[]{:S(2)}) collective-permute-start(bf16[4,128,256]{2,1,0:T(8,128)(2,1)} %bitcast.5), channel_id=1, source_target_pairs={{0,8},{8,16},{16,24},{24,0},{1,9},{9,17},{17,25},{25,1},{2,10},{10... | collective-permute-start | bytes 786440 | tf_op jit(solution)/shard_map/ppermute | solution.py:138
  32.3 10.3 %collective-permute-start.3 = (bf16[4,128,256]{2,1,0:T(8,128)(2,1)S(1)}, bf16[4,128,256]{2,1,0:T(8,128)(2,1)S(1)}, u32[]{:S(2)}, u32[]{:S(2)}) collective-permute-start(bf16[4,128,256]{2,1,0:T(8,128)(2,1)S(1)} %bitcast.18), channel_id=1, source_target_pairs={{0,24},{8,0},{16,8},{24,16},{1,25},{9,1},{17,9},{25,17},{2,26},{10... | collective-permute-start | bytes 786440 | tf_op jit(solution)/shard_map/ppermute | solution.py:138
  33.9 12.9 %collective-permute-start.5 = (bf16[4,128,256]{2,1,0:T(8,128)(2,1)S(1)}, bf16[4,128,256]{2,1,0:T(8,128)(2,1)S(1)}, u32[]{:S(2)}, u32[]{:S(2)}) collective-permute-start(bf16[4,128,256]{2,1,0:T(8,128)(2,1)S(1)} %bitcast.19), channel_id=1, source_target_pairs={{0,8},{8,16},{16,24},{24,0},{1,9},{9,17},{17,25},{25,1},{2,10},{10... | collective-permute-start | bytes 786440 | tf_op jit(solution)/shard_map/ppermute | solution.py:138
  35.5 17.5 %collective-permute-start.7 = (bf16[4,128,256]{2,1,0:T(8,128)(2,1)}, bf16[4,128,256]{2,1,0:T(8,128)(2,1)S(1)}, u32[]{:S(2)}, u32[]{:S(2)}) collective-permute-start(bf16[4,128,256]{2,1,0:T(8,128)(2,1)} %bitcast.5), channel_id=1, source_target_pairs={{0,24},{8,0},{16,8},{24,16},{1,25},{9,1},{17,9},{25,17},{2,26},{10... | collective-permute-start | bytes 786440 | tf_op jit(solution)/shard_map/ppermute | solution.py:138
  41.1 12.5 %collective-permute-start.2 = (bf16[4,128,256]{2,1,0:T(8,128)(2,1)S(1)}, bf16[4,128,256]{2,1,0:T(8,128)(2,1)}, u32[]{:S(2)}, u32[]{:S(2)}) collective-permute-start(bf16[4,128,256]{2,1,0:T(8,128)(2,1)S(1)} %collective-permute-done.1.refs_2_), channel_id=1, source_target_pairs={{0,1},{1,0},{2,3},{3,2},{4,5},{5,4},{6,7},{7,6},{8,9},{9,8},{10,11... | collective-permute-start | bytes 786440 | tf_op jit(solution)/shard_map/ppermute | solution.py:142
  42.7 11.1 %collective-permute-start.9 = (bf16[4,128,256]{2,1,0:T(8,128)(2,1)S(1)}, bf16[4,128,256]{2,1,0:T(8,128)(2,1)}, u32[]{:S(2)}, u32[]{:S(2)}) collective-permute-start(bf16[4,128,256]{2,1,0:T(8,128)(2,1)S(1)} %collective-permute-done.1.refs_2_), channel_id=1, source_target_pairs={{0,8},{8,16},{16,24},{24,0},{1,9},{9,17},{17,25},{25,1},{2,10},{10... | collective-permute-start | bytes 786440 | tf_op jit(solution)/shard_map/ppermute | solution.py:138
  46.8 8.9 %collective-permute-start.11 = (bf16[4,128,256]{2,1,0:T(8,128)(2,1)S(1)}, bf16[4,128,256]{2,1,0:T(8,128)(2,1)}, u32[]{:S(2)}, u32[]{:S(2)}) collective-permute-start(bf16[4,128,256]{2,1,0:T(8,128)(2,1)S(1)} %collective-permute-done.3.refs_4_), channel_id=1, source_target_pairs={{0,24},{8,0},{16,8},{24,16},{1,25},{9,1},{17,9},{25,17},{2,26},{10... | collective-permute-start | bytes 786440 | tf_op jit(solution)/shard_map/ppermute | solution.py:138
  48.3 17.1 %all-to-all-start = ((bf16[32,32,128]{2,1,0:T(8,128)(2,1)}), bf16[32,32,128]{2,1,0:T(8,128)(2,1)S(1)}, u32[]{:S(2)}, u32[]{:S(2)}) async-start(bf16[32,32,128]{2,1,0:T(8,128)(2,1)} %pack.2), calls=%async_computation | async-start | bytes 524288 | tf_op jit(solution)/shard_map/all_to_all | solution.py:150
  53.0 12.5 %copy-start.4 = (s32[8]{0:T(128)S(1)}, s32[8]{0:T(128)}, u32[]{:S(2)}) copy-start(s32[8]{0:T(128)} %valid_ref.1) | copy-start | bytes 100
  53.0 12.4 %collective-permute-start.4 = (bf16[4,128,256]{2,1,0:T(8,128)(2,1)S(1)}, bf16[4,128,256]{2,1,0:T(8,128)(2,1)}, u32[]{:S(2)}, u32[]{:S(2)}) collective-permute-start(bf16[4,128,256]{2,1,0:T(8,128)(2,1)S(1)} %collective-permute-done.3.refs_4_), channel_id=1, source_target_pairs={{0,1},{1,0},{2,3},{3,2},{4,5},{5,4},{6,7},{7,6},{8,9},{9,8},{10,11... | collective-permute-start | bytes 786440 | tf_op jit(solution)/shard_map/ppermute | solution.py:142
  53.2 12.3 %collective-permute-start.6 = (bf16[4,128,256]{2,1,0:T(8,128)(2,1)S(1)}, bf16[4,128,256]{2,1,0:T(8,128)(2,1)}, u32[]{:S(2)}, u32[]{:S(2)}) collective-permute-start(bf16[4,128,256]{2,1,0:T(8,128)(2,1)S(1)} %collective-permute-done.5.refs_6_), channel_id=1, source_target_pairs={{0,1},{1,0},{2,3},{3,2},{4,5},{5,4},{6,7},{7,6},{8,9},{9,8},{10,11... | collective-permute-start | bytes 786440 | tf_op jit(solution)/shard_map/ppermute | solution.py:142
  53.7 11.8 %collective-permute-start.8 = (bf16[4,128,256]{2,1,0:T(8,128)(2,1)S(1)}, bf16[4,128,256]{2,1,0:T(8,128)(2,1)}, u32[]{:S(2)}, u32[]{:S(2)}) collective-permute-start(bf16[4,128,256]{2,1,0:T(8,128)(2,1)S(1)} %collective-permute-done.7.refs_8_), channel_id=1, source_target_pairs={{0,1},{1,0},{2,3},{3,2},{4,5},{5,4},{6,7},{7,6},{8,9},{9,8},{10,11... | collective-permute-start | bytes 786440 | tf_op jit(solution)/shard_map/ppermute | solution.py:142
  53.8 11.7 %collective-permute-start.10 = (bf16[4,128,256]{2,1,0:T(8,128)(2,1)}, bf16[4,128,256]{2,1,0:T(8,128)(2,1)}, u32[]{:S(2)}, u32[]{:S(2)}) collective-permute-start(bf16[4,128,256]{2,1,0:T(8,128)(2,1)} %collective-permute-done.9.refs_10_), channel_id=1, source_target_pairs={{0,1},{1,0},{2,3},{3,2},{4,5},{5,4},{6,7},{7,6},{8,9},{9,8},{10,11... | collective-permute-start | bytes 786440 | tf_op jit(solution)/shard_map/ppermute | solution.py:142
  55.6 9.9 %collective-permute-start.12 = (bf16[4,128,256]{2,1,0:T(8,128)(2,1)}, bf16[4,128,256]{2,1,0:T(8,128)(2,1)}, u32[]{:S(2)}, u32[]{:S(2)}) collective-permute-start(bf16[4,128,256]{2,1,0:T(8,128)(2,1)} %collective-permute-done.11.refs_12_), channel_id=1, source_target_pairs={{0,1},{1,0},{2,3},{3,2},{4,5},{5,4},{6,7},{7,6},{8,9},{9,8},{10,11... | collective-permute-start | bytes 786440 | tf_op jit(solution)/shard_map/ppermute | solution.py:142
  81.7 15.6 %all-to-all-start.2 = ((bf16[32,32,128]{2,1,0:T(8,128)(2,1)}), bf16[32,32,128]{2,1,0:T(8,128)(2,1)S(1)}, u32[]{:S(2)}, u32[]{:S(2)}) async-start(bf16[32,32,128]{2,1,0:T(8,128)(2,1)} %bitcast.7), calls=%async_computation.2 | async-start | bytes 524288 | tf_op jit(solution)/shard_map/all_to_all | solution.py:171
  85.6 0.7 copy-start.5

commit v2 on v1

v2 whole, which is shorter than its diff:
```python
import functools
import math

import jax
import jax.numpy as jnp
from jax import lax
from jax.experimental import pallas as pl
from jax.experimental.pallas import tpu as pltpu
from jax.sharding import Mesh
from jax.sharding import PartitionSpec as P

HD = 128
AX = ("group", "y")
DEAD = -3.0e38
VMEM = pltpu.VMEM
MIB = 1024 * 1024


def pack_kernel(n, *refs):
    out, held, sems = refs[n], refs[n + 1], refs[n + 2]
    copies = [pltpu.make_async_copy(refs[i], held.at[i], sems.at[i]) for i in range(n)]
    for copy in copies:
        copy.start()
    for i in range(n):
        copies[i].wait()
        for h in range(out.shape[0]):
            out[h, :, i * HD : (i + 1) * HD] = held[i, :, h * HD : (h + 1) * HD]


def pack(*arrays):
    tokens, width = arrays[0].shape
    n = len(arrays)
    return pl.pallas_call(
        functools.partial(pack_kernel, n),
        out_shape=jax.ShapeDtypeStruct((width // HD, tokens, n * HD), arrays[0].dtype),
        in_specs=[pl.BlockSpec(memory_space=pl.ANY)] * n,
        out_specs=pl.BlockSpec(memory_space=VMEM),
        scratch_shapes=[
            pltpu.VMEM((n, tokens, width), arrays[0].dtype),
            pltpu.SemaphoreType.DMA((n,)),
        ],
        compiler_params=pltpu.CompilerParams(vmem_limit_bytes=60 * MIB),
        name="pack",
    )(*arrays)


def attend_kernel(places, first, last, valid_ref, qkv_ref, *refs):
    n = len(places)
    kv_in, refs = refs[:n], refs[n:]
    if not first:
        (acc_in, top_in, total_in), refs = refs[:3], refs[3:]
    if last:
        out_ref, refs = refs[0], refs[1:]
    else:
        (acc_out, top_out, total_out), refs = refs[:3], refs[3:]
    q_ref, kv, scores, sems = refs
    groups, chunks, _, _ = kv.shape
    rows = q_ref.shape[1]
    x = lax.axis_index("x")
    core = lax.axis_index("core")
    copies = [pltpu.make_async_copy(qkv_ref.at[:, :, pl.ds(2 * HD, HD)], q_ref, sems.at[n])]
    for i, (_, chunk, side, start) in enumerate(places):
        count = kv_in[i].shape[0]
        copies.append(
            pltpu.make_async_copy(
                kv_in[i].at[:, :, pl.ds(0, 2 * HD)],
                kv.at[pl.ds(start, count), chunk, pl.ds(side * rows, rows)],
                sems.at[i],
            )
        )
    for copy in copies:
        copy.start()
    lane = lax.broadcasted_iota(jnp.int32, (1, 2 * rows), 1)
    side = jnp.where(lane < rows, core, 1 - core)
    lane = lane % rows
    spread = (lane // 32) * 64 + lane % 32 + side * 32
    origin = {chunk: lax.rem(x + dist, 4) * 256 for dist, chunk, _, _ in places}
    live = [
        [spread + origin[c] < valid_ref[j] for c in range(chunks)] for j in range(groups)
    ]
    scale = math.log2(math.e) / math.sqrt(HD)
    early = lax.broadcasted_iota(jnp.int32, (2 * rows, 2 * rows), 0) < rows
    for copy in copies:
        copy.wait()
    for p in range(groups // 2):
        q = q_ref[2 * p : 2 * p + 2].reshape(2 * rows, HD)
        most = None
        for j in range(2 * p + 2):
            for c in range(chunks):
                part = lax.dot_general(
                    q, kv[j, c, :, :HD], (((1,), (1,)), ((), ())), preferred_element_type=jnp.float32
                )
                part = jnp.where(live[j][c], part, DEAD)
                if j == 2 * p + 1:
                    part = jnp.where(early, DEAD, part)
                scores[j, c] = part
                part = jnp.maximum(part[:, :HD], part[:, HD:])
                most = part if most is None else jnp.maximum(most, part)
        top = jnp.max(most, axis=1, keepdims=True)
        pair = slice(2 * p, 2 * p + 2)
        if not first:
            old = top_in[pair].reshape(2 * rows, HD)[:, :1]
            top = jnp.maximum(top, old)
            keep = jnp.exp2((old - top) * scale)
            acc = acc_in[pair].reshape(2 * rows, HD) * keep
            total = total_in[pair].reshape(2 * rows, HD) * keep
        else:
            acc = jnp.zeros((2 * rows, HD), jnp.float32)
            total = jnp.zeros((2 * rows, HD), jnp.float32)
        for j in range(2 * p + 2):
            for c in range(chunks):
                weight = jnp.exp2((scores[j, c] - top) * scale)
                total = total + (weight[:, :HD] + weight[:, HD:])
                acc = acc + jnp.dot(
                    weight.astype(jnp.bfloat16),
                    kv[j, c, :, HD:],
                    preferred_element_type=jnp.float32,
                )
        if last:
            attended = acc / jnp.sum(total, axis=1, keepdims=True)
            at = lax.broadcasted_iota(jnp.int32, (rows, 1), 0)
            at = (at // 32) * 64 + at % 32 + x * 256 + core * 32
            for half in range(2):
                part = attended[half * rows : (half + 1) * rows]
                part = jnp.where(at < valid_ref[2 * p + half], part, 0.0)
                out_ref[2 * p + half] = part.astype(out_ref.dtype)
        else:
            acc_out[pair] = acc.reshape(2, rows, HD)
            total_out[pair] = total.reshape(2, rows, HD)
            top_out[pair] = jnp.broadcast_to(top, acc.shape).reshape(2, rows, HD)


def attend(valid, qkv, arrays, places, state=(), last=False):
    groups, rows, _ = qkv.shape
    chunks = 1 + max(place[1] for place in places)
    pairs = groups * (groups + 1) // 2 * rows * 2 * rows * chunks
    whole = pl.BlockSpec(memory_space=VMEM)
    shape = (groups, rows, HD)
    if last:
        out_shape, out_specs = jax.ShapeDtypeStruct(shape, jnp.bfloat16), whole
    else:
        out_shape, out_specs = [jax.ShapeDtypeStruct(shape, jnp.float32)] * 3, [whole] * 3
    return pl.pallas_call(
        functools.partial(attend_kernel, places, not state, last),
        out_shape=out_shape,
        in_specs=[pl.BlockSpec(memory_space=pltpu.SMEM)]
        + [pl.BlockSpec(memory_space=pl.ANY)] * (1 + len(arrays))
        + [whole] * len(state),
        out_specs=out_specs,
        scratch_shapes=[
            pltpu.VMEM(shape, jnp.bfloat16),
            pltpu.VMEM((groups, chunks, 2 * rows, 2 * HD), jnp.bfloat16),
            pltpu.VMEM((groups, chunks, 2 * rows, 2 * rows), jnp.float32),
            pltpu.SemaphoreType.DMA((1 + len(arrays),)),
        ],
        compiler_params=pltpu.CompilerParams(vmem_limit_bytes=32 * MIB),
        cost_estimate=pl.CostEstimate(
            flops=4 * pairs * HD, bytes_accessed=4 * MIB, transcendentals=pairs
        ),
        name="attend",
    )(valid, qkv, *arrays, *state)


def shift(value, by):
    n = lax.axis_size("x")
    return lax.ppermute(value, "x", [(i, (i + by) % n) for i in range(n)])


def swap(value):
    return lax.ppermute(value, "core", [(0, 1), (1, 0)])


def shards(queries, keys, values, valid, levels, gate_table):
    tokens, width = queries.shape[1:]
    groups = lax.axis_size("group")
    qkv = lax.all_to_all(pack(keys[0], values[0], queries[0]), AX, 0, 0, tiled=True)
    qkv = qkv.reshape(groups, -1, 3 * HD)
    half = groups // 2
    low, high = qkv[:half, :, : 2 * HD], qkv[half:, :, : 2 * HD]
    low_l, high_r = shift(low, 1), shift(high, -1)
    high_l, low_r = shift(high, 1), shift(low, -1)
    state = attend(
        valid,
        qkv,
        [qkv, swap(low), swap(high)],
        [(0, 0, 0, 0), (0, 0, 1, 0), (0, 0, 1, half)],
    )
    state, low_l, high_r = lax.optimization_barrier((state, low_l, high_r))
    low_o, high_o = shift(low_l, 1), shift(high_r, -1)

    def both(*pieces):
        arrays, places = [], []
        for value, dist, chunk, first in pieces:
            arrays += [value, swap(value)]
            places += [(dist, chunk, 0, first), (dist, chunk, 1, first)]
        return arrays, places

    state = attend(
        valid,
        qkv,
        *both((low_l, 3, 0, 0), (high_l, 3, 0, half), (low_r, 1, 1, 0), (high_r, 1, 1, half)),
        state=state,
    )
    state, low_o, high_o = lax.optimization_barrier((state, low_o, high_o))
    attended = attend(
        valid, qkv, *both((low_o, 2, 0, 0), (high_o, 2, 0, half)), state=state, last=True
    )
    returned = lax.all_to_all(attended.reshape(-1, tokens, HD), AX, 0, 0, tiled=True)
    own = lax.axis_index("group")
    level = lax.dynamic_index_in_dim(levels, own, 0, keepdims=False)
    gate = lax.dynamic_index_in_dim(gate_table, level, 0, keepdims=True)
    mixed = returned.transpose(1, 0, 2).reshape(tokens, width).astype(jnp.float32) * gate
    return mixed.astype(jnp.bfloat16)[None]


def solution(mesh):
    fine = Mesh(mesh.devices.reshape(8, 4, 4, 2), ("group", "x", "y", "core"))
    rows = P("group", ("x", "y", "core"), None)
    return jax.shard_map(
        shards,
        mesh=fine,
        in_specs=(rows, rows, rows, P(), P(), P()),
        out_specs=rows,
        check_vma=False,
    )
```

time: 99.8 us -> 89 us (0.89)
  waiting for transfers between devices: 30.4 us -> 20.8 us
  blocking collectives: 29 us -> 34.4 us
  local copies, waits for them, and re-layouts: 4.46 us -> 1.72 us
  starting transfers between devices: 14.8 us -> 12.8 us
    all_to_all x1 -> x0, waiting for transfers between devices: 9.83 us -> none  [shards(): q = lax.all_to_all(pack(queries[0]), AX, 0, 0, tiled=True)]
    all_to_all x1, blocking collectives: 29 us -> 34.4 us  [shards(): lax.all_to_all(pack(keys[0], values[0], queries[0]), AX, 0, 0, tiled=True)]
    all_to_all x1 -> x0, starting transfers between devices: 4.68 us -> none  [shards(): q = lax.all_to_all(pack(queries[0]), AX, 0, 0, tiled=True)]
    ppermute x6, waiting for transfers between devices: 12 us -> 9.39 us  [shift(): return lax.ppermute(value, 'x', [(i, (i + by) % n) for i in range(n)])]
    pallas_call x1 -> x3, Pallas kernels: 16.2 us -> 14 us  [attend(): pl.pallas_call(functools.partial(attend_kernel, places, not state, last),...]
    unnamed x12 -> x6, local copies, waits for them, and re-layouts: 2.65 us -> 0.66 us
    all_to_all x1, waiting for transfers between devices: 8.5 us -> 10 us  [shards(): lax.all_to_all(attended.reshape(-1, tokens, HD), AX, 0, 0, tiled=True)]
    ppermute x7 -> x8, waiting for transfers between devices: 0.02 us -> 1.41 us  [swap(): return lax.ppermute(value, 'core', [(0, 1), (1, 0)])]
  transfers between devices with their start and end apart: 15 -> 15, of which waited for: 6 -> 9; matrix products, arithmetic and copies ran while one was open for 1% -> 1% of each run, Pallas kernels for 1% -> 10%
where the time goes in v2:
time: 89 us; the launch traced here: 88.7 us
  blocking collectives  34.4 us (39%)
  waiting for transfers between devices  20.8 us (23%)
  Pallas kernels  16.1 us (18%)
  starting transfers between devices  12.8 us (14%)
  between operations  2.01 us (2%)
  local copies, waits for them, and re-layouts  1.72 us (2%)
    all_to_all x1, blocking collectives, shards(): lax.all_to_all(pack(keys[0], values[0], queries[0]), AX, 0, 0, tiled=True)  34.4 us
    pallas_call x3, Pallas kernels, attend(): pl.pallas_call(functools.partial(attend_kernel, places, not state, last),...  14 us
    all_to_all x1, waiting for transfers between devices, shards(): lax.all_to_all(attended.reshape(-1, tokens, HD), AX, 0, 0, tiled=True)  10 us
    ppermute x6, waiting for transfers between devices, shift(): return lax.ppermute(value, 'x', [(i, (i + by) % n) for i in range(n)])  9.39 us
    ppermute x6, starting transfers between devices, shift(): return lax.ppermute(value, 'x', [(i, (i + by) % n) for i in range(n)])  6.08 us
    all_to_all x1, starting transfers between devices, shards(): lax.all_to_all(attended.reshape(-1, tokens, HD), AX, 0, 0, tiled=True)  5.1 us
    pallas_call x1, Pallas kernels, pack(): pl.pallas_call(functools.partial(pack_kernel, n), out_shape=jax.ShapeDtyp...  2.14 us
  transfers between devices with their start and end apart: 15, of which 9 were waited for; matrix products, arithmetic and copies ran while one was open for 1% of the time, Pallas kernels for 10%

profile of v2, /device:TPU:6, one launch (start us, length us, event | category | flops | bytes accessed | tf_op | source)
XLA Modules:
  0.0 88.7 jit_solution(14618714110644886473)
XLA Ops:
  0.0 0.0 copy-start
  0.0 2.1 %pack.1 = bf16[32,32,384]{2,1,0:T(8,128)(2,1)} custom-call(bf16[32,4096]{1,0:T(8,128)(2,1)} %bitcast.14, bf16[32,4096]{1,0:T(8,128)(2,1)} %bitcast.15, bf16[32,4096]{1,0:T(8,128)(2,1)} %bitcast.16), custom_call_target="tpu_custom_call" | custom-call | tf_op jit(solution)/shard_map/pack/pallas_call | solution.py:33
  2.2 34.4 %all_to_all.10 = bf16[32,32,384]{2,1,0:T(8,128)(2,1)S(1)} all-to-all(bf16[32,32,384]{2,1,0:T(8,128)(2,1)} %pack.1), channel_id=1, replica_groups=mesh['group'=8,'x'=4,'y'=4,'core'=2] {'group','y'}, dimensions={0} | all-to-all | bytes 1572864 | tf_op jit(solution)/shard_map/all_to_all | solution.py:176
  36.6 0.0 copy-start.1
  36.6 0.1 collective-permute-start
  36.7 0.5 collective-permute-start.1
  37.2 0.5 collective-permute-start.2
  37.7 1.5 %collective-permute-start.3 = (bf16[4,128,256]{2,1,0:T(8,128)(2,1)S(1)}, bf16[4,128,256]{2,1,0:T(8,128)(2,1)S(1)}, u32[]{:S(2)}, u32[]{:S(2)}) collective-permute-start(bf16[4,128,256]{2,1,0:T(8,128)(2,1)S(1)} %get-tuple-element.37), channel_id=1, source_target_pairs={{0,24},{8,0},{16,8},{24,16},{1,25},{9,1},{17,9},{25,17},{2,26},{10... | collective-permute-start | bytes 786440 | tf_op jit(solution)/shard_map/ppermute | solution.py:166
  39.3 1.7 %collective-permute-start.5 = (bf16[4,128,256]{2,1,0:T(8,128)(2,1)S(1)}, bf16[4,128,256]{2,1,0:T(8,128)(2,1)S(1)}, u32[]{:S(2)}, u32[]{:S(2)}) collective-permute-start(bf16[4,128,256]{2,1,0:T(8,128)(2,1)S(1)} %get-tuple-element.37), channel_id=1, source_target_pairs={{0,8},{8,16},{16,24},{24,0},{1,9},{9,17},{17,25},{25,1},{2,10},{10... | collective-permute-start | bytes 786440 | tf_op jit(solution)/shard_map/ppermute | solution.py:166
  40.9 0.0 collective-permute-done.refs_1_
  41.0 0.3 collective-permute-start.7
  41.3 0.0 collective-permute-done.1.refs_2_
  41.3 0.0 copy-done.1
  41.3 3.1 %attend.3 = (f32[8,128,128]{2,1,0:T(8,128)S(1)}, f32[8,128,128]{2,1,0:T(8,128)S(1)}, f32[8,128,128]{2,1,0:T(8,128)S(1)}) custom-call(s32[8]{0:T(128)S(1)} %copy-done.1, bf16[8,128,384]{2,1,0:T(8,128)(2,1)S(1)} %bitcast.10, bf16[8,128,384]{2,1,0:T(8,128)(2,1)S(1)} %bitcast.11, bf16[4,128,256]{2,1,0:T(8,128)(2,1)S(1)} %collective-permute-done.refs_1_, ...), custom_call_target="tpu_custom_call" | custom-call | flops 603979776 | bytes 4194304 | tf_op jit(solution)/shard_map/attend/pallas_call | solution.py:143
  44.4 2.0 %collective-permute-done.2.refs_0_ = bf16[4,128,256]{2,1,0:T(8,128)(2,1)S(1)} collective-permute-done((bf16[4,128,256]{2,1,0:T(8,128)(2,1)S(1)}, bf16[4,128,256]{2,1,0:T(8,128)(2,1)S(1)}, u32[]{:S(2)}, u32[]{:S(2)}) %collective-permute-start.2) | collective-permute-done | bytes 262176 | tf_op jit(solution)/shard_map/ppermute | solution.py:166
  46.4 1.7 %collective-permute-done.3.refs_6_ = bf16[4,128,256]{2,1,0:T(8,128)(2,1)S(1)} collective-permute-done((bf16[4,128,256]{2,1,0:T(8,128)(2,1)S(1)}, bf16[4,128,256]{2,1,0:T(8,128)(2,1)S(1)}, u32[]{:S(2)}, u32[]{:S(2)}) %collective-permute-start.3) | collective-permute-done | bytes 262176 | tf_op jit(solution)/shard_map/ppermute | solution.py:166
  48.1 0.0 collective-permute-start.4
  48.1 0.5 collective-permute-start.9
  48.6 2.5 %collective-permute-done.5.refs_2_ = bf16[4,128,256]{2,1,0:T(8,128)(2,1)S(1)} collective-permute-done((bf16[4,128,256]{2,1,0:T(8,128)(2,1)S(1)}, bf16[4,128,256]{2,1,0:T(8,128)(2,1)S(1)}, u32[]{:S(2)}, u32[]{:S(2)}) %collective-permute-start.5) | collective-permute-done | bytes 262176 | tf_op jit(solution)/shard_map/ppermute | solution.py:166
  51.2 0.0 collective-permute-start.6
  51.2 1.4 %collective-permute-done.7.refs_4_ = bf16[4,128,256]{2,1,0:T(8,128)(2,1)S(1)} collective-permute-done((bf16[4,128,256]{2,1,0:T(8,128)(2,1)S(1)}, bf16[4,128,256]{2,1,0:T(8,128)(2,1)S(1)}, u32[]{:S(2)}, u32[]{:S(2)}) %collective-permute-start.7) | collective-permute-done | bytes 262176 | tf_op jit(solution)/shard_map/ppermute | solution.py:166
  52.6 0.0 collective-permute-start.8
  52.6 0.8 collective-permute-start.10
  53.4 0.0 collective-permute-done.4.refs_1_
  53.4 1.2 %collective-permute-start.11 = (bf16[4,128,256]{2,1,0:T(8,128)(2,1)S(1)}, bf16[4,128,256]{2,1,0:T(8,128)(2,1)S(1)}, u32[]{:S(2)}, u32[]{:S(2)}) collective-permute-start(bf16[4,128,256]{2,1,0:T(8,128)(2,1)S(1)} %collective-permute-done.3.refs_6_), channel_id=1, source_target_pairs={{0,24},{8,0},{16,8},{24,16},{1,25},{9,1},{17,9},{25,17},{2,26},{10... | collective-permute-start | bytes 786440 | tf_op jit(solution)/shard_map/ppermute | solution.py:166
  54.6 0.0 collective-permute-done.9.refs_7_
  54.6 0.0 collective-permute-done.6.refs_3_
  54.6 0.0 collective-permute-done.8.refs_5_
  54.6 6.1 %attend.4 = (f32[8,128,128]{2,1,0:T(8,128)S(1)}, f32[8,128,128]{2,1,0:T(8,128)S(1)}, f32[8,128,128]{2,1,0:T(8,128)S(1)}) custom-call(s32[8]{0:T(128)S(1)} %copy-done.1, bf16[8,128,384]{2,1,0:T(8,128)(2,1)S(1)} %bitcast.12, bf16[4,128,256]{2,1,0:T(8,128)(2,1)S(1)} %collective-permute-done.2.refs_0_, bf16[4,128,256]{2,1,0:T(8,128)(2,1)S(1)} %collective-permute-done.4.refs_1_, ...), custom_call_target="tpu_custom_call" | custom-call | flops 1207959552 | bytes 4194304 | tf_op jit(solution)/shard_map/attend/pallas_call | solution.py:143
  60.8 0.5 collective-permute-done.10.refs_0_
  61.3 1.2 %collective-permute-done.11.refs_2_ = bf16[4,128,256]{2,1,0:T(8,128)(2,1)S(1)} collective-permute-done((bf16[4,128,256]{2,1,0:T(8,128)(2,1)S(1)}, bf16[4,128,256]{2,1,0:T(8,128)(2,1)S(1)}, u32[]{:S(2)}, u32[]{:S(2)}) %collective-permute-start.11) | collective-permute-done | bytes 262176 | tf_op jit(solution)/shard_map/ppermute | solution.py:166
  62.5 0.0 collective-permute-start.12
  62.5 0.5 collective-permute-start.13
  63.0 1.0 %collective-permute-done.12.refs_1_ = bf16[4,128,256]{2,1,0:T(8,128)(2,1)S(1)} collective-permute-done((bf16[4,128,256]{2,1,0:T(8,128)(2,1)S(1)}, bf16[4,128,256]{2,1,0:T(8,128)(2,1)S(1)}, u32[]{:S(2)}, u32[]{:S(2)}) %collective-permute-start.12) | collective-permute-done | bytes 262176 | tf_op jit(solution)/shard_map/ppermute | solution.py:170
  64.1 0.4 collective-permute-done.13.refs_3_
  64.4 4.7 %attend.5 = bf16[8,128,128]{2,1,0:T(8,128)(2,1)} custom-call(s32[8]{0:T(128)S(1)} %copy-done.1, bf16[8,128,384]{2,1,0:T(8,128)(2,1)S(1)} %bitcast.13, bf16[4,128,256]{2,1,0:T(8,128)(2,1)S(1)} %collective-permute-done.10.refs_0_, bf16[4,128,256]{2,1,0:T(8,128)(2,1)S(1)} %collective-permute-done.12.refs_1_, ...), custom_call_target="tpu_custom_call" | custom-call | flops 603979776 | bytes 4194304 | tf_op jit(solution)/shard_map/attend/pallas_call | solution.py:143
  69.1 5.1 %all-to-all-start.1 = ((bf16[32,32,128]{2,1,0:T(8,128)(2,1)}), bf16[32,32,128]{2,1,0:T(8,128)(2,1)S(1)}, u32[]{:S(2)}, u32[]{:S(2)}) async-start(bf16[32,32,128]{2,1,0:T(8,128)(2,1)} %bitcast.4), calls=%async_computation.1 | async-start | bytes 524288 | tf_op jit(solution)/shard_map/all_to_all | solution.py:208
  74.2 0.0 copy-start.2
  74.3 0.6 copy-done.2
  74.9 0.6 dynamic_slice.8
  77.4 0.0 copy-done
  77.4 10.0 %all-to-all-done.1 = bf16[32,32,128]{2,1,0:T(8,128)(2,1)S(1)} async-done(((bf16[32,32,128]{2,1,0:T(8,128)(2,1)}), bf16[32,32,128]{2,1,0:T(8,128)(2,1)S(1)}, u32[]{:S(2)}, u32[]{:S(2)}) %all-to-all-start.1) | async-done | bytes 262176 | tf_op jit(solution)/shard_map/all_to_all | solution.py:208
  87.5 0.1 convert_bitcast_fusion
  87.5 0.3 copy.7
  87.8 0.1 reshape.51
  87.9 0.7 multiply_convert_fusion
  (2 shorter events, 0.1 us)
Async XLA Ops:
  0.0 77.4 %copy-start = (f32[64,4096]{1,0:T(8,128)S(1)}, f32[64,4096]{1,0:T(8,128)}, u32[]{:S(2)}) copy-start(f32[64,4096]{1,0:T(8,128)} %param.11) | copy-start | bytes 3145732
  36.6 4.7 %copy-start.1 = (s32[8]{0:T(128)S(1)}, s32[8]{0:T(128)}, u32[]{:S(2)}) copy-start(s32[8]{0:T(128)} %valid_ref.5) | copy-start | bytes 100
  36.6 4.3 %collective-permute-start = (bf16[4,128,256]{2,1,0:T(8,128)(2,1)S(1)}, bf16[4,128,256]{2,1,0:T(8,128)(2,1)S(1)}, u32[]{:S(2)}, u32[]{:S(2)}) collective-permute-start(bf16[4,128,256]{2,1,0:T(8,128)(2,1)S(1)} %get-tuple-element.38), channel_id=1, source_target_pairs={{0,1},{1,0},{2,3},{3,2},{4,5},{5,4},{6,7},{7,6},{8,9},{9,8},{10,11... | collective-permute-start | bytes 786440 | tf_op jit(solution)/shard_map/ppermute | solution.py:170
  36.7 4.6 %collective-permute-start.1 = (bf16[4,128,256]{2,1,0:T(8,128)(2,1)S(1)}, bf16[4,128,256]{2,1,0:T(8,128)(2,1)S(1)}, u32[]{:S(2)}, u32[]{:S(2)}) collective-permute-start(bf16[4,128,256]{2,1,0:T(8,128)(2,1)S(1)} %get-tuple-element.37), channel_id=1, source_target_pairs={{0,1},{1,0},{2,3},{3,2},{4,5},{5,4},{6,7},{7,6},{8,9},{9,8},{10,11... | collective-permute-start | bytes 786440 | tf_op jit(solution)/shard_map/ppermute | solution.py:170
  37.2 9.2 %collective-permute-start.2 = (bf16[4,128,256]{2,1,0:T(8,128)(2,1)S(1)}, bf16[4,128,256]{2,1,0:T(8,128)(2,1)S(1)}, u32[]{:S(2)}, u32[]{:S(2)}) collective-permute-start(bf16[4,128,256]{2,1,0:T(8,128)(2,1)S(1)} %get-tuple-element.38), channel_id=1, source_target_pairs={{0,8},{8,16},{16,24},{24,0},{1,9},{9,17},{17,25},{25,1},{2,10},{10... | collective-permute-start | bytes 786440 | tf_op jit(solution)/shard_map/ppermute | solution.py:166
  37.7 10.4 %collective-permute-start.3 = (bf16[4,128,256]{2,1,0:T(8,128)(2,1)S(1)}, bf16[4,128,256]{2,1,0:T(8,128)(2,1)S(1)}, u32[]{:S(2)}, u32[]{:S(2)}) collective-permute-start(bf16[4,128,256]{2,1,0:T(8,128)(2,1)S(1)} %get-tuple-element.37), channel_id=1, source_target_pairs={{0,24},{8,0},{16,8},{24,16},{1,25},{9,1},{17,9},{25,17},{2,26},{10... | collective-permute-start | bytes 786440 | tf_op jit(solution)/shard_map/ppermute | solution.py:166
  39.3 11.9 %collective-permute-start.5 = (bf16[4,128,256]{2,1,0:T(8,128)(2,1)S(1)}, bf16[4,128,256]{2,1,0:T(8,128)(2,1)S(1)}, u32[]{:S(2)}, u32[]{:S(2)}) collective-permute-start(bf16[4,128,256]{2,1,0:T(8,128)(2,1)S(1)} %get-tuple-element.37), channel_id=1, source_target_pairs={{0,8},{8,16},{16,24},{24,0},{1,9},{9,17},{17,25},{25,1},{2,10},{10... | collective-permute-start | bytes 786440 | tf_op jit(solution)/shard_map/ppermute | solution.py:166
  41.0 11.6 %collective-permute-start.7 = (bf16[4,128,256]{2,1,0:T(8,128)(2,1)S(1)}, bf16[4,128,256]{2,1,0:T(8,128)(2,1)S(1)}, u32[]{:S(2)}, u32[]{:S(2)}) collective-permute-start(bf16[4,128,256]{2,1,0:T(8,128)(2,1)S(1)} %get-tuple-element.38), channel_id=1, source_target_pairs={{0,24},{8,0},{16,8},{24,16},{1,25},{9,1},{17,9},{25,17},{2,26},{10... | collective-permute-start | bytes 786440 | tf_op jit(solution)/shard_map/ppermute | solution.py:166
  48.1 5.3 %collective-permute-start.4 = (bf16[4,128,256]{2,1,0:T(8,128)(2,1)S(1)}, bf16[4,128,256]{2,1,0:T(8,128)(2,1)S(1)}, u32[]{:S(2)}, u32[]{:S(2)}) collective-permute-start(bf16[4,128,256]{2,1,0:T(8,128)(2,1)S(1)} %collective-permute-done.2.refs_0_), channel_id=1, source_target_pairs={{0,1},{1,0},{2,3},{3,2},{4,5},{5,4},{6,7},{7,6},{8,9},{9,8},{10,11... | collective-permute-start | bytes 786440 | tf_op jit(solution)/shard_map/ppermute | solution.py:170
  48.1 6.5 %collective-permute-start.9 = (bf16[4,128,256]{2,1,0:T(8,128)(2,1)S(1)}, bf16[4,128,256]{2,1,0:T(8,128)(2,1)S(1)}, u32[]{:S(2)}, u32[]{:S(2)}) collective-permute-start(bf16[4,128,256]{2,1,0:T(8,128)(2,1)S(1)} %collective-permute-done.3.refs_6_), channel_id=1, source_target_pairs={{0,1},{1,0},{2,3},{3,2},{4,5},{5,4},{6,7},{7,6},{8,9},{9,8},{10,11... | collective-permute-start | bytes 786440 | tf_op jit(solution)/shard_map/ppermute | solution.py:170
  51.2 3.4 %collective-permute-start.6 = (bf16[4,128,256]{2,1,0:T(8,128)(2,1)S(1)}, bf16[4,128,256]{2,1,0:T(8,128)(2,1)S(1)}, u32[]{:S(2)}, u32[]{:S(2)}) collective-permute-start(bf16[4,128,256]{2,1,0:T(8,128)(2,1)S(1)} %collective-permute-done.5.refs_2_), channel_id=1, source_target_pairs={{0,1},{1,0},{2,3},{3,2},{4,5},{5,4},{6,7},{7,6},{8,9},{9,8},{10,11... | collective-permute-start | bytes 786440 | tf_op jit(solution)/shard_map/ppermute | solution.py:170
  52.6 2.0 %collective-permute-start.8 = (bf16[4,128,256]{2,1,0:T(8,128)(2,1)S(1)}, bf16[4,128,256]{2,1,0:T(8,128)(2,1)S(1)}, u32[]{:S(2)}, u32[]{:S(2)}) collective-permute-start(bf16[4,128,256]{2,1,0:T(8,128)(2,1)S(1)} %collective-permute-done.7.refs_4_), channel_id=1, source_target_pairs={{0,1},{1,0},{2,3},{3,2},{4,5},{5,4},{6,7},{7,6},{8,9},{9,8},{10,11... | collective-permute-start | bytes 786440 | tf_op jit(solution)/shard_map/ppermute | solution.py:170
  52.6 8.7 %collective-permute-start.10 = (bf16[4,128,256]{2,1,0:T(8,128)(2,1)S(1)}, bf16[4,128,256]{2,1,0:T(8,128)(2,1)S(1)}, u32[]{:S(2)}, u32[]{:S(2)}) collective-permute-start(bf16[4,128,256]{2,1,0:T(8,128)(2,1)S(1)} %collective-permute-done.2.refs_0_), channel_id=1, source_target_pairs={{0,8},{8,16},{16,24},{24,0},{1,9},{9,17},{17,25},{25,1},{2,10},{10... | collective-permute-start | bytes 786440 | tf_op jit(solution)/shard_map/ppermute | solution.py:166
  53.4 9.1 %collective-permute-start.11 = (bf16[4,128,256]{2,1,0:T(8,128)(2,1)S(1)}, bf16[4,128,256]{2,1,0:T(8,128)(2,1)S(1)}, u32[]{:S(2)}, u32[]{:S(2)}) collective-permute-start(bf16[4,128,256]{2,1,0:T(8,128)(2,1)S(1)} %collective-permute-done.3.refs_6_), channel_id=1, source_target_pairs={{0,24},{8,0},{16,8},{24,16},{1,25},{9,1},{17,9},{25,17},{2,26},{10... | collective-permute-start | bytes 786440 | tf_op jit(solution)/shard_map/ppermute | solution.py:166
  62.5 1.5 %collective-permute-start.12 = (bf16[4,128,256]{2,1,0:T(8,128)(2,1)S(1)}, bf16[4,128,256]{2,1,0:T(8,128)(2,1)S(1)}, u32[]{:S(2)}, u32[]{:S(2)}) collective-permute-start(bf16[4,128,256]{2,1,0:T(8,128)(2,1)S(1)} %collective-permute-done.10.refs_0_), channel_id=1, source_target_pairs={{0,1},{1,0},{2,3},{3,2},{4,5},{5,4},{6,7},{7,6},{8,9},{9,8},{10,11... | collective-permute-start | bytes 786440 | tf_op jit(solution)/shard_map/ppermute | solution.py:170
  62.5 1.9 %collective-permute-start.13 = (bf16[4,128,256]{2,1,0:T(8,128)(2,1)S(1)}, bf16[4,128,256]{2,1,0:T(8,128)(2,1)S(1)}, u32[]{:S(2)}, u32[]{:S(2)}) collective-permute-start(bf16[4,128,256]{2,1,0:T(8,128)(2,1)S(1)} %collective-permute-done.11.refs_2_), channel_id=1, source_target_pairs={{0,1},{1,0},{2,3},{3,2},{4,5},{5,4},{6,7},{7,6},{8,9},{9,8},{10,11... | collective-permute-start | bytes 786440 | tf_op jit(solution)/shard_map/ppermute | solution.py:170
  69.1 18.3 %all-to-all-start.1 = ((bf16[32,32,128]{2,1,0:T(8,128)(2,1)}), bf16[32,32,128]{2,1,0:T(8,128)(2,1)S(1)}, u32[]{:S(2)}, u32[]{:S(2)}) async-start(bf16[32,32,128]{2,1,0:T(8,128)(2,1)} %bitcast.4), calls=%async_computation.1 | async-start | bytes 524288 | tf_op jit(solution)/shard_map/all_to_all | solution.py:208
  74.2 0.7 copy-start.2

commit v3 on v2

v3 whole, which is shorter than its diff:
```python
import functools
import math

import jax
import jax.numpy as jnp
from jax import lax
from jax.experimental import pallas as pl
from jax.experimental.pallas import tpu as pltpu
from jax.sharding import Mesh
from jax.sharding import PartitionSpec as P

HD = 128
AX = ("group", "y")
DEAD = -3.0e38
VMEM = pltpu.VMEM
MIB = 1024 * 1024


def pack_kernel(n, *refs):
    out, held, sems = refs[n], refs[n + 1], refs[n + 2]
    copies = [pltpu.make_async_copy(refs[i], held.at[i], sems.at[i]) for i in range(n)]
    for copy in copies:
        copy.start()
    for i in range(n):
        copies[i].wait()
        for h in range(out.shape[0]):
            out[h, :, i * HD : (i + 1) * HD] = held[i, :, h * HD : (h + 1) * HD]


def pack(*arrays):
    tokens, width = arrays[0].shape
    n = len(arrays)
    return pl.pallas_call(
        functools.partial(pack_kernel, n),
        out_shape=jax.ShapeDtypeStruct((width // HD, tokens, n * HD), arrays[0].dtype),
        in_specs=[pl.BlockSpec(memory_space=pl.ANY)] * n,
        out_specs=pl.BlockSpec(memory_space=VMEM),
        scratch_shapes=[
            pltpu.VMEM((n, tokens, width), arrays[0].dtype),
            pltpu.SemaphoreType.DMA((n,)),
        ],
        compiler_params=pltpu.CompilerParams(vmem_limit_bytes=60 * MIB),
        name="pack",
    )(*arrays)


def cross_kernel(dists, valid_ref, qkv_ref, far_ref, *refs):
    if dists is None:
        olds, dists = None, (0, 0)
        outs, scores = refs[:6], refs[6:]
    else:
        low_ref, high_ref = refs[:2]
        olds, outs, scores = refs[2:8], refs[8:14], refs[14:]
    own = olds is None
    groups, rows, _ = qkv_ref.shape
    half = groups // 2
    x = lax.axis_index("x")
    core = lax.axis_index("core")
    lane = lax.broadcasted_iota(jnp.int32, (1, 2 * rows), 1)
    place = lane % rows
    spread = (place // 32) * 64 + place % 32 + core * 32
    scale = math.log2(math.e) / math.sqrt(HD)
    wide = (4 * rows, 2 * rows)
    row = lax.broadcasted_iota(jnp.int32, wide, 0)
    ahead = (row % (2 * rows) < rows) & (lax.broadcasted_iota(jnp.int32, wide, 1) >= rows)

    def load(t, columns):
        if own:
            ref, at = qkv_ref, 2 * t
        elif 2 * t < half:
            ref, at = low_ref, 2 * t
        else:
            ref, at = high_ref, 2 * t - half
        return ref[at : at + 2, :, columns].reshape(2 * rows, HD)

    live = []
    for t in range(half):
        token = spread + lax.rem(x + dists[2 * t >= half], 4) * 256
        live.append(token < jnp.where(lane < rows, valid_ref[2 * t], valid_ref[2 * t + 1]))
    def queries(p):
        pair = slice(2 * p, 2 * p + 2)
        return jnp.concatenate(
            [
                qkv_ref[pair, :, 2 * HD :].reshape(2 * rows, HD),
                far_ref[pair].reshape(2 * rows, HD),
            ],
            axis=0,
        )

    def score(p, t, q, most):
        part = lax.dot_general(
            q, load(t, slice(0, HD)), (((1,), (1,)), ((), ())), preferred_element_type=jnp.float32
        )
        part = jnp.where(live[t], part, DEAD)
        if t == p:
            part = jnp.where(ahead, DEAD, part)
        scores[p % 2][t] = part
        part = jnp.maximum(part[:, :HD], part[:, HD:])
        return part if most is None else jnp.maximum(most, part)

    most = score(0, 0, queries(0), None)
    for p in range(half):
        pair = slice(2 * p, 2 * p + 2)
        top = jnp.broadcast_to(jnp.max(most, axis=1, keepdims=True), most.shape)
        if own:
            acc = jnp.zeros((4 * rows, HD), jnp.float32)
            total = jnp.zeros((4 * rows, HD), jnp.float32)
        else:
            acc, old, total = (
                jnp.concatenate(
                    [olds[i][pair].reshape(2 * rows, HD), olds[3 + i][pair].reshape(2 * rows, HD)],
                    axis=0,
                )
                for i in range(3)
            )
            top = jnp.maximum(top, old)
            keep = jnp.exp2((old - top) * scale)
            acc = acc * keep
            total = total * keep
        both = jnp.concatenate([top, top], axis=1)
        most = None
        if p + 1 < half:
            q = queries(p + 1)
            most = score(p + 1, 0, q, most)
        for t in range(p + 1):
            if p + 1 < half:
                most = score(p + 1, t + 1, q, most)
            weight = jnp.exp2((scores[p % 2][t] - both) * scale)
            total = total + (weight[:, :HD] + weight[:, HD:])
            acc = acc + jnp.dot(
                weight.astype(jnp.bfloat16),
                load(t, slice(HD, 2 * HD)),
                preferred_element_type=jnp.float32,
            )
        state = (acc, top, total)
        for i in range(2):
            mine = slice(2 * i * rows, 2 * (i + 1) * rows)
            for k, value in enumerate(state):
                outs[len(state) * i + k][pair] = value[mine].reshape(2, rows, HD)


def cross(valid, qkv, far, low=None, high=None, dists=None, state=()):
    groups, rows, _ = qkv.shape
    whole = pl.BlockSpec(memory_space=VMEM)
    arrays = [] if dists is None else [low, high]
    pairs = groups * (groups + 2) * rows * rows
    return pl.pallas_call(
        functools.partial(cross_kernel, dists),
        out_shape=[jax.ShapeDtypeStruct((groups, rows, HD), jnp.float32)] * 6,
        in_specs=[pl.BlockSpec(memory_space=pltpu.SMEM)]
        + [whole] * (2 + len(arrays) + len(state)),
        out_specs=[whole] * 6,
        scratch_shapes=[pltpu.VMEM((groups // 2, 4 * rows, 2 * rows), jnp.float32)] * 2,

        compiler_params=pltpu.CompilerParams(vmem_limit_bytes=24 * MIB),
        cost_estimate=pl.CostEstimate(
            flops=4 * pairs * HD, bytes_accessed=4 * MIB, transcendentals=pairs
        ),
        name="cross",
    )(valid, qkv, far, *arrays, *state)


def attend_kernel(sets, count_in, valid_ref, qkv_ref, *refs):
    n = sum(len(places) for places in sets)
    kv_in, refs = refs[:n], refs[n:]
    states = [refs[3 * i : 3 * i + 3] for i in range(count_in)]
    refs = refs[3 * count_in :]
    out_ref, scores, held, sems = refs[0], refs[1:3], refs[3], refs[4]
    copies = []
    groups, rows, _ = qkv_ref.shape
    x = lax.axis_index("x")
    core = lax.axis_index("core")
    lane = lax.broadcasted_iota(jnp.int32, (1, 2 * rows), 1)
    side = jnp.where(lane < rows, core, 1 - core)
    lane = lane % rows
    spread = (lane // 32) * 64 + lane % 32 + side * 32
    tiles = []
    for j in range(groups):
        at = 0
        for places in sets:
            here = {}
            for dist, side, start, count in places:
                if start <= j < start + count:
                    here[side] = (kv_in[at], j - start, dist)
                at += 1
            live = spread + lax.rem(x + here[0][2], 4) * 256 < valid_ref[j]
            tiles.append((j, here[0][:2], here[1][:2], live))

    def load(tile, columns):
        return jnp.concatenate([ref[at, :, columns] for ref, at in tile[1:3]], axis=0)

    scale = math.log2(math.e) / math.sqrt(HD)
    early = lax.broadcasted_iota(jnp.int32, (2 * rows, 2 * rows), 0) < rows
    pairs = groups // 2

    def used(p):
        return [tile for tile in tiles if tile[0] < 2 * p + 2]

    def score(p, i, most):
        if p >= pairs or i >= len(used(p)):
            return most
        tile = used(p)[i]
        part = lax.dot_general(
            qkv_ref[2 * p : 2 * p + 2, :, 2 * HD :].reshape(2 * rows, HD),
            load(tile, slice(0, HD)),
            (((1,), (1,)), ((), ())),
            preferred_element_type=jnp.float32,
        )
        part = jnp.where(tile[3], part, DEAD)
        if tile[0] == 2 * p + 1:
            part = jnp.where(early, DEAD, part)
        scores[p % 2][i] = part
        part = jnp.maximum(part[:, :HD], part[:, HD:])
        return part if most is None else jnp.maximum(most, part)

    most = None
    for i in range(len(used(0))):
        most = score(0, i, most)
    for p in range(pairs):
        pair = slice(2 * p, 2 * p + 2)
        top = jnp.broadcast_to(jnp.max(most, axis=1, keepdims=True), most.shape)
        olds = [[ref[pair].reshape(2 * rows, HD) for ref in state] for state in states]
        for _, old, _ in olds:
            top = jnp.maximum(top, old)
        acc = jnp.zeros((2 * rows, HD), jnp.float32)
        total = jnp.zeros((2 * rows, HD), jnp.float32)
        for acc_in, old, total_in in olds:
            keep = jnp.exp2((old - top) * scale)
            acc = acc + acc_in * keep
            total = total + total_in * keep
        both = jnp.concatenate([top, top], axis=1)
        most = None
        for i in range(len(tiles) // pairs):
            most = score(p + 1, i, most)
        for i, tile in enumerate(used(p)):
            most = score(p + 1, len(tiles) // pairs + i, most)
            weight = jnp.exp2((scores[p % 2][i] - both) * scale)
            total = total + (weight[:, :HD] + weight[:, HD:])
            acc = acc + jnp.dot(
                weight.astype(jnp.bfloat16),
                load(tile, slice(HD, 2 * HD)),
                preferred_element_type=jnp.float32,
            )
        attended = acc / jnp.sum(total, axis=1, keepdims=True)
        at = lax.broadcasted_iota(jnp.int32, (rows, 1), 0)
        at = (at // 32) * 64 + at % 32 + x * 256 + core * 32
        for c in (2 * p, 2 * p + 1):
            part = attended[:rows] if c == 2 * p else attended[rows:]
            part = jnp.where(at < valid_ref[c], part, 0.0)
            held[c] = part.astype(held.dtype)
        copies.append(pltpu.make_async_copy(held.at[pair], out_ref.at[pair], sems.at[p]))
        copies[-1].start()
    for copy in copies:
        copy.wait()


def attend(valid, qkv, sets, state):
    groups, rows, _ = qkv.shape
    arrays = [piece[0] for pieces in sets for piece in pieces]
    places = [[piece[1:] for piece in pieces] for pieces in sets]
    pairs = groups * (groups + 1) * rows * rows * len(sets)
    whole = pl.BlockSpec(memory_space=VMEM)
    shape = (groups, rows, HD)
    return pl.pallas_call(
        functools.partial(attend_kernel, places, len(state) // 3),
        out_shape=jax.ShapeDtypeStruct(shape, jnp.bfloat16),
        in_specs=[pl.BlockSpec(memory_space=pltpu.SMEM)]
        + [whole] * (1 + len(arrays) + len(state)),
        out_specs=pl.BlockSpec(memory_space=pltpu.HBM),
        scratch_shapes=[
            pltpu.VMEM((groups * len(sets), 2 * rows, 2 * rows), jnp.float32),
            pltpu.VMEM((groups * len(sets), 2 * rows, 2 * rows), jnp.float32),
            pltpu.VMEM(shape, jnp.bfloat16),
            pltpu.SemaphoreType.DMA((groups // 2,)),
        ],
        compiler_params=pltpu.CompilerParams(vmem_limit_bytes=24 * MIB),
        cost_estimate=pl.CostEstimate(
            flops=4 * pairs * HD, bytes_accessed=4 * MIB, transcendentals=pairs
        ),
        name="attend",
    )(valid, qkv, *arrays, *state)


def shift(value, by):
    n = lax.axis_size("x")
    return lax.ppermute(value, "x", [(i, (i + by) % n) for i in range(n)])


def swap(value):
    return lax.ppermute(value, "core", [(0, 1), (1, 0)])


def shards(queries, keys, values, valid, levels, gate_table):
    tokens, width = queries.shape[1:]
    groups = lax.axis_size("group")
    qkv = lax.all_to_all(pack(keys[0], values[0], queries[0]), AX, 0, 0, tiled=True)
    qkv = qkv.reshape(groups, -1, 3 * HD)
    half = groups // 2
    low, high = qkv[:half, :, : 2 * HD], qkv[half:, :, : 2 * HD]
    far = swap(qkv[:, :, 2 * HD :])
    low_l, high_r = shift(low, 1), shift(high, -1)
    high_l, low_r = shift(high, 1), shift(low, -1)
    state = cross(valid, qkv, far)
    state, low_l, high_r = lax.optimization_barrier((state, low_l, high_r))
    low_o, high_o = shift(low_l, 1), shift(high_r, -1)
    state = cross(valid, qkv, far, low_l, high_r, (3, 1), state)
    state, low_r, high_l = lax.optimization_barrier((state, low_r, high_l))
    state = cross(valid, qkv, far, low_r, high_l, (1, 3), state)
    rest = [
        (low_o, 2, 0, 0, half),
        (swap(low_o), 2, 1, 0, half),
        (high_o, 2, 0, half, half),
        (swap(high_o), 2, 1, half, half),
    ]
    state = [*state[:3], *(swap(part) for part in state[3:])]
    attended = attend(valid, qkv, [rest], state)
    returned = lax.all_to_all(attended.reshape(-1, tokens, HD), AX, 0, 0, tiled=True)
    own = lax.axis_index("group")
    level = lax.dynamic_index_in_dim(levels, own, 0, keepdims=False)
    gate = lax.dynamic_index_in_dim(gate_table, level, 0, keepdims=True)
    mixed = returned.transpose(1, 0, 2).reshape(tokens, width).astype(jnp.float32) * gate
    return mixed.astype(jnp.bfloat16)[None]


def solution(mesh):
    fine = Mesh(mesh.devices.reshape(8, 4, 4, 2), ("group", "x", "y", "core"))
    rows = P("group", ("x", "y", "core"), None)
    return jax.shard_map(
        shards,
        mesh=fine,
        in_specs=(rows, rows, rows, P(), P(), P()),
        out_specs=rows,
        check_vma=False,
    )
```

time: 89 us -> 84.5 us (0.949)
  waiting for transfers between devices: 20.8 us -> 16.6 us
  Pallas kernels: 16.1 us -> 15.1 us
  starting transfers between devices: 12.8 us -> 13.7 us
    ppermute x6, waiting for transfers between devices: 9.39 us -> 3.84 us  [shift(): return lax.ppermute(value, 'x', [(i, (i + by) % n) for i in range(n)])]
    ppermute x6, starting transfers between devices: 6.08 us -> 7.37 us  [shift(): return lax.ppermute(value, 'x', [(i, (i + by) % n) for i in range(n)])]
    ppermute x8 -> x6, waiting for transfers between devices: 1.41 us -> 2.47 us  [swap(): return lax.ppermute(value, 'core', [(0, 1), (1, 0)])]
    pallas_call x3 -> x4, Pallas kernels: 14 us -> 13 us  [the longest x3 9.07 us: cross(): pl.pallas_call(functools.partial(cross_kernel, dists), out_shape=[jax.Sha...]
  transfers between devices with their start and end apart: 15 -> 13, of which waited for: 9 -> 7; matrix products, arithmetic and copies ran while one was open for 1% -> 1% of each run, Pallas kernels for 10% -> 11%
where the time goes in v3:
time: 84.5 us; the launch traced here: 84.1 us
  blocking collectives  34.4 us (41%)
  waiting for transfers between devices  16.6 us (20%)
  Pallas kernels  15.1 us (18%)
  starting transfers between devices  13.7 us (16%)
  between operations  1.83 us (2%)
  local copies, waits for them, and re-layouts  1.75 us (2%)
    all_to_all x1, blocking collectives, shards(): lax.all_to_all(pack(keys[0], values[0], queries[0]), AX, 0, 0, tiled=True)  34.4 us
    all_to_all x1, waiting for transfers between devices, shards(): lax.all_to_all(attended.reshape(-1, tokens, HD), AX, 0, 0, tiled=True)  10.3 us
    pallas_call x3, Pallas kernels, cross(): pl.pallas_call(functools.partial(cross_kernel, dists), out_shape=[jax.Sha...  9.07 us
    ppermute x6, starting transfers between devices, shift(): return lax.ppermute(value, 'x', [(i, (i + by) % n) for i in range(n)])  7.37 us
    all_to_all x1, starting transfers between devices, shards(): lax.all_to_all(attended.reshape(-1, tokens, HD), AX, 0, 0, tiled=True)  5.1 us
    pallas_call x1, Pallas kernels, attend(): pl.pallas_call(functools.partial(attend_kernel, places, len(state) // 3),...  3.88 us
    ppermute x6, waiting for transfers between devices, shift(): return lax.ppermute(value, 'x', [(i, (i + by) % n) for i in range(n)])  3.84 us
    ppermute x6, waiting for transfers between devices, swap(): return lax.ppermute(value, 'core', [(0, 1), (1, 0)])  2.47 us
  transfers between devices with their start and end apart: 13, of which 7 were waited for; matrix products, arithmetic and copies ran while one was open for 1% of the time, Pallas kernels for 11%

profile of v3, /device:TPU:6, one launch (start us, length us, event | category | flops | bytes accessed | tf_op | source)
XLA Modules:
  0.0 84.1 jit_solution(10030671455228263051)
XLA Ops:
  0.0 0.0 copy-start
  0.0 2.1 %pack.1 = bf16[32,32,384]{2,1,0:T(8,128)(2,1)} custom-call(bf16[32,4096]{1,0:T(8,128)(2,1)} %bitcast.15, bf16[32,4096]{1,0:T(8,128)(2,1)} %bitcast.16, bf16[32,4096]{1,0:T(8,128)(2,1)} %bitcast.17), custom_call_target="tpu_custom_call" | custom-call | tf_op jit(solution)/shard_map/pack/pallas_call | solution.py:33
  2.2 34.4 %all_to_all.10 = bf16[32,32,384]{2,1,0:T(8,128)(2,1)S(1)} all-to-all(bf16[32,32,384]{2,1,0:T(8,128)(2,1)} %pack.1), channel_id=1, replica_groups=mesh['group'=8,'x'=4,'y'=4,'core'=2] {'group','y'}, dimensions={0} | all-to-all | bytes 1572864 | tf_op jit(solution)/shard_map/all_to_all | solution.py:296
  36.6 0.1 collective-permute-start
  36.8 0.0 copy-start.1
  36.8 0.6 collective-permute-start.1
  37.4 1.5 %collective-permute-start.2 = (bf16[4,128,256]{2,1,0:T(8,128)(2,1)S(1)}, bf16[4,128,256]{2,1,0:T(8,128)(2,1)S(1)}, u32[]{:S(2)}, u32[]{:S(2)}) collective-permute-start(bf16[4,128,256]{2,1,0:T(8,128)(2,1)S(1)} %get-tuple-element.73), channel_id=1, source_target_pairs={{0,24},{8,0},{16,8},{24,16},{1,25},{9,1},{17,9},{25,17},{2,26},{10... | collective-permute-start | bytes 786440 | tf_op jit(solution)/shard_map/ppermute | solution.py:286
  38.9 0.8 collective-permute-start.7
  39.7 2.4 %collective-permute-start.8 = (bf16[4,128,256]{2,1,0:T(8,128)(2,1)S(1)}, bf16[4,128,256]{2,1,0:T(8,128)(2,1)S(1)}, u32[]{:S(2)}, u32[]{:S(2)}) collective-permute-start(bf16[4,128,256]{2,1,0:T(8,128)(2,1)S(1)} %get-tuple-element.73), channel_id=1, source_target_pairs={{0,8},{8,16},{16,24},{24,0},{1,9},{9,17},{17,25},{25,1},{2,10},{10... | collective-permute-start | bytes 786440 | tf_op jit(solution)/shard_map/ppermute | solution.py:286
  42.1 0.0 collective-permute-done.far_ref
  42.1 0.0 copy-done.1
  42.1 2.9 %cross.3 = (f32[8,128,128]{2,1,0:T(8,128)S(1)}, f32[8,128,128]{2,1,0:T(8,128)S(1)}, f32[8,128,128]{2,1,0:T(8,128)S(1)}, f32[8,128,128]{2,1,0:T(8,128)S(1)}, f32[...) custom-call(s32[8]{0:T(128)S(1)} %copy-done.1, bf16[8,128,384]{2,1,0:T(8,128)(2,1)S(1)} %bitcast.11, ...), custom_call_target="tpu_custom_call" | custom-call | flops 671088640 | bytes 4194304 | tf_op jit(solution)/shard_map/cross/pallas_call | solution.py:147
  45.0 1.0 %collective-permute-done.1.refs_0_ = bf16[4,128,256]{2,1,0:T(8,128)(2,1)S(1)} collective-permute-done((bf16[4,128,256]{2,1,0:T(8,128)(2,1)S(1)}, bf16[4,128,256]{2,1,0:T(8,128)(2,1)S(1)}, u32[]{:S(2)}, u32[]{:S(2)}) %collective-permute-start.1) | collective-permute-done | bytes 262176 | tf_op jit(solution)/shard_map/ppermute | solution.py:286
  46.0 1.7 %collective-permute-done.2.refs_1_ = bf16[4,128,256]{2,1,0:T(8,128)(2,1)S(1)} collective-permute-done((bf16[4,128,256]{2,1,0:T(8,128)(2,1)S(1)}, bf16[4,128,256]{2,1,0:T(8,128)(2,1)S(1)}, u32[]{:S(2)}, u32[]{:S(2)}) %collective-permute-start.2) | collective-permute-done | bytes 262176 | tf_op jit(solution)/shard_map/ppermute | solution.py:286
  47.7 0.3 collective-permute-start.3
  48.0 1.7 %collective-permute-start.5 = (bf16[4,128,256]{2,1,0:T(8,128)(2,1)S(1)}, bf16[4,128,256]{2,1,0:T(8,128)(2,1)S(1)}, u32[]{:S(2)}, u32[]{:S(2)}) collective-permute-start(bf16[4,128,256]{2,1,0:T(8,128)(2,1)S(1)} %collective-permute-done.2.refs_1_), channel_id=1, source_target_pairs={{0,24},{8,0},{16,8},{24,16},{1,25},{9,1},{17,9},{25,17},{2,26},{10... | collective-permute-start | bytes 786440 | tf_op jit(solution)/shard_map/ppermute | solution.py:286
  49.7 3.1 %cross.4 = (f32[8,128,128]{2,1,0:T(8,128)S(1)}, f32[8,128,128]{2,1,0:T(8,128)S(1)}, f32[8,128,128]{2,1,0:T(8,128)S(1)}, f32[8,128,128]{2,1,0:T(8,128)S(1)}, f32[...) custom-call(s32[8]{0:T(128)S(1)} %copy-done.1, bf16[8,128,384]{2,1,0:T(8,128)(2,1)S(1)} %bitcast.12, ...), custom_call_target="tpu_custom_call" | custom-call | flops 671088640 | bytes 4194304 | tf_op jit(solution)/shard_map/cross/pallas_call | solution.py:147
  52.8 0.5 collective-permute-done.7.refs_0_
  53.3 0.0 collective-permute-done.8.refs_1_
  53.3 3.1 %cross.5 = (f32[8,128,128]{2,1,0:T(8,128)S(1)}, f32[8,128,128]{2,1,0:T(8,128)S(1)}, f32[8,128,128]{2,1,0:T(8,128)S(1)}, f32[8,128,128]{2,1,0:T(8,128)S(1)}, f32[...) custom-call(s32[8]{0:T(128)S(1)} %copy-done.1, bf16[8,128,384]{2,1,0:T(8,128)(2,1)S(1)} %bitcast.13, ...), custom_call_target="tpu_custom_call" | custom-call | flops 671088640 | bytes 4194304 | tf_op jit(solution)/shard_map/cross/pallas_call | solution.py:147
  56.4 0.1 collective-permute-start.10
  56.5 0.5 collective-permute-start.11
  57.0 0.1 collective-permute-start.9
  57.1 0.0 collective-permute-done.3.refs_0_
  57.1 0.4 collective-permute-start.4
  57.5 0.7 collective-permute-done.5.refs_2_
  58.2 0.0 collective-permute-start.6
  58.2 2.1 %collective-permute-done.4.refs_1_ = bf16[4,128,256]{2,1,0:T(8,128)(2,1)S(1)} collective-permute-done((bf16[4,128,256]{2,1,0:T(8,128)(2,1)S(1)}, bf16[4,128,256]{2,1,0:T(8,128)(2,1)S(1)}, u32[]{:S(2)}, u32[]{:S(2)}) %collective-permute-start.4) | collective-permute-done | bytes 262176 | tf_op jit(solution)/shard_map/ppermute | solution.py:290
  60.3 0.4 collective-permute-done.6.refs_3_
  60.7 0.0 collective-permute-done.10.refs_8_
  60.7 0.0 collective-permute-done.11.refs_9_
  60.7 0.0 collective-permute-done.9.refs_7_
  60.7 3.9 %attend.1 = bf16[8,128,128]{2,1,0:T(8,128)(2,1)} custom-call(s32[8]{0:T(128)S(1)} %copy-done.1, bf16[8,128,384]{2,1,0:T(8,128)(2,1)S(1)} %bitcast.14, bf16[4,128,256]{2,1,0:T(8,128)(2,1)S(1)} %collective-permute-done.3.refs_0_, bf16[4,128,256]{2,1,0:T(8,128)(2,1)S(1)} %collective-permute-done.4.refs_1_, ...), custom_call_target="tpu_custom_call" | custom-call | flops 603979776 | bytes 4194304 | tf_op jit(solution)/shard_map/attend/pallas_call | solution.py:264
  64.6 5.1 %all-to-all-start.1 = ((bf16[32,32,128]{2,1,0:T(8,128)(2,1)}), bf16[32,32,128]{2,1,0:T(8,128)(2,1)S(1)}, u32[]{:S(2)}, u32[]{:S(2)}) async-start(bf16[32,32,128]{2,1,0:T(8,128)(2,1)} %bitcast.4), calls=%async_computation.1 | async-start | bytes 524288 | tf_op jit(solution)/shard_map/all_to_all | solution.py:317
  69.7 0.0 copy-start.2
  69.7 0.6 copy-done.2
  70.4 0.6 dynamic_slice.8
  72.6 0.0 copy-done
  72.7 10.3 %all-to-all-done.1 = bf16[32,32,128]{2,1,0:T(8,128)(2,1)S(1)} async-done(((bf16[32,32,128]{2,1,0:T(8,128)(2,1)}), bf16[32,32,128]{2,1,0:T(8,128)(2,1)S(1)}, u32[]{:S(2)}, u32[]{:S(2)}) %all-to-all-start.1) | async-done | bytes 262176 | tf_op jit(solution)/shard_map/all_to_all | solution.py:317
  83.0 0.3 copy.7
  83.3 0.1 reshape.51
  83.4 0.7 multiply_convert_fusion
  (4 shorter events, 0.2 us)
Async XLA Ops:
  0.0 72.6 %copy-start = (f32[64,4096]{1,0:T(8,128)S(1)}, f32[64,4096]{1,0:T(8,128)}, u32[]{:S(2)}) copy-start(f32[64,4096]{1,0:T(8,128)} %param.11) | copy-start | bytes 3145732
  36.6 5.5 %collective-permute-start = (bf16[8,128,128]{2,1,0:T(8,128)(2,1)S(1)}, bf16[8,128,128]{2,1,0:T(8,128)(2,1)S(1)}, u32[]{:S(2)}, u32[]{:S(2)}) collective-permute-start(bf16[8,128,128]{2,1,0:T(8,128)(2,1)S(1)} %slice.12), channel_id=1, source_target_pairs={{0,1},{1,0},{2,3},{3,2},{4,5},{5,4},{6,7},{7,6},{8,9},{9,8},{10,11... | collective-permute-start | bytes 786440 | tf_op jit(solution)/shard_map/ppermute | solution.py:290
  36.8 5.4 %copy-start.1 = (s32[8]{0:T(128)S(1)}, s32[8]{0:T(128)}, u32[]{:S(2)}) copy-start(s32[8]{0:T(128)} %valid_ref.7) | copy-start | bytes 100
  36.8 9.2 %collective-permute-start.1 = (bf16[4,128,256]{2,1,0:T(8,128)(2,1)S(1)}, bf16[4,128,256]{2,1,0:T(8,128)(2,1)S(1)}, u32[]{:S(2)}, u32[]{:S(2)}) collective-permute-start(bf16[4,128,256]{2,1,0:T(8,128)(2,1)S(1)} %get-tuple-element.74), channel_id=1, source_target_pairs={{0,8},{8,16},{16,24},{24,0},{1,9},{9,17},{17,25},{25,1},{2,10},{10... | collective-permute-start | bytes 786440 | tf_op jit(solution)/shard_map/ppermute | solution.py:286
  37.4 10.4 %collective-permute-start.2 = (bf16[4,128,256]{2,1,0:T(8,128)(2,1)S(1)}, bf16[4,128,256]{2,1,0:T(8,128)(2,1)S(1)}, u32[]{:S(2)}, u32[]{:S(2)}) collective-permute-start(bf16[4,128,256]{2,1,0:T(8,128)(2,1)S(1)} %get-tuple-element.73), channel_id=1, source_target_pairs={{0,24},{8,0},{16,8},{24,16},{1,25},{9,1},{17,9},{25,17},{2,26},{10... | collective-permute-start | bytes 786440 | tf_op jit(solution)/shard_map/ppermute | solution.py:286
  38.9 14.4 %collective-permute-start.7 = (bf16[4,128,256]{2,1,0:T(8,128)(2,1)S(1)}, bf16[4,128,256]{2,1,0:T(8,128)(2,1)S(1)}, u32[]{:S(2)}, u32[]{:S(2)}) collective-permute-start(bf16[4,128,256]{2,1,0:T(8,128)(2,1)S(1)} %get-tuple-element.74), channel_id=1, source_target_pairs={{0,24},{8,0},{16,8},{24,16},{1,25},{9,1},{17,9},{25,17},{2,26},{10... | collective-permute-start | bytes 786440 | tf_op jit(solution)/shard_map/ppermute | solution.py:286
  39.7 13.6 %collective-permute-start.8 = (bf16[4,128,256]{2,1,0:T(8,128)(2,1)S(1)}, bf16[4,128,256]{2,1,0:T(8,128)(2,1)S(1)}, u32[]{:S(2)}, u32[]{:S(2)}) collective-permute-start(bf16[4,128,256]{2,1,0:T(8,128)(2,1)S(1)} %get-tuple-element.73), channel_id=1, source_target_pairs={{0,8},{8,16},{16,24},{24,0},{1,9},{9,17},{17,25},{25,1},{2,10},{10... | collective-permute-start | bytes 786440 | tf_op jit(solution)/shard_map/ppermute | solution.py:286
  47.7 9.4 %collective-permute-start.3 = (bf16[4,128,256]{2,1,0:T(8,128)(2,1)S(1)}, bf16[4,128,256]{2,1,0:T(8,128)(2,1)S(1)}, u32[]{:S(2)}, u32[]{:S(2)}) collective-permute-start(bf16[4,128,256]{2,1,0:T(8,128)(2,1)S(1)} %collective-permute-done.1.refs_0_), channel_id=1, source_target_pairs={{0,8},{8,16},{16,24},{24,0},{1,9},{9,17},{17,25},{25,1},{2,10},{10... | collective-permute-start | bytes 786440 | tf_op jit(solution)/shard_map/ppermute | solution.py:286
  48.0 10.2 %collective-permute-start.5 = (bf16[4,128,256]{2,1,0:T(8,128)(2,1)S(1)}, bf16[4,128,256]{2,1,0:T(8,128)(2,1)S(1)}, u32[]{:S(2)}, u32[]{:S(2)}) collective-permute-start(bf16[4,128,256]{2,1,0:T(8,128)(2,1)S(1)} %collective-permute-done.2.refs_1_), channel_id=1, source_target_pairs={{0,24},{8,0},{16,8},{24,16},{1,25},{9,1},{17,9},{25,17},{2,26},{10... | collective-permute-start | bytes 786440 | tf_op jit(solution)/shard_map/ppermute | solution.py:286
  56.4 4.2 %collective-permute-start.10 = (f32[8,128,128]{2,1,0:T(8,128)S(1)}, f32[8,128,128]{2,1,0:T(8,128)S(1)}, u32[]{:S(2)}, u32[]{:S(2)}) collective-permute-start(f32[8,128,128]{2,1,0:T(8,128)S(1)} %get-tuple-element.71), channel_id=1, source_target_pairs={{0,1},{1,0},{2,3},{3,2},{4,5},{5,4},{6,7},{7,6},{8,9},{9,8},{10,11... | collective-permute-start | bytes 1572872 | tf_op jit(solution)/shard_map/ppermute | solution.py:290
  56.5 4.2 %collective-permute-start.11 = (f32[8,128,128]{2,1,0:T(8,128)S(1)}, f32[8,128,128]{2,1,0:T(8,128)S(1)}, u32[]{:S(2)}, u32[]{:S(2)}) collective-permute-start(f32[8,128,128]{2,1,0:T(8,128)S(1)} %get-tuple-element.72), channel_id=1, source_target_pairs={{0,1},{1,0},{2,3},{3,2},{4,5},{5,4},{6,7},{7,6},{8,9},{9,8},{10,11... | collective-permute-start | bytes 1572872 | tf_op jit(solution)/shard_map/ppermute | solution.py:290
  57.0 3.7 %collective-permute-start.9 = (f32[8,128,128]{2,1,0:T(8,128)S(1)}, f32[8,128,128]{2,1,0:T(8,128)S(1)}, u32[]{:S(2)}, u32[]{:S(2)}) collective-permute-start(f32[8,128,128]{2,1,0:T(8,128)S(1)} %get-tuple-element.70), channel_id=1, source_target_pairs={{0,1},{1,0},{2,3},{3,2},{4,5},{5,4},{6,7},{7,6},{8,9},{9,8},{10,11... | collective-permute-start | bytes 1572872 | tf_op jit(solution)/shard_map/ppermute | solution.py:290
  57.1 3.2 %collective-permute-start.4 = (bf16[4,128,256]{2,1,0:T(8,128)(2,1)S(1)}, bf16[4,128,256]{2,1,0:T(8,128)(2,1)S(1)}, u32[]{:S(2)}, u32[]{:S(2)}) collective-permute-start(bf16[4,128,256]{2,1,0:T(8,128)(2,1)S(1)} %collective-permute-done.3.refs_0_), channel_id=1, source_target_pairs={{0,1},{1,0},{2,3},{3,2},{4,5},{5,4},{6,7},{7,6},{8,9},{9,8},{10,11... | collective-permute-start | bytes 786440 | tf_op jit(solution)/shard_map/ppermute | solution.py:290
  58.2 2.5 %collective-permute-start.6 = (bf16[4,128,256]{2,1,0:T(8,128)(2,1)S(1)}, bf16[4,128,256]{2,1,0:T(8,128)(2,1)S(1)}, u32[]{:S(2)}, u32[]{:S(2)}) collective-permute-start(bf16[4,128,256]{2,1,0:T(8,128)(2,1)S(1)} %collective-permute-done.5.refs_2_), channel_id=1, source_target_pairs={{0,1},{1,0},{2,3},{3,2},{4,5},{5,4},{6,7},{7,6},{8,9},{9,8},{10,11... | collective-permute-start | bytes 786440 | tf_op jit(solution)/shard_map/ppermute | solution.py:290
  64.6 18.3 %all-to-all-start.1 = ((bf16[32,32,128]{2,1,0:T(8,128)(2,1)}), bf16[32,32,128]{2,1,0:T(8,128)(2,1)S(1)}, u32[]{:S(2)}, u32[]{:S(2)}) async-start(bf16[32,32,128]{2,1,0:T(8,128)(2,1)} %bitcast.4), calls=%async_computation.1 | async-start | bytes 524288 | tf_op jit(solution)/shard_map/all_to_all | solution.py:317
  69.7 0.7 copy-start.2

commit v4 on v3

v4 whole, which is shorter than its diff:
```python
import functools
import math

import jax
import jax.numpy as jnp
from jax import lax
from jax.experimental import pallas as pl
from jax.experimental.pallas import tpu as pltpu
from jax.sharding import Mesh
from jax.sharding import PartitionSpec as P

HD = 128
AX = ("group", "y")
DEAD = -3.0e38
VMEM = pltpu.VMEM
MIB = 1024 * 1024


def pack_kernel(n, *refs):
    out, held, packed, sems = refs[n], refs[n + 1], refs[n + 2], refs[n + 3]
    loads = [pltpu.make_async_copy(refs[i], held.at[i], sems.at[i]) for i in range(n)]
    for copy in loads:
        copy.start()
    stores = []
    for i in range(n):
        loads[i].wait()
        for h in range(out.shape[0]):
            packed[i, h] = held[i, :, h * HD : (h + 1) * HD]
        place = out.at[:, :, pl.ds(i * HD, HD)]
        stores.append(pltpu.make_async_copy(packed.at[i], place, sems.at[n + i]))
        stores[-1].start()
    for copy in stores:
        copy.wait()


def pack(*arrays):
    tokens, width = arrays[0].shape
    n = len(arrays)
    heads = width // HD
    return pl.pallas_call(
        functools.partial(pack_kernel, n),
        out_shape=jax.ShapeDtypeStruct((heads, tokens, n * HD), arrays[0].dtype),
        in_specs=[pl.BlockSpec(memory_space=pl.ANY)] * n,
        out_specs=pl.BlockSpec(memory_space=pl.ANY),
        scratch_shapes=[
            pltpu.VMEM((n, tokens, width), arrays[0].dtype),
            pltpu.VMEM((n, heads, tokens, HD), arrays[0].dtype),
            pltpu.SemaphoreType.DMA((2 * n,)),
        ],
        compiler_params=pltpu.CompilerParams(vmem_limit_bytes=60 * MIB),
        name="pack",
    )(*arrays)


def attend_kernel(dists, other, wide, count_in, last, valid_ref, qkv_ref, *refs):
    refs = list(refs)

    def take(n):
        part, refs[:] = refs[:n], refs[n:]
        return part

    sets = 2 if wide else 1
    far = take(wide)
    own = dists is None
    if own:
        dists = (0, 0)
    else:
        low_ref, high_ref = take(2)
    olds = [take(3 * sets) for _ in range(count_in)]
    if last:
        (out_ref,) = take(1)
        held, sems = refs[2:]
    else:
        outs = take(3 * sets)
    scores = refs[:2]
    groups, rows, _ = qkv_ref.shape
    half = groups // 2
    x = lax.axis_index("x")
    core = lax.axis_index("core")
    copies = []
    lane = lax.broadcasted_iota(jnp.int32, (1, 2 * rows), 1)
    place = lane % rows
    spread = (place // 32) * 64 + place % 32 + (1 - core if other else core) * 32
    scale = math.log2(math.e) / math.sqrt(HD)
    shape = (2 * sets * rows, 2 * rows)
    row = lax.broadcasted_iota(jnp.int32, shape, 0)
    ahead = (row % (2 * rows) < rows) & (lax.broadcasted_iota(jnp.int32, shape, 1) >= rows)

    def load(t, columns):
        if own:
            ref, at = qkv_ref, 2 * t
        elif 2 * t < half:
            ref, at = low_ref, 2 * t
        else:
            ref, at = high_ref, 2 * t - half
        return ref[at : at + 2, :, columns].reshape(2 * rows, HD)

    live = []
    for t in range(half):
        token = spread + lax.rem(x + dists[2 * t >= half], 4) * 256
        live.append(token < jnp.where(lane < rows, valid_ref[2 * t], valid_ref[2 * t + 1]))

    def queries(p):
        pair = slice(2 * p, 2 * p + 2)
        parts = [qkv_ref[pair, :, 2 * HD :]] + [ref[pair] for ref in far]
        return jnp.concatenate([part.reshape(2 * rows, HD) for part in parts], axis=0)

    def score(p, t, q, most):
        part = lax.dot_general(
            q, load(t, slice(0, HD)), (((1,), (1,)), ((), ())), preferred_element_type=jnp.float32
        )
        part = jnp.where(live[t], part, DEAD)
        if t == p:
            part = jnp.where(ahead, DEAD, part)
        scores[p % 2][t] = part
        part = jnp.maximum(part[:, :HD], part[:, HD:])
        return part if most is None else jnp.maximum(most, part)

    most = score(0, 0, queries(0), None)
    for p in range(half):
        pair = slice(2 * p, 2 * p + 2)
        top = jnp.broadcast_to(jnp.max(most, axis=1, keepdims=True), most.shape)
        states = [
            [
                jnp.concatenate(
                    [old[3 * i + k][pair].reshape(2 * rows, HD) for i in range(sets)], axis=0
                )
                for k in range(3)
            ]
            for old in olds
        ]
        for _, old_top, _ in states:
            top = jnp.maximum(top, old_top)
        acc = jnp.zeros((2 * sets * rows, HD), jnp.float32)
        total = jnp.zeros((2 * sets * rows, HD), jnp.float32)
        for old_acc, old_top, old_total in states:
            keep = jnp.exp2((old_top - top) * scale)
            acc = acc + old_acc * keep
            total = total + old_total * keep
        both = jnp.concatenate([top, top], axis=1)
        most = None
        if p + 1 < half:
            q = queries(p + 1)
            most = score(p + 1, 0, q, most)
        for t in range(p + 1):
            if p + 1 < half:
                most = score(p + 1, t + 1, q, most)
            weight = jnp.exp2((scores[p % 2][t] - both) * scale)
            total = total + (weight[:, :HD] + weight[:, HD:])
            acc = acc + jnp.dot(
                weight.astype(jnp.bfloat16),
                load(t, slice(HD, 2 * HD)),
                preferred_element_type=jnp.float32,
            )
        if not last:
            for i in range(sets):
                mine = slice(2 * i * rows, 2 * (i + 1) * rows)
                for k, value in enumerate((acc, top, total)):
                    outs[3 * i + k][pair] = value[mine].reshape(2, rows, HD)
            continue
        attended = acc / jnp.sum(total, axis=1, keepdims=True)
        at = lax.broadcasted_iota(jnp.int32, (rows, 1), 0)
        at = (at // 32) * 64 + at % 32 + x * 256 + core * 32
        for c in (2 * p, 2 * p + 1):
            part = attended[:rows] if c == 2 * p else attended[rows:]
            held[c] = jnp.where(at < valid_ref[c], part, 0.0).astype(held.dtype)
        copies.append(pltpu.make_async_copy(held.at[pair], out_ref.at[pair], sems.at[p]))
        copies[-1].start()
    for copy in copies:
        copy.wait()


def attend(valid, qkv, far=(), keys=(), dists=None, other=False, states=(), last=False):
    groups, rows, _ = qkv.shape
    shape = (groups, rows, HD)
    whole = pl.BlockSpec(memory_space=VMEM)
    far_off = pl.BlockSpec(memory_space=pl.ANY)
    sets = 1 + len(far)
    pairs = groups * (groups + 2) // 2 * rows * rows * sets
    score_tiles = pltpu.VMEM((groups // 2, 2 * sets * rows, 2 * rows), jnp.float32)
    scratch = [score_tiles] * 2
    arrays = [*far, *keys] + [part for state in states for part in state]
    if last:
        out_shape, out_specs = jax.ShapeDtypeStruct(shape, jnp.bfloat16), far_off
        scratch += [
            pltpu.VMEM(shape, jnp.bfloat16),
            pltpu.SemaphoreType.DMA((groups // 2,)),
        ]
    else:
        out_shape = [jax.ShapeDtypeStruct(shape, jnp.float32)] * (3 * sets)
        out_specs = [whole] * (3 * sets)
    return pl.pallas_call(
        functools.partial(attend_kernel, dists, other, len(far), len(states), last),
        out_shape=out_shape,
        in_specs=[pl.BlockSpec(memory_space=pltpu.SMEM)] + [whole] * (1 + len(arrays)),
        out_specs=out_specs,
        scratch_shapes=scratch,
        compiler_params=pltpu.CompilerParams(vmem_limit_bytes=24 * MIB),
        cost_estimate=pl.CostEstimate(
            flops=4 * pairs * HD, bytes_accessed=4 * MIB, transcendentals=pairs
        ),
        name="attend",
    )(valid, qkv, *arrays)


def shift(value, by):
    n = lax.axis_size("x")
    return lax.ppermute(value, "x", [(i, (i + by) % n) for i in range(n)])


def swap(value):
    return lax.ppermute(value, "core", [(0, 1), (1, 0)])


def shards(queries, keys, values, valid, levels, gate_table):
    tokens, width = queries.shape[1:]
    groups = lax.axis_size("group")
    qkv = lax.all_to_all(pack(keys[0], values[0], queries[0]), AX, 0, 0, tiled=True)
    qkv = qkv.reshape(groups, -1, 3 * HD)
    half = groups // 2
    low, high = qkv[:half, :, : 2 * HD], qkv[half:, :, : 2 * HD]
    far = [swap(qkv[:, :, 2 * HD :])]
    low_l, high_r = shift(low, 1), shift(high, -1)
    high_l, low_r = shift(high, 1), shift(low, -1)
    part = functools.partial(attend, valid, qkv)
    state = part(far)
    state, low_l, high_r = lax.optimization_barrier((state, low_l, high_r))
    low_o, high_o = shift(low_l, 1), shift(high_r, -1)
    state = part(far, [low_l, high_r], (3, 1), states=[state])
    state, low_r, high_l = lax.optimization_barrier((state, low_r, high_l))
    state = part(far, [low_r, high_l], (1, 3), states=[state])
    mine, sent = state[:3], [swap(value) for value in state[3:]]
    mine = part(keys=[low_o, high_o], dists=(2, 2), states=[mine])
    attended = part(
        keys=[swap(low_o), swap(high_o)],
        dists=(2, 2),
        other=True,
        states=[mine, sent],
        last=True,
    )
    returned = lax.all_to_all(attended.reshape(-1, tokens, HD), AX, 0, 0, tiled=True)
    own = lax.axis_index("group")
    level = lax.dynamic_index_in_dim(levels, own, 0, keepdims=False)
    gate = lax.dynamic_index_in_dim(gate_table, level, 0, keepdims=True)
    mixed = returned.transpose(1, 0, 2).reshape(tokens, width).astype(jnp.float32) * gate
    return mixed.astype(jnp.bfloat16)[None]


def solution(mesh):
    fine = Mesh(mesh.devices.reshape(8, 4, 4, 2), ("group", "x", "y", "core"))
    rows = P("group", ("x", "y", "core"), None)
    return jax.shard_map(
        shards,
        mesh=fine,
        in_specs=(rows, rows, rows, P(), P(), P()),
        out_specs=rows,
        check_vma=False,
    )
```

time: 84.5 us -> 83.2 us (0.985)
  waiting for transfers between devices: 16.6 us -> 14.6 us
    ppermute x6, waiting for transfers between devices: 2.47 us -> 0.65 us  [swap(): return lax.ppermute(value, 'core', [(0, 1), (1, 0)])]
    pallas_call x4 -> x5, Pallas kernels: 13 us -> 13.7 us  [attend(): pl.pallas_call(functools.partial(attend_kernel, dists, other, len(far), l...]
  transfers between devices with their start and end apart: 13 -> 13, of which waited for: 7 -> 7; matrix products, arithmetic and copies ran while one was open for 1% -> 1% of each run, Pallas kernels for 11% -> 13%
where the time goes in v4:
time: 83.2 us; the launch traced here: 82.9 us
  blocking collectives  34.4 us (41%)
  Pallas kernels  15.7 us (19%)
  waiting for transfers between devices  14.6 us (18%)
  starting transfers between devices  13.6 us (16%)
  between operations  2.03 us (2%)
  local copies, waits for them, and re-layouts  1.77 us (2%)
    all_to_all x1, blocking collectives, shards(): lax.all_to_all(pack(keys[0], values[0], queries[0]), AX, 0, 0, tiled=True)  34.4 us
    pallas_call x5, Pallas kernels, attend(): pl.pallas_call(functools.partial(attend_kernel, dists, other, len(far), l...  13.7 us
    all_to_all x1, waiting for transfers between devices, shards(): lax.all_to_all(attended.reshape(-1, tokens, HD), AX, 0, 0, tiled=True)  10.1 us
    ppermute x6, starting transfers between devices, shift(): return lax.ppermute(value, 'x', [(i, (i + by) % n) for i in range(n)])  7.37 us
    all_to_all x1, starting transfers between devices, shards(): lax.all_to_all(attended.reshape(-1, tokens, HD), AX, 0, 0, tiled=True)  5.08 us
    ppermute x6, waiting for transfers between devices, shift(): return lax.ppermute(value, 'x', [(i, (i + by) % n) for i in range(n)])  3.86 us
    pallas_call x1, Pallas kernels, pack(): pl.pallas_call(functools.partial(pack_kernel, n), out_shape=jax.ShapeDtyp...  2.02 us
  transfers between devices with their start and end apart: 13, of which 7 were waited for; matrix products, arithmetic and copies ran while one was open for 1% of the time, Pallas kernels for 13%

profile of v4, /device:TPU:6, one launch (start us, length us, event | category | flops | bytes accessed | tf_op | source)
XLA Modules:
  0.0 82.9 jit_solution(64650482416532414)
XLA Ops:
  0.0 0.0 copy-start
  0.0 2.0 %pack.1 = bf16[32,32,384]{2,1,0:T(8,128)(2,1)} custom-call(bf16[32,4096]{1,0:T(8,128)(2,1)} %bitcast.16, bf16[32,4096]{1,0:T(8,128)(2,1)} %bitcast.17, bf16[32,4096]{1,0:T(8,128)(2,1)} %bitcast.18), custom_call_target="tpu_custom_call" | custom-call | tf_op jit(solution)/shard_map/pack/pallas_call | solution.py:40
  2.0 34.4 %all_to_all.10 = bf16[32,32,384]{2,1,0:T(8,128)(2,1)S(1)} all-to-all(bf16[32,32,384]{2,1,0:T(8,128)(2,1)} %pack.1), channel_id=1, replica_groups=mesh['group'=8,'x'=4,'y'=4,'core'=2] {'group','y'}, dimensions={0} | all-to-all | bytes 1572864 | tf_op jit(solution)/shard_map/all_to_all | solution.py:218
  36.5 0.1 collective-permute-start
  36.7 0.0 copy-start.1
  36.7 0.6 collective-permute-start.1
  37.2 1.5 %collective-permute-start.2 = (bf16[4,128,256]{2,1,0:T(8,128)(2,1)S(1)}, bf16[4,128,256]{2,1,0:T(8,128)(2,1)S(1)}, u32[]{:S(2)}, u32[]{:S(2)}) collective-permute-start(bf16[4,128,256]{2,1,0:T(8,128)(2,1)S(1)} %get-tuple-element.79), channel_id=1, source_target_pairs={{0,24},{8,0},{16,8},{24,16},{1,25},{9,1},{17,9},{25,17},{2,26},{10... | collective-permute-start | bytes 786440 | tf_op jit(solution)/shard_map/ppermute | solution.py:208
  38.8 0.8 collective-permute-start.7
  39.6 2.4 %collective-permute-start.8 = (bf16[4,128,256]{2,1,0:T(8,128)(2,1)S(1)}, bf16[4,128,256]{2,1,0:T(8,128)(2,1)S(1)}, u32[]{:S(2)}, u32[]{:S(2)}) collective-permute-start(bf16[4,128,256]{2,1,0:T(8,128)(2,1)S(1)} %get-tuple-element.79), channel_id=1, source_target_pairs={{0,8},{8,16},{16,24},{24,0},{1,9},{9,17},{17,25},{25,1},{2,10},{10... | collective-permute-start | bytes 786440 | tf_op jit(solution)/shard_map/ppermute | solution.py:208
  42.0 0.0 collective-permute-done.refs_0_
  42.0 0.0 copy-done.1
  42.0 2.8 %attend.5 = (f32[8,128,128]{2,1,0:T(8,128)S(1)}, f32[8,128,128]{2,1,0:T(8,128)S(1)}, f32[8,128,128]{2,1,0:T(8,128)S(1)}, f32[8,128,128]{2,1,0:T(8,128)S(1)}, f32...) custom-call(s32[8]{0:T(128)S(1)} %copy-done.1, bf16[8,128,384]{2,1,0:T(8,128)(2,1)S(1)} %bitcast.11, ...), custom_call_target="tpu_custom_call" | custom-call | flops 671088640 | bytes 4194304 | tf_op jit(solution)/shard_map/attend/pallas_call | solution.py:192
  44.9 1.0 %collective-permute-done.1.refs_1_ = bf16[4,128,256]{2,1,0:T(8,128)(2,1)S(1)} collective-permute-done((bf16[4,128,256]{2,1,0:T(8,128)(2,1)S(1)}, bf16[4,128,256]{2,1,0:T(8,128)(2,1)S(1)}, u32[]{:S(2)}, u32[]{:S(2)}) %collective-permute-start.1) | collective-permute-done | bytes 262176 | tf_op jit(solution)/shard_map/ppermute | solution.py:208
  45.8 1.7 %collective-permute-done.2.refs_2_ = bf16[4,128,256]{2,1,0:T(8,128)(2,1)S(1)} collective-permute-done((bf16[4,128,256]{2,1,0:T(8,128)(2,1)S(1)}, bf16[4,128,256]{2,1,0:T(8,128)(2,1)S(1)}, u32[]{:S(2)}, u32[]{:S(2)}) %collective-permute-start.2) | collective-permute-done | bytes 262176 | tf_op jit(solution)/shard_map/ppermute | solution.py:208
  47.6 0.3 collective-permute-start.3
  47.9 1.7 %collective-permute-start.5 = (bf16[4,128,256]{2,1,0:T(8,128)(2,1)S(1)}, bf16[4,128,256]{2,1,0:T(8,128)(2,1)S(1)}, u32[]{:S(2)}, u32[]{:S(2)}) collective-permute-start(bf16[4,128,256]{2,1,0:T(8,128)(2,1)S(1)} %collective-permute-done.2.refs_2_), channel_id=1, source_target_pairs={{0,24},{8,0},{16,8},{24,16},{1,25},{9,1},{17,9},{25,17},{2,26},{10... | collective-permute-start | bytes 786440 | tf_op jit(solution)/shard_map/ppermute | solution.py:208
  49.6 3.1 %attend.6 = (f32[8,128,128]{2,1,0:T(8,128)S(1)}, f32[8,128,128]{2,1,0:T(8,128)S(1)}, f32[8,128,128]{2,1,0:T(8,128)S(1)}, f32[8,128,128]{2,1,0:T(8,128)S(1)}, f32...) custom-call(s32[8]{0:T(128)S(1)} %copy-done.1, bf16[8,128,384]{2,1,0:T(8,128)(2,1)S(1)} %bitcast.12, ...), custom_call_target="tpu_custom_call" | custom-call | flops 671088640 | bytes 4194304 | tf_op jit(solution)/shard_map/attend/pallas_call | solution.py:192
  52.7 0.5 collective-permute-done.7.refs_1_
  53.2 0.0 collective-permute-done.8.refs_2_
  53.2 3.1 %attend.7 = (f32[8,128,128]{2,1,0:T(8,128)S(1)}, f32[8,128,128]{2,1,0:T(8,128)S(1)}, f32[8,128,128]{2,1,0:T(8,128)S(1)}, f32[8,128,128]{2,1,0:T(8,128)S(1)}, f32...) custom-call(s32[8]{0:T(128)S(1)} %copy-done.1, bf16[8,128,384]{2,1,0:T(8,128)(2,1)S(1)} %bitcast.13, ...), custom_call_target="tpu_custom_call" | custom-call | flops 671088640 | bytes 4194304 | tf_op jit(solution)/shard_map/attend/pallas_call | solution.py:192
  56.3 0.1 collective-permute-start.10
  56.4 0.5 collective-permute-start.11
  56.9 0.1 collective-permute-start.9
  57.0 0.0 collective-permute-done.3.refs_0_
  57.0 0.4 collective-permute-start.4
  57.4 0.7 collective-permute-done.5.refs_1_
  58.1 0.0 collective-permute-start.6
  58.1 1.8 %attend.8 = (f32[8,128,128]{2,1,0:T(8,128)S(1)}, f32[8,128,128]{2,1,0:T(8,128)S(1)}, f32[8,128,128]{2,1,0:T(8,128)S(1)}) custom-call(s32[8]{0:T(128)S(1)} %copy-done.1, bf16[8,128,384]{2,1,0:T(8,128)(2,1)S(1)} %bitcast.14, bf16[4,128,256]{2,1,0:T(8,128)(2,1)S(1)} %collective-permute-done.3.refs_0_, bf16[4,128,256]{2,1,0:T(8,128)(2,1)S(1)} %collective-permute-done.5.refs_1_, ...), custom_call_target="tpu_custom_call" | custom-call | flops 335544320 | bytes 4194304 | tf_op jit(solution)/shard_map/attend/pallas_call | solution.py:192
  59.9 0.3 collective-permute-done.4.refs_0_
  60.2 0.4 collective-permute-done.6.refs_1_
  60.6 0.0 collective-permute-done.10.refs_6_
  60.6 0.0 collective-permute-done.11.refs_7_
  60.6 0.0 collective-permute-done.9.refs_5_
  60.6 2.8 %attend.9 = bf16[8,128,128]{2,1,0:T(8,128)(2,1)} custom-call(s32[8]{0:T(128)S(1)} %copy-done.1, bf16[8,128,384]{2,1,0:T(8,128)(2,1)S(1)} %bitcast.15, bf16[4,128,256]{2,1,0:T(8,128)(2,1)S(1)} %collective-permute-done.4.refs_0_, bf16[4,128,256]{2,1,0:T(8,128)(2,1)S(1)} %collective-permute-done.6.refs_1_, f32[8,128,128]{2,1,0:T(8,128)S(1)} %get-tuple-element.73.refs_2_, ...), custom_call_target="tpu_custom_call" | custom-call | flops 335544320 | bytes 4194304 | tf_op jit(solution)/shard_map/attend/pallas_call | solution.py:192
  63.4 5.1 %all-to-all-start.1 = ((bf16[32,32,128]{2,1,0:T(8,128)(2,1)}), bf16[32,32,128]{2,1,0:T(8,128)(2,1)S(1)}, u32[]{:S(2)}, u32[]{:S(2)}) async-start(bf16[32,32,128]{2,1,0:T(8,128)(2,1)} %bitcast.4), calls=%async_computation.1 | async-start | bytes 524288 | tf_op jit(solution)/shard_map/all_to_all | solution.py:241
  68.5 0.0 copy-start.2
  68.5 0.6 copy-done.2
  69.1 0.6 dynamic_slice.8
  71.6 0.0 copy-done
  71.6 10.1 %all-to-all-done.1 = bf16[32,32,128]{2,1,0:T(8,128)(2,1)S(1)} async-done(((bf16[32,32,128]{2,1,0:T(8,128)(2,1)}), bf16[32,32,128]{2,1,0:T(8,128)(2,1)S(1)}, u32[]{:S(2)}, u32[]{:S(2)}) %all-to-all-start.1) | async-done | bytes 262176 | tf_op jit(solution)/shard_map/all_to_all | solution.py:241
  81.7 0.1 convert_bitcast_fusion
  81.8 0.3 copy.7
  82.1 0.1 reshape.51
  82.2 0.7 multiply_convert_fusion
  (3 shorter events, 0.1 us)
Async XLA Ops:
  0.0 71.6 %copy-start = (f32[64,4096]{1,0:T(8,128)S(1)}, f32[64,4096]{1,0:T(8,128)}, u32[]{:S(2)}) copy-start(f32[64,4096]{1,0:T(8,128)} %param.11) | copy-start | bytes 3145732
  36.5 5.5 %collective-permute-start = (bf16[8,128,128]{2,1,0:T(8,128)(2,1)S(1)}, bf16[8,128,128]{2,1,0:T(8,128)(2,1)S(1)}, u32[]{:S(2)}, u32[]{:S(2)}) collective-permute-start(bf16[8,128,128]{2,1,0:T(8,128)(2,1)S(1)} %slice.12), channel_id=1, source_target_pairs={{0,1},{1,0},{2,3},{3,2},{4,5},{5,4},{6,7},{7,6},{8,9},{9,8},{10,11... | collective-permute-start | bytes 786440 | tf_op jit(solution)/shard_map/ppermute | solution.py:212
  36.7 5.4 %copy-start.1 = (s32[8]{0:T(128)S(1)}, s32[8]{0:T(128)}, u32[]{:S(2)}) copy-start(s32[8]{0:T(128)} %valid_ref.9) | copy-start | bytes 100
  36.7 9.2 %collective-permute-start.1 = (bf16[4,128,256]{2,1,0:T(8,128)(2,1)S(1)}, bf16[4,128,256]{2,1,0:T(8,128)(2,1)S(1)}, u32[]{:S(2)}, u32[]{:S(2)}) collective-permute-start(bf16[4,128,256]{2,1,0:T(8,128)(2,1)S(1)} %get-tuple-element.80), channel_id=1, source_target_pairs={{0,8},{8,16},{16,24},{24,0},{1,9},{9,17},{17,25},{25,1},{2,10},{10... | collective-permute-start | bytes 786440 | tf_op jit(solution)/shard_map/ppermute | solution.py:208
  37.2 10.4 %collective-permute-start.2 = (bf16[4,128,256]{2,1,0:T(8,128)(2,1)S(1)}, bf16[4,128,256]{2,1,0:T(8,128)(2,1)S(1)}, u32[]{:S(2)}, u32[]{:S(2)}) collective-permute-start(bf16[4,128,256]{2,1,0:T(8,128)(2,1)S(1)} %get-tuple-element.79), channel_id=1, source_target_pairs={{0,24},{8,0},{16,8},{24,16},{1,25},{9,1},{17,9},{25,17},{2,26},{10... | collective-permute-start | bytes 786440 | tf_op jit(solution)/shard_map/ppermute | solution.py:208
  38.8 14.4 %collective-permute-start.7 = (bf16[4,128,256]{2,1,0:T(8,128)(2,1)S(1)}, bf16[4,128,256]{2,1,0:T(8,128)(2,1)S(1)}, u32[]{:S(2)}, u32[]{:S(2)}) collective-permute-start(bf16[4,128,256]{2,1,0:T(8,128)(2,1)S(1)} %get-tuple-element.80), channel_id=1, source_target_pairs={{0,24},{8,0},{16,8},{24,16},{1,25},{9,1},{17,9},{25,17},{2,26},{10... | collective-permute-start | bytes 786440 | tf_op jit(solution)/shard_map/ppermute | solution.py:208
  39.6 13.6 %collective-permute-start.8 = (bf16[4,128,256]{2,1,0:T(8,128)(2,1)S(1)}, bf16[4,128,256]{2,1,0:T(8,128)(2,1)S(1)}, u32[]{:S(2)}, u32[]{:S(2)}) collective-permute-start(bf16[4,128,256]{2,1,0:T(8,128)(2,1)S(1)} %get-tuple-element.79), channel_id=1, source_target_pairs={{0,8},{8,16},{16,24},{24,0},{1,9},{9,17},{17,25},{25,1},{2,10},{10... | collective-permute-start | bytes 786440 | tf_op jit(solution)/shard_map/ppermute | solution.py:208
  47.6 9.4 %collective-permute-start.3 = (bf16[4,128,256]{2,1,0:T(8,128)(2,1)S(1)}, bf16[4,128,256]{2,1,0:T(8,128)(2,1)S(1)}, u32[]{:S(2)}, u32[]{:S(2)}) collective-permute-start(bf16[4,128,256]{2,1,0:T(8,128)(2,1)S(1)} %collective-permute-done.1.refs_1_), channel_id=1, source_target_pairs={{0,8},{8,16},{16,24},{24,0},{1,9},{9,17},{17,25},{25,1},{2,10},{10... | collective-permute-start | bytes 786440 | tf_op jit(solution)/shard_map/ppermute | solution.py:208
  47.9 10.2 %collective-permute-start.5 = (bf16[4,128,256]{2,1,0:T(8,128)(2,1)S(1)}, bf16[4,128,256]{2,1,0:T(8,128)(2,1)S(1)}, u32[]{:S(2)}, u32[]{:S(2)}) collective-permute-start(bf16[4,128,256]{2,1,0:T(8,128)(2,1)S(1)} %collective-permute-done.2.refs_2_), channel_id=1, source_target_pairs={{0,24},{8,0},{16,8},{24,16},{1,25},{9,1},{17,9},{25,17},{2,26},{10... | collective-permute-start | bytes 786440 | tf_op jit(solution)/shard_map/ppermute | solution.py:208
  56.3 4.2 %collective-permute-start.10 = (f32[8,128,128]{2,1,0:T(8,128)S(1)}, f32[8,128,128]{2,1,0:T(8,128)S(1)}, u32[]{:S(2)}, u32[]{:S(2)}) collective-permute-start(f32[8,128,128]{2,1,0:T(8,128)S(1)} %get-tuple-element.77), channel_id=1, source_target_pairs={{0,1},{1,0},{2,3},{3,2},{4,5},{5,4},{6,7},{7,6},{8,9},{9,8},{10,11... | collective-permute-start | bytes 1572872 | tf_op jit(solution)/shard_map/ppermute | solution.py:212
  56.4 4.2 %collective-permute-start.11 = (f32[8,128,128]{2,1,0:T(8,128)S(1)}, f32[8,128,128]{2,1,0:T(8,128)S(1)}, u32[]{:S(2)}, u32[]{:S(2)}) collective-permute-start(f32[8,128,128]{2,1,0:T(8,128)S(1)} %get-tuple-element.78), channel_id=1, source_target_pairs={{0,1},{1,0},{2,3},{3,2},{4,5},{5,4},{6,7},{7,6},{8,9},{9,8},{10,11... | collective-permute-start | bytes 1572872 | tf_op jit(solution)/shard_map/ppermute | solution.py:212
  56.9 3.7 %collective-permute-start.9 = (f32[8,128,128]{2,1,0:T(8,128)S(1)}, f32[8,128,128]{2,1,0:T(8,128)S(1)}, u32[]{:S(2)}, u32[]{:S(2)}) collective-permute-start(f32[8,128,128]{2,1,0:T(8,128)S(1)} %get-tuple-element.76), channel_id=1, source_target_pairs={{0,1},{1,0},{2,3},{3,2},{4,5},{5,4},{6,7},{7,6},{8,9},{9,8},{10,11... | collective-permute-start | bytes 1572872 | tf_op jit(solution)/shard_map/ppermute | solution.py:212
  57.0 3.2 %collective-permute-start.4 = (bf16[4,128,256]{2,1,0:T(8,128)(2,1)S(1)}, bf16[4,128,256]{2,1,0:T(8,128)(2,1)S(1)}, u32[]{:S(2)}, u32[]{:S(2)}) collective-permute-start(bf16[4,128,256]{2,1,0:T(8,128)(2,1)S(1)} %collective-permute-done.3.refs_0_), channel_id=1, source_target_pairs={{0,1},{1,0},{2,3},{3,2},{4,5},{5,4},{6,7},{7,6},{8,9},{9,8},{10,11... | collective-permute-start | bytes 786440 | tf_op jit(solution)/shard_map/ppermute | solution.py:212
  58.1 2.5 %collective-permute-start.6 = (bf16[4,128,256]{2,1,0:T(8,128)(2,1)S(1)}, bf16[4,128,256]{2,1,0:T(8,128)(2,1)S(1)}, u32[]{:S(2)}, u32[]{:S(2)}) collective-permute-start(bf16[4,128,256]{2,1,0:T(8,128)(2,1)S(1)} %collective-permute-done.5.refs_1_), channel_id=1, source_target_pairs={{0,1},{1,0},{2,3},{3,2},{4,5},{5,4},{6,7},{7,6},{8,9},{9,8},{10,11... | collective-permute-start | bytes 786440 | tf_op jit(solution)/shard_map/ppermute | solution.py:212
  63.4 18.3 %all-to-all-start.1 = ((bf16[32,32,128]{2,1,0:T(8,128)(2,1)}), bf16[32,32,128]{2,1,0:T(8,128)(2,1)S(1)}, u32[]{:S(2)}, u32[]{:S(2)}) async-start(bf16[32,32,128]{2,1,0:T(8,128)(2,1)} %bitcast.4), calls=%async_computation.1 | async-start | bytes 524288 | tf_op jit(solution)/shard_map/all_to_all | solution.py:241
  68.5 0.7 copy-start.2

commit v5 on v4

--- a/solution.py
+++ b/solution.py
@@ -59,8 +59,8 @@
         part, refs[:] = refs[:n], refs[n:]
         return part
 
-    sets = 2 if wide else 1
-    far = take(wide)
+    sets = max(1, wide)
+    far = take(wide > 0)
     own = dists is None
     if own:
         dists = (0, 0)
@@ -102,7 +102,9 @@
 
     def queries(p):
         pair = slice(2 * p, 2 * p + 2)
-        parts = [qkv_ref[pair, :, 2 * HD :]] + [ref[pair] for ref in far]
+        parts = [ref[pair] for ref in far]
+        if wide != 1:
+            parts.insert(0, qkv_ref[pair, :, 2 * HD :])
         return jnp.concatenate([part.reshape(2 * rows, HD) for part in parts], axis=0)
 
     def score(p, t, q, most):
@@ -170,12 +172,12 @@
         copy.wait()
 
 
-def attend(valid, qkv, far=(), keys=(), dists=None, other=False, states=(), last=False):
+def attend(valid, qkv, far=(), wide=0, keys=(), dists=None, other=False, states=(), last=False):
     groups, rows, _ = qkv.shape
     shape = (groups, rows, HD)
     whole = pl.BlockSpec(memory_space=VMEM)
     far_off = pl.BlockSpec(memory_space=pl.ANY)
-    sets = 1 + len(far)
+    sets = max(1, wide)
     pairs = groups * (groups + 2) // 2 * rows * rows * sets
     score_tiles = pltpu.VMEM((groups // 2, 2 * sets * rows, 2 * rows), jnp.float32)
     scratch = [score_tiles] * 2
@@ -190,7 +192,7 @@
         out_shape = [jax.ShapeDtypeStruct(shape, jnp.float32)] * (3 * sets)
         out_specs = [whole] * (3 * sets)
     return pl.pallas_call(
-        functools.partial(attend_kernel, dists, other, len(far), len(states), last),
+        functools.partial(attend_kernel, dists, other, wide, len(states), last),
         out_shape=out_shape,
         in_specs=[pl.BlockSpec(memory_space=pltpu.SMEM)] + [whole] * (1 + len(arrays)),
         out_specs=out_specs,
@@ -221,14 +223,15 @@
     low, high = qkv[:half, :, : 2 * HD], qkv[half:, :, : 2 * HD]
     far = [swap(qkv[:, :, 2 * HD :])]
     low_l, high_r = shift(low, 1), shift(high, -1)
+    part = functools.partial(attend, valid, qkv)
+    mine, low, high = lax.optimization_barrier((part(), low, high))
     high_l, low_r = shift(high, 1), shift(low, -1)
-    part = functools.partial(attend, valid, qkv)
-    state = part(far)
+    state = [*mine, *part(far, 1)]
     state, low_l, high_r = lax.optimization_barrier((state, low_l, high_r))
     low_o, high_o = shift(low_l, 1), shift(high_r, -1)
-    state = part(far, [low_l, high_r], (3, 1), states=[state])
+    state = part(far, 2, [low_l, high_r], (3, 1), states=[state])
     state, low_r, high_l = lax.optimization_barrier((state, low_r, high_l))
-    state = part(far, [low_r, high_l], (1, 3), states=[state])
+    state = part(far, 2, [low_r, high_l], (1, 3), states=[state])
     mine, sent = state[:3], [swap(value) for value in state[3:]]
     mine = part(keys=[low_o, high_o], dists=(2, 2), states=[mine])
     attended = part(

time: 83.2 us -> 83.3 us (level)
    pallas_call x5 -> x6, Pallas kernels: 13.7 us -> 14.2 us  [attend(): pl.pallas_call(functools.partial(attend_kernel, dists, other, wide, len(s...]
  transfers between devices with their start and end apart: 13 -> 13, of which waited for: 7 -> 7; matrix products, arithmetic and copies ran while one was open for 1% -> 1% of each run, Pallas kernels for 13% -> 14%
where the time goes in v5:
time: 83.3 us; the launch traced here: 82.9 us
  blocking collectives  34.4 us (41%)
  Pallas kernels  16.3 us (20%)
  waiting for transfers between devices  13.9 us (17%)
  starting transfers between devices  13.7 us (16%)
  between operations  2.05 us (2%)
  local copies, waits for them, and re-layouts  1.79 us (2%)
    all_to_all x1, blocking collectives, shards(): lax.all_to_all(pack(keys[0], values[0], queries[0]), AX, 0, 0, tiled=True)  34.4 us
    pallas_call x6, Pallas kernels, attend(): pl.pallas_call(functools.partial(attend_kernel, dists, other, wide, len(s...  14.2 us
    all_to_all x1, waiting for transfers between devices, shards(): lax.all_to_all(attended.reshape(-1, tokens, HD), AX, 0, 0, tiled=True)  10 us
    ppermute x6, starting transfers between devices, shift(): return lax.ppermute(value, 'x', [(i, (i + by) % n) for i in range(n)])  7.44 us
    all_to_all x1, starting transfers between devices, shards(): lax.all_to_all(attended.reshape(-1, tokens, HD), AX, 0, 0, tiled=True)  5.09 us
    ppermute x6, waiting for transfers between devices, shift(): return lax.ppermute(value, 'x', [(i, (i + by) % n) for i in range(n)])  3.21 us
    pallas_call x1, Pallas kernels, pack(): pl.pallas_call(functools.partial(pack_kernel, n), out_shape=jax.ShapeDtyp...  2.06 us
  transfers between devices with their start and end apart: 13, of which 7 were waited for; matrix products, arithmetic and copies ran while one was open for 1% of the time, Pallas kernels for 14%

profile of v5, /device:TPU:6, one launch (start us, length us, event | category | flops | bytes accessed | tf_op | source)
XLA Modules:
  0.0 82.9 jit_solution(16102698591387658736)
XLA Ops:
  0.0 0.0 copy-start
  0.0 2.1 %pack.1 = bf16[32,32,384]{2,1,0:T(8,128)(2,1)} custom-call(bf16[32,4096]{1,0:T(8,128)(2,1)} %bitcast.17, bf16[32,4096]{1,0:T(8,128)(2,1)} %bitcast.18, bf16[32,4096]{1,0:T(8,128)(2,1)} %bitcast.19), custom_call_target="tpu_custom_call" | custom-call | tf_op jit(solution)/shard_map/pack/pallas_call | solution.py:40
  2.1 34.4 %all_to_all.10 = bf16[32,32,384]{2,1,0:T(8,128)(2,1)S(1)} all-to-all(bf16[32,32,384]{2,1,0:T(8,128)(2,1)} %pack.1), channel_id=1, replica_groups=mesh['group'=8,'x'=4,'y'=4,'core'=2] {'group','y'}, dimensions={0} | all-to-all | bytes 1572864 | tf_op jit(solution)/shard_map/all_to_all | solution.py:220
  36.6 0.1 collective-permute-start
  36.7 0.0 copy-start.1
  36.7 0.6 collective-permute-start.1
  37.3 1.5 %collective-permute-start.2 = (bf16[4,128,256]{2,1,0:T(8,128)(2,1)S(1)}, bf16[4,128,256]{2,1,0:T(8,128)(2,1)S(1)}, u32[]{:S(2)}, u32[]{:S(2)}) collective-permute-start(bf16[4,128,256]{2,1,0:T(8,128)(2,1)S(1)} %get-tuple-element.71), channel_id=1, source_target_pairs={{0,24},{8,0},{16,8},{24,16},{1,25},{9,1},{17,9},{25,17},{2,26},{10... | collective-permute-start | bytes 786440 | tf_op jit(solution)/shard_map/ppermute | solution.py:210
  38.8 0.0 copy-done.1
  38.8 1.7 %attend.6 = (f32[8,128,128]{2,1,0:T(8,128)S(1)}, f32[8,128,128]{2,1,0:T(8,128)S(1)}, f32[8,128,128]{2,1,0:T(8,128)S(1)}) custom-call(s32[8]{0:T(128)S(1)} %copy-done.1, bf16[8,128,384]{2,1,0:T(8,128)(2,1)S(1)} %bitcast.11), custom_call_target="tpu_custom_call" | custom-call | flops 335544320 | bytes 4194304 | tf_op jit(solution)/shard_map/attend/pallas_call | solution.py:194
  40.5 0.9 %collective-permute-start.7 = (bf16[4,128,256]{2,1,0:T(8,128)(2,1)S(1)}, bf16[4,128,256]{2,1,0:T(8,128)(2,1)S(1)}, u32[]{:S(2)}, u32[]{:S(2)}) collective-permute-start(bf16[4,128,256]{2,1,0:T(8,128)(2,1)S(1)} %get-tuple-element.70), channel_id=1, source_target_pairs={{0,24},{8,0},{16,8},{24,16},{1,25},{9,1},{17,9},{25,17},{2,26},{10... | collective-permute-start | bytes 786440 | tf_op jit(solution)/shard_map/ppermute | solution.py:210
  41.4 2.4 %collective-permute-start.8 = (bf16[4,128,256]{2,1,0:T(8,128)(2,1)S(1)}, bf16[4,128,256]{2,1,0:T(8,128)(2,1)S(1)}, u32[]{:S(2)}, u32[]{:S(2)}) collective-permute-start(bf16[4,128,256]{2,1,0:T(8,128)(2,1)S(1)} %get-tuple-element.71), channel_id=1, source_target_pairs={{0,8},{8,16},{16,24},{24,0},{1,9},{9,17},{17,25},{25,1},{2,10},{10... | collective-permute-start | bytes 786440 | tf_op jit(solution)/shard_map/ppermute | solution.py:210
  43.8 0.0 collective-permute-done.refs_0_
  43.8 1.7 %attend.7 = (f32[8,128,128]{2,1,0:T(8,128)S(1)}, f32[8,128,128]{2,1,0:T(8,128)S(1)}, f32[8,128,128]{2,1,0:T(8,128)S(1)}) custom-call(s32[8]{0:T(128)S(1)} %copy-done.1, bf16[8,128,384]{2,1,0:T(8,128)(2,1)S(1)} %bitcast.12, bf16[8,128,128]{2,1,0:T(8,128)(2,1)S(1)} %collective-permute-done.refs_0_), custom_call_target="tpu_custom_call" | custom-call | flops 335544320 | bytes 4194304 | tf_op jit(solution)/shard_map/attend/pallas_call | solution.py:194
  45.6 0.3 collective-permute-done.1.refs_1_
  45.9 1.7 %collective-permute-done.2.refs_2_ = bf16[4,128,256]{2,1,0:T(8,128)(2,1)S(1)} collective-permute-done((bf16[4,128,256]{2,1,0:T(8,128)(2,1)S(1)}, bf16[4,128,256]{2,1,0:T(8,128)(2,1)S(1)}, u32[]{:S(2)}, u32[]{:S(2)}) %collective-permute-start.2) | collective-permute-done | bytes 262176 | tf_op jit(solution)/shard_map/ppermute | solution.py:210
  47.6 0.3 collective-permute-start.3
  47.9 1.7 %collective-permute-start.5 = (bf16[4,128,256]{2,1,0:T(8,128)(2,1)S(1)}, bf16[4,128,256]{2,1,0:T(8,128)(2,1)S(1)}, u32[]{:S(2)}, u32[]{:S(2)}) collective-permute-start(bf16[4,128,256]{2,1,0:T(8,128)(2,1)S(1)} %collective-permute-done.2.refs_2_), channel_id=1, source_target_pairs={{0,24},{8,0},{16,8},{24,16},{1,25},{9,1},{17,9},{25,17},{2,26},{10... | collective-permute-start | bytes 786440 | tf_op jit(solution)/shard_map/ppermute | solution.py:210
  49.6 3.1 %attend.8 = (f32[8,128,128]{2,1,0:T(8,128)S(1)}, f32[8,128,128]{2,1,0:T(8,128)S(1)}, f32[8,128,128]{2,1,0:T(8,128)S(1)}, f32[8,128,128]{2,1,0:T(8,128)S(1)}, f32...) custom-call(s32[8]{0:T(128)S(1)} %copy-done.1, bf16[8,128,384]{2,1,0:T(8,128)(2,1)S(1)} %bitcast.13, ...), custom_call_target="tpu_custom_call" | custom-call | flops 671088640 | bytes 4194304 | tf_op jit(solution)/shard_map/attend/pallas_call | solution.py:194
  52.8 0.5 collective-permute-done.7.refs_1_
  53.2 0.0 collective-permute-done.8.refs_2_
  53.2 3.1 %attend.9 = (f32[8,128,128]{2,1,0:T(8,128)S(1)}, f32[8,128,128]{2,1,0:T(8,128)S(1)}, f32[8,128,128]{2,1,0:T(8,128)S(1)}, f32[8,128,128]{2,1,0:T(8,128)S(1)}, f32...) custom-call(s32[8]{0:T(128)S(1)} %copy-done.1, bf16[8,128,384]{2,1,0:T(8,128)(2,1)S(1)} %bitcast.14, ...), custom_call_target="tpu_custom_call" | custom-call | flops 671088640 | bytes 4194304 | tf_op jit(solution)/shard_map/attend/pallas_call | solution.py:194
  56.4 0.1 collective-permute-start.10
  56.5 0.5 collective-permute-start.11
  56.9 0.1 collective-permute-start.9
  57.0 0.0 collective-permute-done.3.refs_0_
  57.1 0.4 collective-permute-start.4
  57.5 0.7 collective-permute-done.5.refs_1_
  58.1 0.0 collective-permute-start.6
  58.1 1.8 %attend.10 = (f32[8,128,128]{2,1,0:T(8,128)S(1)}, f32[8,128,128]{2,1,0:T(8,128)S(1)}, f32[8,128,128]{2,1,0:T(8,128)S(1)}) custom-call(s32[8]{0:T(128)S(1)} %copy-done.1, bf16[8,128,384]{2,1,0:T(8,128)(2,1)S(1)} %bitcast.15, bf16[4,128,256]{2,1,0:T(8,128)(2,1)S(1)} %collective-permute-done.3.refs_0_, bf16[4,128,256]{2,1,0:T(8,128)(2,1)S(1)} %collective-permute-done.5.refs_1_, ...), custom_call_target="tpu_custom_call" | custom-call | flops 335544320 | bytes 4194304 | tf_op jit(solution)/shard_map/attend/pallas_call | solution.py:194
  60.0 0.3 collective-permute-done.4.refs_0_
  60.2 0.4 collective-permute-done.6.refs_1_
  60.6 0.0 collective-permute-done.10.refs_6_
  60.6 0.0 collective-permute-done.11.refs_7_
  60.6 0.0 collective-permute-done.9.refs_5_
  60.6 2.8 %attend.11 = bf16[8,128,128]{2,1,0:T(8,128)(2,1)} custom-call(s32[8]{0:T(128)S(1)} %copy-done.1, bf16[8,128,384]{2,1,0:T(8,128)(2,1)S(1)} %bitcast.16, bf16[4,128,256]{2,1,0:T(8,128)(2,1)S(1)} %collective-permute-done.4.refs_0_, bf16[4,128,256]{2,1,0:T(8,128)(2,1)S(1)} %collective-permute-done.6.refs_1_, f32[8,128,128]{2,1,0:T(8,128)S(1)} %get-tuple-element.83.refs_2_, ...), custom_call_target="tpu_custom_call" | custom-call | flops 335544320 | bytes 4194304 | tf_op jit(solution)/shard_map/attend/pallas_call | solution.py:194
  63.4 5.1 %all-to-all-start.1 = ((bf16[32,32,128]{2,1,0:T(8,128)(2,1)}), bf16[32,32,128]{2,1,0:T(8,128)(2,1)S(1)}, u32[]{:S(2)}, u32[]{:S(2)}) async-start(bf16[32,32,128]{2,1,0:T(8,128)(2,1)} %bitcast.4), calls=%async_computation.1 | async-start | bytes 524288 | tf_op jit(solution)/shard_map/all_to_all | solution.py:244
  68.5 0.0 copy-start.2
  68.5 0.6 copy-done.2
  69.1 0.6 dynamic_slice.8
  71.7 0.0 copy-done
  71.7 10.0 %all-to-all-done.1 = bf16[32,32,128]{2,1,0:T(8,128)(2,1)S(1)} async-done(((bf16[32,32,128]{2,1,0:T(8,128)(2,1)}), bf16[32,32,128]{2,1,0:T(8,128)(2,1)S(1)}, u32[]{:S(2)}, u32[]{:S(2)}) %all-to-all-start.1) | async-done | bytes 262176 | tf_op jit(solution)/shard_map/all_to_all | solution.py:244
  81.8 0.3 copy.7
  82.1 0.1 reshape.51
  82.2 0.7 multiply_convert_fusion
  (4 shorter events, 0.2 us)
Async XLA Ops:
  0.0 71.7 %copy-start = (f32[64,4096]{1,0:T(8,128)S(1)}, f32[64,4096]{1,0:T(8,128)}, u32[]{:S(2)}) copy-start(f32[64,4096]{1,0:T(8,128)} %param.11) | copy-start | bytes 3145732
  36.6 7.3 %collective-permute-start = (bf16[8,128,128]{2,1,0:T(8,128)(2,1)S(1)}, bf16[8,128,128]{2,1,0:T(8,128)(2,1)S(1)}, u32[]{:S(2)}, u32[]{:S(2)}) collective-permute-start(bf16[8,128,128]{2,1,0:T(8,128)(2,1)S(1)} %slice.14), channel_id=1, source_target_pairs={{0,1},{1,0},{2,3},{3,2},{4,5},{5,4},{6,7},{7,6},{8,9},{9,8},{10,11... | collective-permute-start | bytes 786440 | tf_op jit(solution)/shard_map/ppermute | solution.py:214
  36.7 2.1 %copy-start.1 = (s32[8]{0:T(128)S(1)}, s32[8]{0:T(128)}, u32[]{:S(2)}) copy-start(s32[8]{0:T(128)} %valid_ref.11) | copy-start | bytes 100
  36.7 9.2 %collective-permute-start.1 = (bf16[4,128,256]{2,1,0:T(8,128)(2,1)S(1)}, bf16[4,128,256]{2,1,0:T(8,128)(2,1)S(1)}, u32[]{:S(2)}, u32[]{:S(2)}) collective-permute-start(bf16[4,128,256]{2,1,0:T(8,128)(2,1)S(1)} %get-tuple-element.70), channel_id=1, source_target_pairs={{0,8},{8,16},{16,24},{24,0},{1,9},{9,17},{17,25},{25,1},{2,10},{10... | collective-permute-start | bytes 786440 | tf_op jit(solution)/shard_map/ppermute | solution.py:210
  37.3 10.4 %collective-permute-start.2 = (bf16[4,128,256]{2,1,0:T(8,128)(2,1)S(1)}, bf16[4,128,256]{2,1,0:T(8,128)(2,1)S(1)}, u32[]{:S(2)}, u32[]{:S(2)}) collective-permute-start(bf16[4,128,256]{2,1,0:T(8,128)(2,1)S(1)} %get-tuple-element.71), channel_id=1, source_target_pairs={{0,24},{8,0},{16,8},{24,16},{1,25},{9,1},{17,9},{25,17},{2,26},{10... | collective-permute-start | bytes 786440 | tf_op jit(solution)/shard_map/ppermute | solution.py:210
  40.5 12.7 %collective-permute-start.7 = (bf16[4,128,256]{2,1,0:T(8,128)(2,1)S(1)}, bf16[4,128,256]{2,1,0:T(8,128)(2,1)S(1)}, u32[]{:S(2)}, u32[]{:S(2)}) collective-permute-start(bf16[4,128,256]{2,1,0:T(8,128)(2,1)S(1)} %get-tuple-element.70), channel_id=1, source_target_pairs={{0,24},{8,0},{16,8},{24,16},{1,25},{9,1},{17,9},{25,17},{2,26},{10... | collective-permute-start | bytes 786440 | tf_op jit(solution)/shard_map/ppermute | solution.py:210
  41.4 11.8 %collective-permute-start.8 = (bf16[4,128,256]{2,1,0:T(8,128)(2,1)S(1)}, bf16[4,128,256]{2,1,0:T(8,128)(2,1)S(1)}, u32[]{:S(2)}, u32[]{:S(2)}) collective-permute-start(bf16[4,128,256]{2,1,0:T(8,128)(2,1)S(1)} %get-tuple-element.71), channel_id=1, source_target_pairs={{0,8},{8,16},{16,24},{24,0},{1,9},{9,17},{17,25},{25,1},{2,10},{10... | collective-permute-start | bytes 786440 | tf_op jit(solution)/shard_map/ppermute | solution.py:210
  47.6 9.4 %collective-permute-start.3 = (bf16[4,128,256]{2,1,0:T(8,128)(2,1)S(1)}, bf16[4,128,256]{2,1,0:T(8,128)(2,1)S(1)}, u32[]{:S(2)}, u32[]{:S(2)}) collective-permute-start(bf16[4,128,256]{2,1,0:T(8,128)(2,1)S(1)} %collective-permute-done.1.refs_1_), channel_id=1, source_target_pairs={{0,8},{8,16},{16,24},{24,0},{1,9},{9,17},{17,25},{25,1},{2,10},{10... | collective-permute-start | bytes 786440 | tf_op jit(solution)/shard_map/ppermute | solution.py:210
  47.9 10.2 %collective-permute-start.5 = (bf16[4,128,256]{2,1,0:T(8,128)(2,1)S(1)}, bf16[4,128,256]{2,1,0:T(8,128)(2,1)S(1)}, u32[]{:S(2)}, u32[]{:S(2)}) collective-permute-start(bf16[4,128,256]{2,1,0:T(8,128)(2,1)S(1)} %collective-permute-done.2.refs_2_), channel_id=1, source_target_pairs={{0,24},{8,0},{16,8},{24,16},{1,25},{9,1},{17,9},{25,17},{2,26},{10... | collective-permute-start | bytes 786440 | tf_op jit(solution)/shard_map/ppermute | solution.py:210
  56.4 4.2 %collective-permute-start.10 = (f32[8,128,128]{2,1,0:T(8,128)S(1)}, f32[8,128,128]{2,1,0:T(8,128)S(1)}, u32[]{:S(2)}, u32[]{:S(2)}) collective-permute-start(f32[8,128,128]{2,1,0:T(8,128)S(1)} %get-tuple-element.87), channel_id=1, source_target_pairs={{0,1},{1,0},{2,3},{3,2},{4,5},{5,4},{6,7},{7,6},{8,9},{9,8},{10,11... | collective-permute-start | bytes 1572872 | tf_op jit(solution)/shard_map/ppermute | solution.py:214
  56.5 4.2 %collective-permute-start.11 = (f32[8,128,128]{2,1,0:T(8,128)S(1)}, f32[8,128,128]{2,1,0:T(8,128)S(1)}, u32[]{:S(2)}, u32[]{:S(2)}) collective-permute-start(f32[8,128,128]{2,1,0:T(8,128)S(1)} %get-tuple-element.88), channel_id=1, source_target_pairs={{0,1},{1,0},{2,3},{3,2},{4,5},{5,4},{6,7},{7,6},{8,9},{9,8},{10,11... | collective-permute-start | bytes 1572872 | tf_op jit(solution)/shard_map/ppermute | solution.py:214
  56.9 3.7 %collective-permute-start.9 = (f32[8,128,128]{2,1,0:T(8,128)S(1)}, f32[8,128,128]{2,1,0:T(8,128)S(1)}, u32[]{:S(2)}, u32[]{:S(2)}) collective-permute-start(f32[8,128,128]{2,1,0:T(8,128)S(1)} %get-tuple-element.86), channel_id=1, source_target_pairs={{0,1},{1,0},{2,3},{3,2},{4,5},{5,4},{6,7},{7,6},{8,9},{9,8},{10,11... | collective-permute-start | bytes 1572872 | tf_op jit(solution)/shard_map/ppermute | solution.py:214
  57.1 3.2 %collective-permute-start.4 = (bf16[4,128,256]{2,1,0:T(8,128)(2,1)S(1)}, bf16[4,128,256]{2,1,0:T(8,128)(2,1)S(1)}, u32[]{:S(2)}, u32[]{:S(2)}) collective-permute-start(bf16[4,128,256]{2,1,0:T(8,128)(2,1)S(1)} %collective-permute-done.3.refs_0_), channel_id=1, source_target_pairs={{0,1},{1,0},{2,3},{3,2},{4,5},{5,4},{6,7},{7,6},{8,9},{9,8},{10,11... | collective-permute-start | bytes 786440 | tf_op jit(solution)/shard_map/ppermute | solution.py:214
  58.1 2.5 %collective-permute-start.6 = (bf16[4,128,256]{2,1,0:T(8,128)(2,1)S(1)}, bf16[4,128,256]{2,1,0:T(8,128)(2,1)S(1)}, u32[]{:S(2)}, u32[]{:S(2)}) collective-permute-start(bf16[4,128,256]{2,1,0:T(8,128)(2,1)S(1)} %collective-permute-done.5.refs_1_), channel_id=1, source_target_pairs={{0,1},{1,0},{2,3},{3,2},{4,5},{5,4},{6,7},{7,6},{8,9},{9,8},{10,11... | collective-permute-start | bytes 786440 | tf_op jit(solution)/shard_map/ppermute | solution.py:214
  63.4 18.3 %all-to-all-start.1 = ((bf16[32,32,128]{2,1,0:T(8,128)(2,1)}), bf16[32,32,128]{2,1,0:T(8,128)(2,1)S(1)}, u32[]{:S(2)}, u32[]{:S(2)}) async-start(bf16[32,32,128]{2,1,0:T(8,128)(2,1)} %bitcast.4), calls=%async_computation.1 | async-start | bytes 524288 | tf_op jit(solution)/shard_map/all_to_all | solution.py:244
  68.5 0.7 copy-start.2

commit v6 on v5

--- a/solution.py
+++ b/solution.py
@@ -214,6 +214,25 @@
     return lax.ppermute(value, "core", [(0, 1), (1, 0)])
 
 
+def finish_kernel(heads_ref, gate_ref, out_ref):
+    for h in range(heads_ref.shape[0]):
+        columns = slice(h * HD, (h + 1) * HD)
+        mixed = heads_ref[h].astype(jnp.float32) * gate_ref[:, columns]
+        out_ref[:, columns] = mixed.astype(out_ref.dtype)
+
+
+def finish(heads, gate):
+    count, tokens, _ = heads.shape
+    return pl.pallas_call(
+        finish_kernel,
+        out_shape=jax.ShapeDtypeStruct((tokens, count * HD), heads.dtype),
+        in_specs=[pl.BlockSpec(memory_space=VMEM)] * 2,
+        out_specs=pl.BlockSpec(memory_space=VMEM),
+        compiler_params=pltpu.CompilerParams(vmem_limit_bytes=8 * MIB),
+        name="finish",
+    )(heads, gate)
+
+
 def shards(queries, keys, values, valid, levels, gate_table):
     tokens, width = queries.shape[1:]
     groups = lax.axis_size("group")
@@ -245,8 +264,7 @@
     own = lax.axis_index("group")
     level = lax.dynamic_index_in_dim(levels, own, 0, keepdims=False)
     gate = lax.dynamic_index_in_dim(gate_table, level, 0, keepdims=True)
-    mixed = returned.transpose(1, 0, 2).reshape(tokens, width).astype(jnp.float32) * gate
-    return mixed.astype(jnp.bfloat16)[None]
+    return finish(returned, gate)[None]
 
 
 def solution(mesh):

time: 83.3 us -> 82.8 us (level)
  no operation moved by 1% of the time
where the time goes in v6:
time: 82.8 us; the launch traced here: 82.5 us
  blocking collectives  34.4 us (42%)
  Pallas kernels  17 us (21%)
  waiting for transfers between devices  13.9 us (17%)
  starting transfers between devices  13.7 us (17%)
  between operations  2.03 us (2%)
  local copies, waits for them, and re-layouts  1.38 us (2%)
    all_to_all x1, blocking collectives, shards(): lax.all_to_all(pack(keys[0], values[0], queries[0]), AX, 0, 0, tiled=True)  34.4 us
    pallas_call x6, Pallas kernels, attend(): pl.pallas_call(functools.partial(attend_kernel, dists, other, wide, len(s...  14.2 us
    all_to_all x1, waiting for transfers between devices, shards(): lax.all_to_all(attended.reshape(-1, tokens, HD), AX, 0, 0, tiled=True)  10 us
    ppermute x6, starting transfers between devices, shift(): return lax.ppermute(value, 'x', [(i, (i + by) % n) for i in range(n)])  7.44 us
    all_to_all x1, starting transfers between devices, shards(): lax.all_to_all(attended.reshape(-1, tokens, HD), AX, 0, 0, tiled=True)  5.09 us
    ppermute x6, waiting for transfers between devices, shift(): return lax.ppermute(value, 'x', [(i, (i + by) % n) for i in range(n)])  3.21 us
    pallas_call x1, Pallas kernels, pack(): pl.pallas_call(functools.partial(pack_kernel, n), out_shape=jax.ShapeDtyp...  2.06 us
  transfers between devices with their start and end apart: 13, of which 7 were waited for; matrix products, arithmetic and copies ran while one was open for 1% of the time, Pallas kernels for 14%

profile of v6, /device:TPU:6, one launch (start us, length us, event | category | flops | bytes accessed | tf_op | source)
XLA Modules:
  0.0 82.5 jit_solution(6693499793201295999)
XLA Ops:
  0.0 0.0 copy-start
  0.0 2.1 %pack.1 = bf16[32,32,384]{2,1,0:T(8,128)(2,1)} custom-call(bf16[32,4096]{1,0:T(8,128)(2,1)} %bitcast.15, bf16[32,4096]{1,0:T(8,128)(2,1)} %bitcast.16, bf16[32,4096]{1,0:T(8,128)(2,1)} %bitcast.17), custom_call_target="tpu_custom_call" | custom-call | tf_op jit(solution)/shard_map/pack/pallas_call | solution.py:40
  2.1 34.4 %all_to_all.10 = bf16[32,32,384]{2,1,0:T(8,128)(2,1)S(1)} all-to-all(bf16[32,32,384]{2,1,0:T(8,128)(2,1)} %pack.1), channel_id=1, replica_groups=mesh['group'=8,'x'=4,'y'=4,'core'=2] {'group','y'}, dimensions={0} | all-to-all | bytes 1572864 | tf_op jit(solution)/shard_map/all_to_all | solution.py:239
  36.6 0.1 collective-permute-start
  36.7 0.0 copy-start.1
  36.7 0.6 collective-permute-start.1
  37.3 1.5 %collective-permute-start.2 = (bf16[4,128,256]{2,1,0:T(8,128)(2,1)S(1)}, bf16[4,128,256]{2,1,0:T(8,128)(2,1)S(1)}, u32[]{:S(2)}, u32[]{:S(2)}) collective-permute-start(bf16[4,128,256]{2,1,0:T(8,128)(2,1)S(1)} %get-tuple-element.71), channel_id=1, source_target_pairs={{0,24},{8,0},{16,8},{24,16},{1,25},{9,1},{17,9},{25,17},{2,26},{10... | collective-permute-start | bytes 786440 | tf_op jit(solution)/shard_map/ppermute | solution.py:210
  38.8 0.0 copy-done.1
  38.8 1.7 %attend.6 = (f32[8,128,128]{2,1,0:T(8,128)S(1)}, f32[8,128,128]{2,1,0:T(8,128)S(1)}, f32[8,128,128]{2,1,0:T(8,128)S(1)}) custom-call(s32[8]{0:T(128)S(1)} %copy-done.1, bf16[8,128,384]{2,1,0:T(8,128)(2,1)S(1)} %bitcast.9), custom_call_target="tpu_custom_call" | custom-call | flops 335544320 | bytes 4194304 | tf_op jit(solution)/shard_map/attend/pallas_call | solution.py:194
  40.5 0.9 %collective-permute-start.7 = (bf16[4,128,256]{2,1,0:T(8,128)(2,1)S(1)}, bf16[4,128,256]{2,1,0:T(8,128)(2,1)S(1)}, u32[]{:S(2)}, u32[]{:S(2)}) collective-permute-start(bf16[4,128,256]{2,1,0:T(8,128)(2,1)S(1)} %get-tuple-element.70), channel_id=1, source_target_pairs={{0,24},{8,0},{16,8},{24,16},{1,25},{9,1},{17,9},{25,17},{2,26},{10... | collective-permute-start | bytes 786440 | tf_op jit(solution)/shard_map/ppermute | solution.py:210
  41.4 2.4 %collective-permute-start.8 = (bf16[4,128,256]{2,1,0:T(8,128)(2,1)S(1)}, bf16[4,128,256]{2,1,0:T(8,128)(2,1)S(1)}, u32[]{:S(2)}, u32[]{:S(2)}) collective-permute-start(bf16[4,128,256]{2,1,0:T(8,128)(2,1)S(1)} %get-tuple-element.71), channel_id=1, source_target_pairs={{0,8},{8,16},{16,24},{24,0},{1,9},{9,17},{17,25},{25,1},{2,10},{10... | collective-permute-start | bytes 786440 | tf_op jit(solution)/shard_map/ppermute | solution.py:210
  43.8 0.0 collective-permute-done.refs_0_
  43.8 1.7 %attend.7 = (f32[8,128,128]{2,1,0:T(8,128)S(1)}, f32[8,128,128]{2,1,0:T(8,128)S(1)}, f32[8,128,128]{2,1,0:T(8,128)S(1)}) custom-call(s32[8]{0:T(128)S(1)} %copy-done.1, bf16[8,128,384]{2,1,0:T(8,128)(2,1)S(1)} %bitcast.10, bf16[8,128,128]{2,1,0:T(8,128)(2,1)S(1)} %collective-permute-done.refs_0_), custom_call_target="tpu_custom_call" | custom-call | flops 335544320 | bytes 4194304 | tf_op jit(solution)/shard_map/attend/pallas_call | solution.py:194
  45.6 0.3 collective-permute-done.1.refs_1_
  45.9 1.7 %collective-permute-done.2.refs_2_ = bf16[4,128,256]{2,1,0:T(8,128)(2,1)S(1)} collective-permute-done((bf16[4,128,256]{2,1,0:T(8,128)(2,1)S(1)}, bf16[4,128,256]{2,1,0:T(8,128)(2,1)S(1)}, u32[]{:S(2)}, u32[]{:S(2)}) %collective-permute-start.2) | collective-permute-done | bytes 262176 | tf_op jit(solution)/shard_map/ppermute | solution.py:210
  47.6 0.3 collective-permute-start.3
  47.9 1.7 %collective-permute-start.5 = (bf16[4,128,256]{2,1,0:T(8,128)(2,1)S(1)}, bf16[4,128,256]{2,1,0:T(8,128)(2,1)S(1)}, u32[]{:S(2)}, u32[]{:S(2)}) collective-permute-start(bf16[4,128,256]{2,1,0:T(8,128)(2,1)S(1)} %collective-permute-done.2.refs_2_), channel_id=1, source_target_pairs={{0,24},{8,0},{16,8},{24,16},{1,25},{9,1},{17,9},{25,17},{2,26},{10... | collective-permute-start | bytes 786440 | tf_op jit(solution)/shard_map/ppermute | solution.py:210
  49.6 3.1 %attend.8 = (f32[8,128,128]{2,1,0:T(8,128)S(1)}, f32[8,128,128]{2,1,0:T(8,128)S(1)}, f32[8,128,128]{2,1,0:T(8,128)S(1)}, f32[8,128,128]{2,1,0:T(8,128)S(1)}, f32...) custom-call(s32[8]{0:T(128)S(1)} %copy-done.1, bf16[8,128,384]{2,1,0:T(8,128)(2,1)S(1)} %bitcast.11, ...), custom_call_target="tpu_custom_call" | custom-call | flops 671088640 | bytes 4194304 | tf_op jit(solution)/shard_map/attend/pallas_call | solution.py:194
  52.8 0.5 collective-permute-done.7.refs_1_
  53.2 0.0 collective-permute-done.8.refs_2_
  53.2 3.1 %attend.9 = (f32[8,128,128]{2,1,0:T(8,128)S(1)}, f32[8,128,128]{2,1,0:T(8,128)S(1)}, f32[8,128,128]{2,1,0:T(8,128)S(1)}, f32[8,128,128]{2,1,0:T(8,128)S(1)}, f32...) custom-call(s32[8]{0:T(128)S(1)} %copy-done.1, bf16[8,128,384]{2,1,0:T(8,128)(2,1)S(1)} %bitcast.12, ...), custom_call_target="tpu_custom_call" | custom-call | flops 671088640 | bytes 4194304 | tf_op jit(solution)/shard_map/attend/pallas_call | solution.py:194
  56.4 0.1 collective-permute-start.10
  56.5 0.5 collective-permute-start.11
  56.9 0.1 collective-permute-start.9
  57.0 0.0 collective-permute-done.3.refs_0_
  57.1 0.4 collective-permute-start.4
  57.5 0.7 collective-permute-done.5.refs_1_
  58.1 0.0 collective-permute-start.6
  58.1 1.8 %attend.10 = (f32[8,128,128]{2,1,0:T(8,128)S(1)}, f32[8,128,128]{2,1,0:T(8,128)S(1)}, f32[8,128,128]{2,1,0:T(8,128)S(1)}) custom-call(s32[8]{0:T(128)S(1)} %copy-done.1, bf16[8,128,384]{2,1,0:T(8,128)(2,1)S(1)} %bitcast.13, bf16[4,128,256]{2,1,0:T(8,128)(2,1)S(1)} %collective-permute-done.3.refs_0_, bf16[4,128,256]{2,1,0:T(8,128)(2,1)S(1)} %collective-permute-done.5.refs_1_, ...), custom_call_target="tpu_custom_call" | custom-call | flops 335544320 | bytes 4194304 | tf_op jit(solution)/shard_map/attend/pallas_call | solution.py:194
  60.0 0.3 collective-permute-done.4.refs_0_
  60.2 0.4 collective-permute-done.6.refs_1_
  60.6 0.0 collective-permute-done.10.refs_6_
  60.6 0.0 collective-permute-done.11.refs_7_
  60.6 0.0 collective-permute-done.9.refs_5_
  60.6 2.8 %attend.11 = bf16[8,128,128]{2,1,0:T(8,128)(2,1)} custom-call(s32[8]{0:T(128)S(1)} %copy-done.1, bf16[8,128,384]{2,1,0:T(8,128)(2,1)S(1)} %bitcast.14, bf16[4,128,256]{2,1,0:T(8,128)(2,1)S(1)} %collective-permute-done.4.refs_0_, bf16[4,128,256]{2,1,0:T(8,128)(2,1)S(1)} %collective-permute-done.6.refs_1_, f32[8,128,128]{2,1,0:T(8,128)S(1)} %get-tuple-element.83.refs_2_, ...), custom_call_target="tpu_custom_call" | custom-call | flops 335544320 | bytes 4194304 | tf_op jit(solution)/shard_map/attend/pallas_call | solution.py:194
  63.4 5.1 %all-to-all-start.1 = ((bf16[32,32,128]{2,1,0:T(8,128)(2,1)}), bf16[32,32,128]{2,1,0:T(8,128)(2,1)S(1)}, u32[]{:S(2)}, u32[]{:S(2)}) async-start(bf16[32,32,128]{2,1,0:T(8,128)(2,1)} %bitcast.4), calls=%async_computation.1 | async-start | bytes 524288 | tf_op jit(solution)/shard_map/all_to_all | solution.py:263
  68.5 0.0 copy-start.2
  68.5 0.6 copy-done.2
  69.1 0.6 dynamic_slice.8
  71.7 0.0 copy-done
  71.7 10.0 %all-to-all-done.1.heads_ref = bf16[32,32,128]{2,1,0:T(8,128)(2,1)S(1)} async-done(((bf16[32,32,128]{2,1,0:T(8,128)(2,1)}), bf16[32,32,128]{2,1,0:T(8,128)(2,1)S(1)}, u32[]{:S(2)}, u32[]{:S(2)}) %all-to-all-start.1) | async-done | bytes 262176 | tf_op jit(solution)/shard_map/all_to_all | solution.py:263
  81.7 0.8 finish.1
  (3 shorter events, 0.1 us)
Async XLA Ops:
  0.0 71.7 %copy-start = (f32[64,4096]{1,0:T(8,128)S(1)}, f32[64,4096]{1,0:T(8,128)}, u32[]{:S(2)}) copy-start(f32[64,4096]{1,0:T(8,128)} %param.11) | copy-start | bytes 3145732
  36.6 7.3 %collective-permute-start = (bf16[8,128,128]{2,1,0:T(8,128)(2,1)S(1)}, bf16[8,128,128]{2,1,0:T(8,128)(2,1)S(1)}, u32[]{:S(2)}, u32[]{:S(2)}) collective-permute-start(bf16[8,128,128]{2,1,0:T(8,128)(2,1)S(1)} %slice.14), channel_id=1, source_target_pairs={{0,1},{1,0},{2,3},{3,2},{4,5},{5,4},{6,7},{7,6},{8,9},{9,8},{10,11... | collective-permute-start | bytes 786440 | tf_op jit(solution)/shard_map/ppermute | solution.py:214
  36.7 2.1 %copy-start.1 = (s32[8]{0:T(128)S(1)}, s32[8]{0:T(128)}, u32[]{:S(2)}) copy-start(s32[8]{0:T(128)} %valid_ref.11) | copy-start | bytes 100
  36.7 9.2 %collective-permute-start.1 = (bf16[4,128,256]{2,1,0:T(8,128)(2,1)S(1)}, bf16[4,128,256]{2,1,0:T(8,128)(2,1)S(1)}, u32[]{:S(2)}, u32[]{:S(2)}) collective-permute-start(bf16[4,128,256]{2,1,0:T(8,128)(2,1)S(1)} %get-tuple-element.70), channel_id=1, source_target_pairs={{0,8},{8,16},{16,24},{24,0},{1,9},{9,17},{17,25},{25,1},{2,10},{10... | collective-permute-start | bytes 786440 | tf_op jit(solution)/shard_map/ppermute | solution.py:210
  37.3 10.4 %collective-permute-start.2 = (bf16[4,128,256]{2,1,0:T(8,128)(2,1)S(1)}, bf16[4,128,256]{2,1,0:T(8,128)(2,1)S(1)}, u32[]{:S(2)}, u32[]{:S(2)}) collective-permute-start(bf16[4,128,256]{2,1,0:T(8,128)(2,1)S(1)} %get-tuple-element.71), channel_id=1, source_target_pairs={{0,24},{8,0},{16,8},{24,16},{1,25},{9,1},{17,9},{25,17},{2,26},{10... | collective-permute-start | bytes 786440 | tf_op jit(solution)/shard_map/ppermute | solution.py:210
  40.5 12.7 %collective-permute-start.7 = (bf16[4,128,256]{2,1,0:T(8,128)(2,1)S(1)}, bf16[4,128,256]{2,1,0:T(8,128)(2,1)S(1)}, u32[]{:S(2)}, u32[]{:S(2)}) collective-permute-start(bf16[4,128,256]{2,1,0:T(8,128)(2,1)S(1)} %get-tuple-element.70), channel_id=1, source_target_pairs={{0,24},{8,0},{16,8},{24,16},{1,25},{9,1},{17,9},{25,17},{2,26},{10... | collective-permute-start | bytes 786440 | tf_op jit(solution)/shard_map/ppermute | solution.py:210
  41.4 11.8 %collective-permute-start.8 = (bf16[4,128,256]{2,1,0:T(8,128)(2,1)S(1)}, bf16[4,128,256]{2,1,0:T(8,128)(2,1)S(1)}, u32[]{:S(2)}, u32[]{:S(2)}) collective-permute-start(bf16[4,128,256]{2,1,0:T(8,128)(2,1)S(1)} %get-tuple-element.71), channel_id=1, source_target_pairs={{0,8},{8,16},{16,24},{24,0},{1,9},{9,17},{17,25},{25,1},{2,10},{10... | collective-permute-start | bytes 786440 | tf_op jit(solution)/shard_map/ppermute | solution.py:210
  47.6 9.4 %collective-permute-start.3 = (bf16[4,128,256]{2,1,0:T(8,128)(2,1)S(1)}, bf16[4,128,256]{2,1,0:T(8,128)(2,1)S(1)}, u32[]{:S(2)}, u32[]{:S(2)}) collective-permute-start(bf16[4,128,256]{2,1,0:T(8,128)(2,1)S(1)} %collective-permute-done.1.refs_1_), channel_id=1, source_target_pairs={{0,8},{8,16},{16,24},{24,0},{1,9},{9,17},{17,25},{25,1},{2,10},{10... | collective-permute-start | bytes 786440 | tf_op jit(solution)/shard_map/ppermute | solution.py:210
  47.9 10.2 %collective-permute-start.5 = (bf16[4,128,256]{2,1,0:T(8,128)(2,1)S(1)}, bf16[4,128,256]{2,1,0:T(8,128)(2,1)S(1)}, u32[]{:S(2)}, u32[]{:S(2)}) collective-permute-start(bf16[4,128,256]{2,1,0:T(8,128)(2,1)S(1)} %collective-permute-done.2.refs_2_), channel_id=1, source_target_pairs={{0,24},{8,0},{16,8},{24,16},{1,25},{9,1},{17,9},{25,17},{2,26},{10... | collective-permute-start | bytes 786440 | tf_op jit(solution)/shard_map/ppermute | solution.py:210
  56.4 4.2 %collective-permute-start.10 = (f32[8,128,128]{2,1,0:T(8,128)S(1)}, f32[8,128,128]{2,1,0:T(8,128)S(1)}, u32[]{:S(2)}, u32[]{:S(2)}) collective-permute-start(f32[8,128,128]{2,1,0:T(8,128)S(1)} %get-tuple-element.87), channel_id=1, source_target_pairs={{0,1},{1,0},{2,3},{3,2},{4,5},{5,4},{6,7},{7,6},{8,9},{9,8},{10,11... | collective-permute-start | bytes 1572872 | tf_op jit(solution)/shard_map/ppermute | solution.py:214
  56.5 4.2 %collective-permute-start.11 = (f32[8,128,128]{2,1,0:T(8,128)S(1)}, f32[8,128,128]{2,1,0:T(8,128)S(1)}, u32[]{:S(2)}, u32[]{:S(2)}) collective-permute-start(f32[8,128,128]{2,1,0:T(8,128)S(1)} %get-tuple-element.88), channel_id=1, source_target_pairs={{0,1},{1,0},{2,3},{3,2},{4,5},{5,4},{6,7},{7,6},{8,9},{9,8},{10,11... | collective-permute-start | bytes 1572872 | tf_op jit(solution)/shard_map/ppermute | solution.py:214
  56.9 3.7 %collective-permute-start.9 = (f32[8,128,128]{2,1,0:T(8,128)S(1)}, f32[8,128,128]{2,1,0:T(8,128)S(1)}, u32[]{:S(2)}, u32[]{:S(2)}) collective-permute-start(f32[8,128,128]{2,1,0:T(8,128)S(1)} %get-tuple-element.86), channel_id=1, source_target_pairs={{0,1},{1,0},{2,3},{3,2},{4,5},{5,4},{6,7},{7,6},{8,9},{9,8},{10,11... | collective-permute-start | bytes 1572872 | tf_op jit(solution)/shard_map/ppermute | solution.py:214
  57.1 3.2 %collective-permute-start.4 = (bf16[4,128,256]{2,1,0:T(8,128)(2,1)S(1)}, bf16[4,128,256]{2,1,0:T(8,128)(2,1)S(1)}, u32[]{:S(2)}, u32[]{:S(2)}) collective-permute-start(bf16[4,128,256]{2,1,0:T(8,128)(2,1)S(1)} %collective-permute-done.3.refs_0_), channel_id=1, source_target_pairs={{0,1},{1,0},{2,3},{3,2},{4,5},{5,4},{6,7},{7,6},{8,9},{9,8},{10,11... | collective-permute-start | bytes 786440 | tf_op jit(solution)/shard_map/ppermute | solution.py:214
  58.1 2.5 %collective-permute-start.6 = (bf16[4,128,256]{2,1,0:T(8,128)(2,1)S(1)}, bf16[4,128,256]{2,1,0:T(8,128)(2,1)S(1)}, u32[]{:S(2)}, u32[]{:S(2)}) collective-permute-start(bf16[4,128,256]{2,1,0:T(8,128)(2,1)S(1)} %collective-permute-done.5.refs_1_), channel_id=1, source_target_pairs={{0,1},{1,0},{2,3},{3,2},{4,5},{5,4},{6,7},{7,6},{8,9},{9,8},{10,11... | collective-permute-start | bytes 786440 | tf_op jit(solution)/shard_map/ppermute | solution.py:214
  63.4 18.3 %all-to-all-start.1 = ((bf16[32,32,128]{2,1,0:T(8,128)(2,1)}), bf16[32,32,128]{2,1,0:T(8,128)(2,1)S(1)}, u32[]{:S(2)}, u32[]{:S(2)}) async-start(bf16[32,32,128]{2,1,0:T(8,128)(2,1)} %bitcast.4), calls=%async_computation.1 | async-start | bytes 524288 | tf_op jit(solution)/shard_map/all_to_all | solution.py:263
  68.5 0.7 copy-start.2
